TPU v7x, 256 devices: a whole 4x4x8 slice. The times are simulated.
256 devices in a mesh: curve: 64 (over y, z, core), owner: 4 (over x).
Axes of the slice: x: 4, y: 4, z: 8, core: 2. Of those that a mesh axis runs over, the one named last changes fastest.
Arguments:
- operator_blocks: bfloat16 [2048, 64, 448], P(('curve', 'owner')), may hold values from -0.25 to 0.25
- operator_columns: int32 [2048, 7], P(('curve', 'owner')), may hold values from 0 to 2047, as said below
- prolong_blocks: bfloat16 [2048, 64, 256], P(('curve', 'owner')), may hold values from -0.890625 to 0.890625
- prolong_columns: int32 [2048, 4], P(('curve', 'owner')), may hold values from 0 to 255, as said below
Outputs:
- coarse_band: bfloat16 [256, 64, 2112], P('curve', 'owner')
Inputs may be any that keep to these rules, and one draw needn't show every extreme that they name: operator_columns[i, 0] = i; the other 6 entries of row i are, in some order, the elements beside i across its six faces in the grid of Morton coordinates, with i itself where the grid ends. prolong_columns[i, 0] = i // 8; the other 3 entries are, in some order, the aggregates beside i's aggregate across the three of its faces that element i touches, with i // 8 where the grid ends.
All inputs are finite; a program needn't handle non-finite values.
Results may differ from a plain program's by a relative error of at most 0.0054.
Values may be sent and summed in bfloat16 or wider, within the bound.
No kernel may reach another device: no remote copies, remote signals or barrier semaphores. Data moves between devices by JAX's collectives and lax.ppermute only.
A program may use at most 128 MiB of HBM per device.

v0:
```python
import jax
import jax.numpy as jnp
import numpy as np
from jax import lax
from jax.sharding import PartitionSpec as P

G = 8


UNIT_STEPS = ((0, 0, 0), (1, 0, 0), (-1, 0, 0), (0, 1, 0), (0, -1, 0), (0, 0, 1), (0, 0, -1))


def shifted_2(value, axis, by):
    length = lax.axis_size(axis)
    pairs = [(i, i + by) for i in range(length) if 0 <= i + by < length]
    return lax.ppermute(value, axis, pairs)


def pick_where(flags):
    return np.array([place for place in range(len(flags)) if flags[place]], np.int32)


def offset_table():
    table = []
    for first_off in range(-2, 3):
        for second_off in range(-2, 3):
            for third_off in range(-2, 3):
                reach = sum(
                    (max(0, 2 * abs(value) - 1) for value in (first_off, second_off, third_off))
                )
                if reach <= 3:
                    table.append((first_off, second_off, third_off))
    return table


def offset_code(steps):
    return (steps[0] + 3) * 49 + (steps[1] + 3) * 7 + (steps[2] + 3)


def decode_position(values, bit_count):
    position = [values * 0, values * 0, values * 0]
    for place in range(bit_count):
        digit = values // 2**place % 2
        position[place % 3] = position[place % 3] + digit * 2 ** (place // 3)
    return position


def relative_codes(targets, anchor, bit_count):
    target_pos = decode_position(targets, bit_count)
    anchor_pos = decode_position(anchor, bit_count)
    steps = [jnp.clip(target_pos[axis_id] - anchor_pos[axis_id], -3, 3) for axis_id in range(3)]
    return offset_code(steps)


def remap_table(offsets, unit):
    where_of = {entry: place for place, entry in enumerate(offsets)}
    source = np.zeros(len(offsets), np.int32)
    keep = np.zeros(len(offsets), np.float32)
    for place, entry in enumerate(offsets):
        shifted = (entry[0] + unit[0], entry[1] + unit[1], entry[2] + unit[2])
        if shifted in where_of:
            source[place] = where_of[shifted]
            keep[place] = 1.0
    return (source, keep)


def shards(operator_blocks, operator_columns, prolong_blocks, prolong_columns):
    rows_dev = operator_columns.shape[0]
    width = operator_blocks.shape[1]
    per_a = operator_columns.shape[1]
    per_p = prolong_columns.shape[1]
    devices = lax.axis_size("curve") * lax.axis_size("owner")
    local_bits = rows_dev.bit_length() - 1
    device_bits = devices.bit_length() - 1
    coarse_bits = local_bits + device_bits - 3
    groups = rows_dev // G
    offsets = offset_table()
    count_off = len(offsets)
    count_unit = len(UNIT_STEPS)
    offset_codes = jnp.array([offset_code(entry) for entry in offsets], jnp.int32)
    unit_codes = jnp.array([offset_code(entry) for entry in UNIT_STEPS], jnp.int32)
    highest = lax.Precision.HIGHEST
    device_now = lax.axis_index(("curve", "owner"))
    local_pos = np.zeros((3, rows_dev), np.int64)
    for place in range(local_bits):
        local_pos[place % 3] += (np.arange(rows_dev) >> place & 1) << place // 3
    sides = [int(local_pos[axis_id].max()) + 1 for axis_id in range(3)]
    group_pos = local_pos[:, ::G] // 2
    group_sides = [max(1, side // 2) for side in sides]
    group_index = {
        tuple((int(group_pos[axis_id, member]) for axis_id in range(3))): member
        for member in range(groups)
    }
    places = [
        [place for place in range(device_bits) if (local_bits + place) % 3 == axis_id]
        for axis_id in range(3)
    ]
    slots = []
    for axis_id in range(3):
        chosen = places[axis_id]
        for sense in (1, -1):
            for depth in range(len(chosen)):
                jump = 2 ** chosen[depth] - sum((2 ** chosen[lower] for lower in range(depth)))
                slots.append((axis_id, sense, depth, jump))
    blocks_list = [prolong_blocks]
    columns_list = [prolong_columns]
    lookup = np.zeros((rows_dev, len(slots)), np.int32)
    senders = []
    filled = rows_dev
    for slot_id, (axis_id, sense, depth, jump) in enumerate(slots):
        wanted = np.arange(rows_dev)
        lookup[wanted, slot_id] = filled + np.arange(wanted.size)
        filled = filled + wanted.size
        arrived_blocks, arrived_columns = shifted_2(
            (prolong_blocks, prolong_columns), ("curve", "owner"), -sense * jump
        )
        blocks_list.append(arrived_blocks)
        columns_list.append(arrived_columns)
        senders.append(sense * jump)
    ext_blocks = jnp.concatenate(blocks_list, 0)
    ext_columns = jnp.concatenate(columns_list, 0)
    holder = operator_columns // rows_dev
    within = operator_columns % rows_dev
    match = (holder[..., None] == device_now + jnp.array(senders, jnp.int32)).astype(jnp.int32)
    pick_row = (within[..., None] == jnp.arange(rows_dev, dtype=jnp.int32)).astype(jnp.int32)
    slot_place = jnp.sum(pick_row[..., None] * jnp.asarray(lookup)[None, None], axis=2)
    remote = jnp.sum(slot_place * match, axis=2)
    position = jnp.where(holder == device_now, within, remote)
    gathered = ext_blocks[position]
    gathered_cols = ext_columns[position]
    own_group = prolong_columns[:, 0]
    fetched_codes = relative_codes(gathered_cols, own_group[:, None, None], coarse_bits)
    route = (fetched_codes[..., None] == offset_codes).astype(jnp.float32)
    slot_codes = relative_codes(prolong_columns, own_group[:, None], coarse_bits)
    unit_pick = (slot_codes[..., None] == unit_codes).astype(jnp.float32)

    def one_group(inputs):
        a_rows, p_fetched, route_rows, p_rows, unit_rows = inputs
        product = jnp.einsum(
            "iakb,ikbn->iakn", a_rows, p_fetched, preferred_element_type=jnp.float32
        )
        product = product.reshape(G, width, per_a, per_p, width)
        product_ap = jnp.einsum("iakmc,ikmo->iaoc", product, route_rows, precision=highest).astype(
            jnp.bfloat16
        )
        total = jnp.zeros((count_unit, width, count_off, width), jnp.float32)
        for slot in range(per_p):
            contrib = jnp.einsum(
                "iax,iaoc->ixoc",
                p_rows[:, :, slot, :],
                product_ap,
                preferred_element_type=jnp.float32,
            )
            total = total + jnp.einsum(
                "ixoc,iu->uxoc", contrib, unit_rows[:, slot, :], precision=highest
            )
        return total

    partial_rel = lax.map(
        one_group,
        (
            operator_blocks.reshape(groups, G, width, per_a, width),
            gathered.reshape(groups, G, per_a, width, per_p * width),
            route.reshape(groups, G, per_a, per_p, count_off),
            prolong_blocks.reshape(groups, G, width, per_p, width),
            unit_pick.reshape(groups, G, per_p, count_unit),
        ),
    )
    own_sum = jnp.zeros((groups, width, count_off, width), jnp.float32)
    outgoing = {}
    for unit_id, unit in enumerate(UNIT_STEPS):
        source, keep = remap_table(offsets, unit)
        moved = partial_rel[:, unit_id][:, :, source, :] * jnp.asarray(keep)[None, None, :, None]
        if unit_id == 0:
            own_sum = own_sum + moved
        else:
            axis_id = [place for place in range(3) if unit[place] != 0][0]
            sense = unit[axis_id]
            landing = group_pos[axis_id] + sense
            inside = pick_where((landing >= 0) & (landing < group_sides[axis_id]))
            if inside.size > 0:
                targets = []
                for member in inside:
                    spot = [int(group_pos[place, member]) for place in range(3)]
                    spot[axis_id] = spot[axis_id] + sense
                    targets.append(group_index[tuple(spot)])
                own_sum = own_sum.at[np.array(targets, np.int32)].add(moved[inside])
            edge = group_sides[axis_id] - 1 if sense == 1 else 0
            outside = pick_where(group_pos[axis_id] == edge)
            outgoing[axis_id, sense] = moved[outside].astype(jnp.bfloat16)
    for slot_id, (axis_id, sense, depth, jump) in enumerate(slots):
        arrived = shifted_2(outgoing[axis_id, sense], ("curve", "owner"), sense * jump)
        lower_value = 0 if sense == 1 else 1
        chosen = places[axis_id]
        valid = device_now // 2 ** chosen[depth] % 2 == 1 - lower_value
        for lower in range(depth):
            valid = jnp.logical_and(valid, device_now // 2 ** chosen[lower] % 2 == lower_value)
        facing = 0 if sense == 1 else group_sides[axis_id] - 1
        landing = pick_where(group_pos[axis_id] == facing)
        own_sum = own_sum.at[landing].add(jnp.where(valid, arrived.astype(jnp.float32), 0.0))
    settled = own_sum.astype(jnp.bfloat16).reshape(groups, width, count_off * width)
    return lax.all_to_all(settled, "owner", split_axis=1, concat_axis=0, tiled=True)


def solution(mesh):
    return jax.shard_map(
        shards,
        mesh=mesh,
        in_specs=(
            P(("curve", "owner"), None, None),
            P(("curve", "owner"), None),
            P(("curve", "owner"), None, None),
            P(("curve", "owner"), None),
        ),
        out_specs=P("curve", "owner", None),
        check_vma=False,
    )
```

profile of v0, /device:TPU:89, one launch (start us, length us, event | category | flops | bytes accessed | tf_op | source)
XLA Modules:
  0.0 554.5 jit_solution(17238385805076667689)
XLA Ops:
  7.0 7.6 %collective-permute-start.10 = (s32[8,4]{0,1:T(4,128)}, s32[8,4]{0,1:T(4,128)S(1)}, u32[]{:S(2)}, u32[]{:S(2)}) collective-permute-start(s32[8,4]{0,1:T(4,128)} %param.108), channel_id=1, source_target_pairs={{0,14},{1,15},{2,16},{3,17},{4,18},{5,19},{6,20},{7,21},{8,22},{9,... | collective-permute-start | bytes 392 | tf_op jit(solution)/shard_map/ppermute | solution.py:16
  28.6 7.8 %collective-permute-start.13 = (s32[8,4]{0,1:T(4,128)S(1)}, s32[8,4]{0,1:T(4,128)S(1)}, u32[]{:S(2)}, u32[]{:S(2)}) collective-permute-start(s32[8,4]{0,1:T(4,128)S(1)} %copy-done.12), channel_id=1, source_target_pairs={{28,0},{29,1},{30,2},{31,3},{32,4},{33,5},{34,6},{35,7},{36,8},{37... | collective-permute-start | bytes 392 | tf_op jit(solution)/shard_map/ppermute | solution.py:16
  64.3 11.3 %collective-permute-start.8 = (s32[8,4]{0,1:T(4,128)S(1)}, s32[8,4]{0,1:T(4,128)S(1)}, u32[]{:S(2)}, u32[]{:S(2)}) collective-permute-start(s32[8,4]{0,1:T(4,128)S(1)} %copy-done.12), channel_id=1, source_target_pairs={{110,0},{111,1},{112,2},{113,3},{114,4},{115,5},{116,6},{117,7},{1... | collective-permute-start | bytes 392 | tf_op jit(solution)/shard_map/ppermute | solution.py:16
  119.2 6.9 %collective-permute-start.26 = (bf16[8,64,256]{2,1,0:T(8,128)(2,1)S(1)}, bf16[8,64,256]{2,1,0:T(8,128)(2,1)S(1)}, u32[]{:S(2)}, u32[]{:S(2)}) collective-permute-start(bf16[8,64,256]{2,1,0:T(8,128)(2,1)S(1)} %copy-done.4), channel_id=1, source_target_pairs={{0,14},{1,15},{2,16},{3,17},{4,18},{5,19},{6,20},{7,21},{8,22},{9,... | collective-permute-start | bytes 786440 | tf_op jit(solution)/shard_map/ppermute | solution.py:16
  167.7 7.6 %reshape.1408 = f32[8,64,7,4,64]{4,3,1,2,0:T(4,128)} reshape(f32[8,64,7,256]{3,1,2,0:T(8,128)} %convolution_bitcast_fusion.4) | data formatting | bytes 7340032 | tf_op jit(solution)/shard_map/while/body/eval_jaxpr/reshape | solution.py:142
  175.2 17.9 %fusion.2 = bf16[8,64,33,64]{3,2,1,0:T(8,128)(2,1)} fusion(f32[8,64,7,4,64]{4,3,1,2,0:T(4,128)} %reshape.1408, s32[33]{0:T(128)S(1)} %copy-done.29, s32[8,7,4]{1,2,0:T(4,128)S(1)} %copy.234), kind=kOutput, calls=%fused_computation.13 | convolution fusion | flops 364420320 | bytes 5833732 | tf_op jit(solution)/shard_map/while/body/eval_jaxpr/iakmc,ikmo->iaoc/dot_general | solution.py:143
  193.1 7.9 %copy.237 = bf16[8,64,33,64]{1,3,2,0:T(8,128)(2,1)} copy(bf16[8,64,33,64]{3,2,1,0:T(8,128)(2,1)} %fusion.2) | data formatting | bytes 4325376 | tf_op jit(solution)/shard_map/while/body/eval_jaxpr/convert_element_type | solution.py:143
  201.1 6.9 %convolution_bitcast_fusion.2 = f32[8,64,33,64]{1,3,2,0:T(8,128)} fusion(bf16[8,64,33,64]{1,3,2,0:T(8,128)(2,1)} %copy.237, bf16[8,64,1,64]{3,2,1,0:T(2,128)(2,1)S(1)} %copy-done.6), kind=kOutput, calls=%fused_computation.16 | convolution fusion | flops 138412032 | bytes 6553600 | tf_op jit(solution)/shard_map/while/body/eval_jaxpr/iax,iaoc->ixoc/dot_general | solution.py:148
  208.0 9.9 %copy.242 = f32[8,64,33,64]{3,0,2,1:T(8,128)} copy(f32[8,64,33,64]{1,3,2,0:T(8,128)} %convolution_bitcast_fusion.2) | data formatting | bytes 8650752 | tf_op jit(solution)/shard_map/while/body/eval_jaxpr/iax,iaoc->ixoc/dot_general | solution.py:148
  224.8 9.9 %copy.239 = f32[8,64,33,64]{3,0,2,1:T(8,128)} copy(f32[8,64,33,64]{1,3,2,0:T(8,128)} %convolution_bitcast_fusion.3) | data formatting | bytes 8650752 | tf_op jit(solution)/shard_map/while/body/eval_jaxpr/iax,iaoc->ixoc/dot_general | solution.py:148
  234.7 11.4 %fusion.86 = f32[7,64,33,64]{3,0,2,1:T(8,128)} fusion(f32[8,64,33,64]{3,0,2,1:T(8,128)} %copy.242, pred[8,4,7]{2,0,1:T(8,128)(4,1)S(1)} %broadcast_compare_fusion), kind=kOutput, calls=%fused_computation.198 | convolution fusion | flops 90832896 | bytes 8111104 | tf_op jit(solution)/shard_map/while/body/eval_jaxpr/ixoc,iu->uxoc/dot_general | solution.py:154
  257.0 9.9 %copy.245 = f32[8,64,33,64]{3,0,2,1:T(8,128)} copy(f32[8,64,33,64]{1,3,2,0:T(8,128)} %convolution_bitcast_fusion.1) | data formatting | bytes 8650752 | tf_op jit(solution)/shard_map/while/body/eval_jaxpr/iax,iaoc->ixoc/dot_general | solution.py:148
  266.9 10.4 %fusion.85 = f32[7,64,33,64]{3,0,2,1:T(8,128)} fusion(f32[8,64,33,64]{3,0,2,1:T(8,128)} %copy.245, pred[8,4,7]{2,0,1:T(8,128)(4,1)S(1)} %broadcast_compare_fusion), kind=kOutput, calls=%fused_computation.196 | convolution fusion | flops 90832896 | bytes 8111104 | tf_op jit(solution)/shard_map/while/body/eval_jaxpr/ixoc,iu->uxoc/dot_general | solution.py:154
  281.9 9.9 %copy.248 = f32[8,64,33,64]{3,0,2,1:T(8,128)} copy(f32[8,64,33,64]{1,3,2,0:T(8,128)} %convolution_bitcast_fusion) | data formatting | bytes 8650752 | tf_op jit(solution)/shard_map/while/body/eval_jaxpr/iax,iaoc->ixoc/dot_general | solution.py:148
  291.8 15.4 %add_bitcast_fusion = f32[1,7,64,33,64]{4,1,3,2,0:T(8,128)} fusion(f32[7,64,33,64]{3,0,2,1:T(8,128)} %fusion.85, f32[7,64,33,64]{3,0,2,1:T(8,128)} %fusion.87, f32[7,64,33,64]{3,0,2,1:T(8,128)} %fusion.86, f32[8,64,33,64]{3,0,2,1:T(8,128)} %copy.248, pred[8,4,7]{2,0,1:T(8,128)(4,1)S(1)} %broadcast_compare_fusion), kind=kOutput, calls=%fused_computation.10 | convolution fusion | flops 93671424 | bytes 19465216 | tf_op jit(solution)/shard_map/while/body/eval_jaxpr/ixoc,iu->uxoc/dot_general | solution.py:154
  307.2 24.3 %fusion.164 = (f32[1,1,64,33,64]{4,1,3,2,0:T(1,128)}, f32[1,1,64,33,64]{4,1,3,2,0:T(1,128)}, f32[1,1,64,33,64]{4,1,3,2,0:T(1,128)}, f32[1,1,64,33,64]{4,1,3,2,0:...) fusion(f32[1,7,64,33,64]{4,1,3,2,0:T(8,128)} %add_bitcast_fusion), kind=kLoop, calls=%fused_computation.415 | loop fusion | bytes 7569408 | tf_op jit(solution)/shard_map/slice | solution.py:173
  333.5 8.3 %collective-permute-start.32 = (bf16[1,64,33,64]{3,1,2,0:T(8,128)(2,1)}, bf16[1,64,33,64]{3,1,2,0:T(8,128)(2,1)}, u32[]{:S(2)}, u32[]{:S(2)}) collective-permute-start(bf16[1,64,33,64]{3,1,2,0:T(8,128)(2,1)} %fusion.10), channel_id=1, source_target_pairs={{0,1},{1,2},{2,3},{3,4},{4,5},{5,6},{6,7},{7,8},{8,9},{9,10},{10,1... | collective-permute-start | bytes 811016 | tf_op jit(solution)/shard_map/ppermute | solution.py:16
  383.8 7.9 %collective-permute-start.41 = (bf16[1,64,33,64]{3,1,2,0:T(8,128)(2,1)}, bf16[1,64,33,64]{3,1,2,0:T(8,128)(2,1)}, u32[]{:S(2)}, u32[]{:S(2)}) collective-permute-start(bf16[1,64,33,64]{3,1,2,0:T(8,128)(2,1)} %fusion.7), channel_id=1, source_target_pairs={{2,0},{3,1},{4,2},{5,3},{6,4},{7,5},{8,6},{9,7},{10,8},{11,9},{12,... | collective-permute-start | bytes 811016 | tf_op jit(solution)/shard_map/ppermute | solution.py:16
  398.7 32.1 %collective-permute-done.38 = bf16[1,64,33,64]{3,1,2,0:T(8,128)(2,1)S(1)} collective-permute-done((bf16[1,64,33,64]{3,1,2,0:T(8,128)(2,1)}, bf16[1,64,33,64]{3,1,2,0:T(8,128)(2,1)S(1)}, u32[]{:S(2)}, u32[]{:S(2)}) %collective-permute-start.38) | collective-permute-done | bytes 270368 | tf_op jit(solution)/shard_map/ppermute | solution.py:16
  430.9 15.8 %collective-permute-start.43 = (bf16[1,64,33,64]{3,1,2,0:T(8,128)(2,1)}, bf16[1,64,33,64]{3,1,2,0:T(8,128)(2,1)}, u32[]{:S(2)}, u32[]{:S(2)}) collective-permute-start(bf16[1,64,33,64]{3,1,2,0:T(8,128)(2,1)} %fusion.7), channel_id=1, source_target_pairs={{110,0},{111,1},{112,2},{113,3},{114,4},{115,5},{116,6},{117,7},{1... | collective-permute-start | bytes 811016 | tf_op jit(solution)/shard_map/ppermute | solution.py:16
  446.7 11.0 %collective-permute-start.44 = (bf16[1,64,33,64]{3,1,2,0:T(8,128)(2,1)}, bf16[1,64,33,64]{3,1,2,0:T(8,128)(2,1)}, u32[]{:S(2)}, u32[]{:S(2)}) collective-permute-start(bf16[1,64,33,64]{3,1,2,0:T(8,128)(2,1)} %fusion.6), channel_id=1, source_target_pairs={{0,4},{1,5},{2,6},{3,7},{4,8},{5,9},{6,10},{7,11},{8,12},{9,13},{1... | collective-permute-start | bytes 811016 | tf_op jit(solution)/shard_map/ppermute | solution.py:16
  461.5 21.7 %collective-permute-start.47 = (bf16[1,64,33,64]{3,1,2,0:T(8,128)(2,1)}, bf16[1,64,33,64]{3,1,2,0:T(8,128)(2,1)}, u32[]{:S(2)}, u32[]{:S(2)}) collective-permute-start(bf16[1,64,33,64]{3,1,2,0:T(8,128)(2,1)} %fusion.5), channel_id=1, source_target_pairs={{28,0},{29,1},{30,2},{31,3},{32,4},{33,5},{34,6},{35,7},{36,8},{37... | collective-permute-start | bytes 811016 | tf_op jit(solution)/shard_map/ppermute | solution.py:16
  484.4 48.7 %collective-permute-done.45 = bf16[1,64,33,64]{3,1,2,0:T(8,128)(2,1)} collective-permute-done((bf16[1,64,33,64]{3,1,2,0:T(8,128)(2,1)}, bf16[1,64,33,64]{3,1,2,0:T(8,128)(2,1)}, u32[]{:S(2)}, u32[]{:S(2)}) %collective-permute-start.45) | collective-permute-done | bytes 270368 | tf_op jit(solution)/shard_map/ppermute | solution.py:16
  542.5 10.5 %all_to_all.12 = bf16[4,2,16896]{2,1,0:T(2,128)(2,1)S(1)} all-to-all(bf16[4,2,16896]{2,1,0:T(2,128)(2,1)S(1)} %reshape.1541), channel_id=1, replica_groups=mesh['curve'=64,'owner'=4] {'owner'}, dimensions={0} | all-to-all | bytes 540672 | tf_op jit(solution)/shard_map/all_to_all | solution.py:202
  (235 shorter events, 221.6 us)
Async XLA Ops:
  0.0 26.6 %collective-permute-start = (s32[8,4]{0,1:T(4,128)}, s32[8,4]{0,1:T(4,128)S(1)}, u32[]{:S(2)}, u32[]{:S(2)}) collective-permute-start(s32[8,4]{0,1:T(4,128)} %param.108), channel_id=1, source_target_pairs={{1,0},{2,1},{3,2},{4,3},{5,4},{6,5},{7,6},{8,7},{9,8},{10,9},{11,1... | collective-permute-start | bytes 392 | tf_op jit(solution)/shard_map/ppermute | solution.py:16
  7.0 29.3 %collective-permute-start.10 = (s32[8,4]{0,1:T(4,128)}, s32[8,4]{0,1:T(4,128)S(1)}, u32[]{:S(2)}, u32[]{:S(2)}) collective-permute-start(s32[8,4]{0,1:T(4,128)} %param.108), channel_id=1, source_target_pairs={{0,14},{1,15},{2,16},{3,17},{4,18},{5,19},{6,20},{7,21},{8,22},{9,... | collective-permute-start | bytes 392 | tf_op jit(solution)/shard_map/ppermute | solution.py:16
  16.0 81.1 %collective-permute-start.16 = (bf16[8,64,256]{2,1,0:T(8,128)(2,1)}, bf16[8,64,256]{2,1,0:T(8,128)(2,1)S(1)}, u32[]{:S(2)}, u32[]{:S(2)}) collective-permute-start(bf16[8,64,256]{2,1,0:T(8,128)(2,1)} %param.107), channel_id=1, source_target_pairs={{1,0},{2,1},{3,2},{4,3},{5,4},{6,5},{7,6},{8,7},{9,8},{10,9},{11,1... | collective-permute-start | bytes 786440 | tf_op jit(solution)/shard_map/ppermute | solution.py:16
  54.6 26.2 %collective-permute-start.6 = (s32[8,4]{0,1:T(4,128)S(1)}, s32[8,4]{0,1:T(4,128)S(1)}, u32[]{:S(2)}, u32[]{:S(2)}) collective-permute-start(s32[8,4]{0,1:T(4,128)S(1)} %copy-done.12), channel_id=1, source_target_pairs={{2,0},{3,1},{4,2},{5,3},{6,4},{7,5},{8,6},{9,7},{10,8},{11,9},{12,... | collective-permute-start | bytes 392 | tf_op jit(solution)/shard_map/ppermute | solution.py:16
  89.5 27.1 %collective-permute-start.20 = (bf16[8,64,256]{2,1,0:T(8,128)(2,1)S(1)}, bf16[8,64,256]{2,1,0:T(8,128)(2,1)S(1)}, u32[]{:S(2)}, u32[]{:S(2)}) collective-permute-start(bf16[8,64,256]{2,1,0:T(8,128)(2,1)S(1)} %copy-done.4), channel_id=1, source_target_pairs={{0,7},{1,8},{2,9},{3,10},{4,11},{5,12},{6,13},{7,14},{8,15},{9,16}... | collective-permute-start | bytes 786440 | tf_op jit(solution)/shard_map/ppermute | solution.py:16
  99.1 27.8 %collective-permute-start.22 = (bf16[8,64,256]{2,1,0:T(8,128)(2,1)S(1)}, bf16[8,64,256]{2,1,0:T(8,128)(2,1)S(1)}, u32[]{:S(2)}, u32[]{:S(2)}) collective-permute-start(bf16[8,64,256]{2,1,0:T(8,128)(2,1)S(1)} %copy-done.4), channel_id=1, source_target_pairs={{2,0},{3,1},{4,2},{5,3},{6,4},{7,5},{8,6},{9,7},{10,8},{11,9},{12,... | collective-permute-start | bytes 786440 | tf_op jit(solution)/shard_map/ppermute | solution.py:16
  126.9 25.4 %collective-permute-start.27 = (bf16[8,64,256]{2,1,0:T(8,128)(2,1)S(1)}, bf16[8,64,256]{2,1,0:T(8,128)(2,1)S(1)}, u32[]{:S(2)}, u32[]{:S(2)}) collective-permute-start(bf16[8,64,256]{2,1,0:T(8,128)(2,1)S(1)} %copy-done.4), channel_id=1, source_target_pairs={{0,110},{1,111},{2,112},{3,113},{4,114},{5,115},{6,116},{7,117},{8... | collective-permute-start | bytes 786440 | tf_op jit(solution)/shard_map/ppermute | solution.py:16
  128.9 24.1 %collective-permute-start.28 = (bf16[8,64,256]{2,1,0:T(8,128)(2,1)S(1)}, bf16[8,64,256]{2,1,0:T(8,128)(2,1)S(1)}, u32[]{:S(2)}, u32[]{:S(2)}) collective-permute-start(bf16[8,64,256]{2,1,0:T(8,128)(2,1)S(1)} %copy-done.4), channel_id=1, source_target_pairs={{4,0},{5,1},{6,2},{7,3},{8,4},{9,5},{10,6},{11,7},{12,8},{13,9},{1... | collective-permute-start | bytes 786440 | tf_op jit(solution)/shard_map/ppermute | solution.py:16
  333.5 29.1 %collective-permute-start.32 = (bf16[1,64,33,64]{3,1,2,0:T(8,128)(2,1)}, bf16[1,64,33,64]{3,1,2,0:T(8,128)(2,1)}, u32[]{:S(2)}, u32[]{:S(2)}) collective-permute-start(bf16[1,64,33,64]{3,1,2,0:T(8,128)(2,1)} %fusion.10), channel_id=1, source_target_pairs={{0,1},{1,2},{2,3},{3,4},{4,5},{5,6},{6,7},{7,8},{8,9},{9,10},{10,1... | collective-permute-start | bytes 811016 | tf_op jit(solution)/shard_map/ppermute | solution.py:16
  341.7 33.1 %collective-permute-start.33 = (bf16[1,64,33,64]{3,1,2,0:T(8,128)(2,1)}, bf16[1,64,33,64]{3,1,2,0:T(8,128)(2,1)}, u32[]{:S(2)}, u32[]{:S(2)}) collective-permute-start(bf16[1,64,33,64]{3,1,2,0:T(8,128)(2,1)} %fusion.10), channel_id=1, source_target_pairs={{0,7},{1,8},{2,9},{3,10},{4,11},{5,12},{6,13},{7,14},{8,15},{9,16}... | collective-permute-start | bytes 811016 | tf_op jit(solution)/shard_map/ppermute | solution.py:16
  344.2 36.3 %collective-permute-start.34 = (bf16[1,64,33,64]{3,1,2,0:T(8,128)(2,1)}, bf16[1,64,33,64]{3,1,2,0:T(8,128)(2,1)}, u32[]{:S(2)}, u32[]{:S(2)}) collective-permute-start(bf16[1,64,33,64]{3,1,2,0:T(8,128)(2,1)} %fusion.10), channel_id=1, source_target_pairs={{0,55},{1,56},{2,57},{3,58},{4,59},{5,60},{6,61},{7,62},{8,63},{9,... | collective-permute-start | bytes 811016 | tf_op jit(solution)/shard_map/ppermute | solution.py:16
  347.2 35.3 %collective-permute-start.35 = (bf16[1,64,33,64]{3,1,2,0:T(8,128)(2,1)}, bf16[1,64,33,64]{3,1,2,0:T(8,128)(2,1)}, u32[]{:S(2)}, u32[]{:S(2)}) collective-permute-start(bf16[1,64,33,64]{3,1,2,0:T(8,128)(2,1)} %fusion.9), channel_id=1, source_target_pairs={{1,0},{2,1},{3,2},{4,3},{5,4},{6,5},{7,6},{8,7},{9,8},{10,9},{11,1... | collective-permute-start | bytes 811016 | tf_op jit(solution)/shard_map/ppermute | solution.py:16
  353.5 30.3 %collective-permute-start.36 = (bf16[1,64,33,64]{3,1,2,0:T(8,128)(2,1)}, bf16[1,64,33,64]{3,1,2,0:T(8,128)(2,1)}, u32[]{:S(2)}, u32[]{:S(2)}) collective-permute-start(bf16[1,64,33,64]{3,1,2,0:T(8,128)(2,1)} %fusion.9), channel_id=1, source_target_pairs={{7,0},{8,1},{9,2},{10,3},{11,4},{12,5},{13,6},{14,7},{15,8},{16,9}... | collective-permute-start | bytes 811016 | tf_op jit(solution)/shard_map/ppermute | solution.py:16
  362.6 29.1 %collective-permute-start.37 = (bf16[1,64,33,64]{3,1,2,0:T(8,128)(2,1)}, bf16[1,64,33,64]{3,1,2,0:T(8,128)(2,1)}, u32[]{:S(2)}, u32[]{:S(2)}) collective-permute-start(bf16[1,64,33,64]{3,1,2,0:T(8,128)(2,1)} %fusion.9), channel_id=1, source_target_pairs={{55,0},{56,1},{57,2},{58,3},{59,4},{60,5},{61,6},{62,7},{63,8},{64... | collective-permute-start | bytes 811016 | tf_op jit(solution)/shard_map/ppermute | solution.py:16
  374.9 56.0 %collective-permute-start.38 = (bf16[1,64,33,64]{3,1,2,0:T(8,128)(2,1)}, bf16[1,64,33,64]{3,1,2,0:T(8,128)(2,1)S(1)}, u32[]{:S(2)}, u32[]{:S(2)}) collective-permute-start(bf16[1,64,33,64]{3,1,2,0:T(8,128)(2,1)} %fusion.8), channel_id=1, source_target_pairs={{0,2},{1,3},{2,4},{3,5},{4,6},{5,7},{6,8},{7,9},{8,10},{9,11},{10,... | collective-permute-start | bytes 811016 | tf_op jit(solution)/shard_map/ppermute | solution.py:16
  380.5 66.1 %collective-permute-start.39 = (bf16[1,64,33,64]{3,1,2,0:T(8,128)(2,1)}, bf16[1,64,33,64]{3,1,2,0:T(8,128)(2,1)S(1)}, u32[]{:S(2)}, u32[]{:S(2)}) collective-permute-start(bf16[1,64,33,64]{3,1,2,0:T(8,128)(2,1)} %fusion.8), channel_id=1, source_target_pairs={{0,14},{1,15},{2,16},{3,17},{4,18},{5,19},{6,20},{7,21},{8,22},{9,... | collective-permute-start | bytes 811016 | tf_op jit(solution)/shard_map/ppermute | solution.py:16
  382.5 75.2 %collective-permute-start.40 = (bf16[1,64,33,64]{3,1,2,0:T(8,128)(2,1)}, bf16[1,64,33,64]{3,1,2,0:T(8,128)(2,1)}, u32[]{:S(2)}, u32[]{:S(2)}) collective-permute-start(bf16[1,64,33,64]{3,1,2,0:T(8,128)(2,1)} %fusion.8), channel_id=1, source_target_pairs={{0,110},{1,111},{2,112},{3,113},{4,114},{5,115},{6,116},{7,117},{8... | collective-permute-start | bytes 811016 | tf_op jit(solution)/shard_map/ppermute | solution.py:16
  383.8 75.8 %collective-permute-start.41 = (bf16[1,64,33,64]{3,1,2,0:T(8,128)(2,1)}, bf16[1,64,33,64]{3,1,2,0:T(8,128)(2,1)}, u32[]{:S(2)}, u32[]{:S(2)}) collective-permute-start(bf16[1,64,33,64]{3,1,2,0:T(8,128)(2,1)} %fusion.7), channel_id=1, source_target_pairs={{2,0},{3,1},{4,2},{5,3},{6,4},{7,5},{8,6},{9,7},{10,8},{11,9},{12,... | collective-permute-start | bytes 811016 | tf_op jit(solution)/shard_map/ppermute | solution.py:16
  391.7 69.8 %collective-permute-start.42 = (bf16[1,64,33,64]{3,1,2,0:T(8,128)(2,1)}, bf16[1,64,33,64]{3,1,2,0:T(8,128)(2,1)}, u32[]{:S(2)}, u32[]{:S(2)}) collective-permute-start(bf16[1,64,33,64]{3,1,2,0:T(8,128)(2,1)} %fusion.7), channel_id=1, source_target_pairs={{14,0},{15,1},{16,2},{17,3},{18,4},{19,5},{20,6},{21,7},{22,8},{23... | collective-permute-start | bytes 811016 | tf_op jit(solution)/shard_map/ppermute | solution.py:16
  430.9 53.5 %collective-permute-start.43 = (bf16[1,64,33,64]{3,1,2,0:T(8,128)(2,1)}, bf16[1,64,33,64]{3,1,2,0:T(8,128)(2,1)}, u32[]{:S(2)}, u32[]{:S(2)}) collective-permute-start(bf16[1,64,33,64]{3,1,2,0:T(8,128)(2,1)} %fusion.7), channel_id=1, source_target_pairs={{110,0},{111,1},{112,2},{113,3},{114,4},{115,5},{116,6},{117,7},{1... | collective-permute-start | bytes 811016 | tf_op jit(solution)/shard_map/ppermute | solution.py:16
  446.7 37.7 %collective-permute-start.44 = (bf16[1,64,33,64]{3,1,2,0:T(8,128)(2,1)}, bf16[1,64,33,64]{3,1,2,0:T(8,128)(2,1)}, u32[]{:S(2)}, u32[]{:S(2)}) collective-permute-start(bf16[1,64,33,64]{3,1,2,0:T(8,128)(2,1)} %fusion.6), channel_id=1, source_target_pairs={{0,4},{1,5},{2,6},{3,7},{4,8},{5,9},{6,10},{7,11},{8,12},{9,13},{1... | collective-permute-start | bytes 811016 | tf_op jit(solution)/shard_map/ppermute | solution.py:16
  457.6 75.4 %collective-permute-start.45 = (bf16[1,64,33,64]{3,1,2,0:T(8,128)(2,1)}, bf16[1,64,33,64]{3,1,2,0:T(8,128)(2,1)}, u32[]{:S(2)}, u32[]{:S(2)}) collective-permute-start(bf16[1,64,33,64]{3,1,2,0:T(8,128)(2,1)} %fusion.6), channel_id=1, source_target_pairs={{0,28},{1,29},{2,30},{3,31},{4,32},{5,33},{6,34},{7,35},{8,36},{9,... | collective-permute-start | bytes 811016 | tf_op jit(solution)/shard_map/ppermute | solution.py:16
  459.6 73.5 %collective-permute-start.46 = (bf16[1,64,33,64]{3,1,2,0:T(8,128)(2,1)}, bf16[1,64,33,64]{3,1,2,0:T(8,128)(2,1)}, u32[]{:S(2)}, u32[]{:S(2)}) collective-permute-start(bf16[1,64,33,64]{3,1,2,0:T(8,128)(2,1)} %fusion.5), channel_id=1, source_target_pairs={{4,0},{5,1},{6,2},{7,3},{8,4},{9,5},{10,6},{11,7},{12,8},{13,9},{1... | collective-permute-start | bytes 811016 | tf_op jit(solution)/shard_map/ppermute | solution.py:16
  461.5 71.6 %collective-permute-start.47 = (bf16[1,64,33,64]{3,1,2,0:T(8,128)(2,1)}, bf16[1,64,33,64]{3,1,2,0:T(8,128)(2,1)}, u32[]{:S(2)}, u32[]{:S(2)}) collective-permute-start(bf16[1,64,33,64]{3,1,2,0:T(8,128)(2,1)} %fusion.5), channel_id=1, source_target_pairs={{28,0},{29,1},{30,2},{31,3},{32,4},{33,5},{34,6},{35,7},{36,8},{37... | collective-permute-start | bytes 811016 | tf_op jit(solution)/shard_map/ppermute | solution.py:16
  (58 other events, 1054.4 us)
where the time goes:
time: 562 us; the launch traced here: 555 us
  starting transfers between devices  234 us (42%)
  local copies, waits for them, and re-layouts  115 us (20%)
  waiting for transfers between devices  91.5 us (16%)
  matrix products  86.8 us (15%)
  other arithmetic  15.1 us (3%)
  blocking collectives  10.5 us (2%)
    ppermute x48, starting transfers between devices, shifted_2(): return lax.ppermute(value, axis, pairs)  234 us
    ppermute x48, waiting for transfers between devices, shifted_2(): return lax.ppermute(value, axis, pairs)  91.5 us
    dot_general x4, matrix products, one_group(): jnp.einsum('ixoc,iu->uxoc', contrib, unit_rows[:, slot, :], precision=hig...  43.4 us
    dot_general x4, local copies, waits for them, and re-layouts, one_group(): jnp.einsum('iax,iaoc->ixoc', p_rows[:, :, slot, :], product_ap, preferred...  39.6 us
    slice x2, local copies, waits for them, and re-layouts, shards(): partial_rel[:, unit_id][:, :, source, :]  24.5 us
    dot_general x4, matrix products, one_group(): jnp.einsum('iax,iaoc->ixoc', p_rows[:, :, slot, :], product_ap, preferred...  23.1 us
    dot_general x1, matrix products, one_group(): jnp.einsum('iakmc,ikmo->iaoc', product, route_rows, precision=highest)  17.9 us
    unnamed x90, local copies, waits for them, and re-layouts  14.9 us
  transfers between devices with their start and end apart: 48, of which 4 were waited for; matrix products, arithmetic and copies ran while one was open for 6% of the time, Pallas kernels for 0%

commit v1 on v0

v1 whole, which is shorter than its diff:
```python
import jax
import jax.numpy as jnp
from jax import lax
from jax.experimental import pallas as pl
from jax.experimental.pallas import tpu as pltpu
from jax.sharding import PartitionSpec as P


W = 64
G = 8
AXES = (0, 1, 2)
F32 = jnp.float32
BF16 = jnp.bfloat16
ZERO = (0, 0, 0)


def step(axis, sign):
    return tuple(sign if a == axis else 0 for a in AXES)


def plus(u, v):
    return tuple(a + b for a, b in zip(u, v))


def both(a, sa, b, sb):
    return plus(step(a, sa), step(b, sb))


def axis_mask(axis, bits):
    return sum(1 << b for b in range(bits) if b % 3 == axis)


ROW = [
    (ZERO, step(0, 1)),
    (step(1, 1), step(2, 1)),
    (step(0, -1), step(1, -1)),
    (step(2, -1), both(0, 1, 1, 1)),
    (both(0, 1, 2, 1), both(1, 1, 2, 1)),
]
FACES = [
    (ZERO, step(0, 1)),
    (step(0, -1), step(1, 1)),
    (step(1, -1), step(2, 1)),
    (step(2, -1), None),
]
PAIRS = ((0, 1), (0, 2), (1, 2))


def edge_columns(a, b):
    return [
        (both(a, 1, b, 1), both(a, 1, b, -1)),
        (both(a, -1, b, -1), both(a, -1, b, 1)),
    ]


OWN = FACES + [c for a, b in PAIRS for c in edge_columns(a, b)]


def side_columns(axis, sign):
    out = [(pair, (n, n)) for n, pair in enumerate(FACES)]
    for p, (a, b) in enumerate(PAIRS):
        n = 4 + 2 * p
        first, second = edge_columns(a, b)
        if axis == a:
            out.append((first, (n, n)) if sign > 0 else (second, (n + 1, n + 1)))
        elif axis == b:
            if sign > 0:
                out.append(((first[0], second[1]), (n, n + 1)))
            else:
                out.append(((second[0], first[1]), (n + 1, n)))
        else:
            out.append((first, (n, n)))
            out.append((second, (n + 1, n + 1)))
    return out


def corner(x, y, z):
    return (x, y, z)


FULL = (
    FACES[:3]
    + [(step(2, -1), step(0, 2))]
    + OWN[4:]
    + [
        (corner(1, 1, 1), corner(1, 1, -1)),
        (corner(1, -1, -1), corner(1, -1, 1)),
        (corner(-1, 1, 1), corner(-1, 1, -1)),
        (corner(-1, -1, -1), corner(-1, -1, 1)),
        (step(0, -2), step(1, 2)),
        (step(1, -2), step(2, 2)),
        (step(2, -2), None),
    ]
)


def offset_table():
    table = []
    for x in range(-2, 3):
        for y in range(-2, 3):
            for z in range(-2, 3):
                if sum(max(0, 2 * abs(v) - 1) for v in (x, y, z)) <= 3:
                    table.append((x, y, z))
    return table


def mirrored(slot, axis):
    return tuple(-v if a == axis else v for a, v in enumerate(slot))


def arrived_layout(axis, sign):
    back = []
    for pair, _ in side_columns(axis, sign):
        back.append(
            tuple(
                None if s is None else plus(mirrored(s, axis), step(axis, sign))
                for s in pair
            )
        )
    return back


def places(layout):
    return {
        slot: (n, h)
        for n, pair in enumerate(layout)
        for h, slot in enumerate(pair)
        if slot is not None
    }


class Columns:
    def __init__(self, columns):
        self.columns = columns
        self.turned = {}

    def get(self, n, turn):
        if not turn:
            return self.columns[n]
        if n not in self.turned:
            self.turned[n] = swap(self.columns[n])
        return self.turned[n]


def swap(column):
    if column.dtype == F32:
        return pltpu.roll(column, W, 1)
    return pltpu.roll(column.astype(F32), W, 1).astype(column.dtype)


def compose(source, left_at, right_at, left):
    if left_at is None and right_at is None:
        return None
    a = None if left_at is None else source.get(left_at[0], left_at[1] != 0)
    b = None if right_at is None else source.get(right_at[0], right_at[1] != 1)
    if a is None:
        return jnp.where(left, jnp.zeros_like(b), b)
    if b is None:
        return jnp.where(left, a, jnp.zeros_like(a))
    if left_at[0] == right_at[0] and left_at[1] == 0 and right_at[1] == 1:
        return a
    if left_at[0] == right_at[0] and left_at[1] == 1 and right_at[1] == 0:
        return a
    return jnp.where(left, a, b)


def left_half(rows):
    return lax.broadcasted_iota(jnp.int32, (rows, 128), 1) < W


def split(value):
    return [value[:, n * 128 : (n + 1) * 128] for n in range(value.shape[1] // 128)]


def flag(condition):
    return jnp.where(condition, jnp.int32(1), jnp.int32(0))


def order_kernel(bits, columns, p_ref, own_ref, *side_refs):
    device = columns[0, 0]
    turn = 7 - (device & 7)
    left = left_half(W)
    for member in range(G):
        row = member ^ turn
        raw = p_ref[row].astype(F32)
        first, second = raw[:, :128], raw[:, 128:]
        first_t, second_t = swap(first), swap(second)
        wide = [
            jnp.where(left, first_t, first),
            jnp.where(left, second, second_t),
            jnp.where(left, second_t, second),
        ]
        a = jnp.where(left, first, 0.0)
        b = jnp.zeros((W, 128), F32)
        for m in (1, 2, 3):
            gap = columns[row, m] ^ device
            along = [
                flag((gap & axis_mask(axis, bits)) != 0).astype(F32) for axis in AXES
            ]
            stays = flag(gap == 0).astype(F32)
            a = a + jnp.where(left, stays, along[0]) * wide[m - 1]
            b = b + jnp.where(left, along[1], along[2]) * wide[m - 1]
        a, b = a.astype(BF16), b.astype(BF16)
        own_ref[member, :, :128] = a
        own_ref[member, :, 128:] = b
        for axis in AXES:
            side = side_refs[2 * axis + (member >> axis & 1)]
            rest = half_index(member, axis)
            side[rest, :, :128] = a
            side[rest, :, 128:] = b


def half_index(member, axis):
    others = [a for a in AXES if a != axis]
    return (member >> others[0] & 1) + 2 * (member >> others[1] & 1)


def product_kernel(
    bits, columns, a_ref, own_ref, e0, o0, e1, o1, e2, o2, sum_ref, *rest
):
    outs, (w_ref, b_ref, l_ref, lt_ref) = rest[:6], rest[6:]
    halo = ((e0, o0), (e1, o1), (e2, o2))
    device = columns[0, 0] >> 3
    turn = 7 - (device & 7)
    left = left_half(W)
    missing = []
    for axis in AXES:
        mask = axis_mask(axis, bits)
        here = device & mask
        missing.append(flag(here == 0) + flag(here == mask))
    blocks = ((0, 0), (0, 1), (1, 0), (1, 1))
    row_places = places(ROW)
    zeros = jnp.zeros((W, 128), BF16)

    def arranged(source, where):
        out = []
        for pair in ROW:
            at = [blocks[where[s]] if s in where else None for s in pair]
            column = compose(source, at[0], at[1], left)
            out.append(zeros if column is None else column)
        return out

    def outward(axis):
        return step(axis, 1)

    self_where = {ZERO: 0}
    for axis in AXES:
        self_where[outward(axis)] = axis + 1
    for member in range(G):
        row = member ^ turn
        buffer = member
        inner = [jnp.int32(0)] * 3
        outer = [jnp.int32(0)] * 3
        edge = [jnp.int32(0)] * 3
        count = jnp.int32(0)
        for k in range(1, 7):
            entry = columns[row, k]
            gap = (entry & 7) ^ row
            near = flag((entry >> 3) == device)
            for axis in AXES:
                hit = flag(gap == (1 << axis))
                inner[axis] = inner[axis] + k * hit * near
                outer[axis] = outer[axis] + k * hit * (1 - near)
            ends = flag(gap == 0)
            for n in range(3):
                edge[n] = edge[n] + k * ends * flag(count == n)
            count = count + ends
        absent = [missing[axis] * (member >> axis & 1) for axis in AXES]
        rank = jnp.int32(0)
        for axis in AXES:
            if member >> axis & 1:
                at = jnp.where(
                    rank == 0, edge[0], jnp.where(rank == 1, edge[1], edge[2])
                )
                outer[axis] = outer[axis] + absent[axis] * at
                rank = rank + absent[axis]

        def put(position, columns_):
            for n, column in enumerate(columns_):
                w_ref[buffer, position, :, n * 128 : (n + 1) * 128] = column

        mine = Columns(split(own_ref[member]))
        self_columns = arranged(mine, self_where)
        put(0, self_columns)
        for axis in AXES:
            others = [b for b in AXES if b != axis]
            where = {ZERO: 0, step(axis, -1): axis + 1}
            for b in others:
                where[outward(b)] = b + 1
            put(
                inner[axis],
                arranged(Columns(split(own_ref[member ^ (1 << axis)])), where),
            )
            where = {outward(axis): 0, ZERO: axis + 1}
            for b in others:
                where[plus(outward(axis), outward(b))] = b + 1
            side = member >> axis & 1
            there = arranged(
                Columns(split(halo[axis][side][half_index(member, axis)])), where
            )
            if side:
                there = [
                    jnp.where(absent[axis] == 1, s, t)
                    for s, t in zip(self_columns, there)
                ]
            put(outer[axis], there)
        factor = a_ref[row]
        source = []
        for first, last in ((0, 256), (256, 512), (512, 640)):
            source += split(
                jnp.dot(
                    factor,
                    w_ref[buffer, :7, :, first:last].reshape(7 * W, last - first),
                    preferred_element_type=F32,
                )
            )
        source = Columns(source)

        def local(slot):
            if slot is None:
                return None
            turned = tuple(
                v if member >> a & 1 else -v for a, v in enumerate(slot)
            )
            return row_places.get(turned)

        for n, pair in enumerate(OWN):
            column = compose(source, local(pair[0]), local(pair[1]), left)
            column = zeros if column is None else column.astype(BF16)
            b_ref[member * W : (member + 1) * W, n * 128 : (n + 1) * 128] = column
        wanted = [(0, 0)]
        for axis in AXES:
            side = member >> axis & 1
            for s in (0, 1):
                wanted.append(blocks[axis + 1] if s == side else None)
        wanted.append(None)
        for n in range(4):
            column = compose(mine, wanted[2 * n], wanted[2 * n + 1], left)
            l_ref[member * W : (member + 1) * W, n * 128 : (n + 1) * 128] = (
                zeros if column is None else column
            )
    lt_ref[...] = l_ref[...].T
    held = {}
    done = 0
    for chunk in range(len(OWN) // 2):
        total = jnp.dot(
            lt_ref[: 7 * W],
            b_ref[:, chunk * 256 : (chunk + 1) * 256],
            preferred_element_type=F32,
        )
        for half in (0, 1):
            held[2 * chunk + half] = total[:, half * 128 : (half + 1) * 128]
            n = 2 * chunk + half
            sum_ref[:, n * 128 : (n + 1) * 128] = held[n][:W]
        for axis in AXES:
            for s in (0, 1):
                rows = slice((1 + 2 * axis + s) * W, (2 + 2 * axis + s) * W)
                for n, (_, (i, j)) in enumerate(side_columns(axis, 2 * s - 1)):
                    if max(i, j) // 2 != chunk:
                        continue
                    column = (
                        held[i][rows]
                        if i == j
                        else jnp.where(left, held[i][rows], held[j][rows])
                    )
                    outs[2 * axis + s][:, n * 128 : (n + 1) * 128] = column.astype(BF16)


def gather_kernel(sum_ref, even0, even1, o0, o1, e2, o2, out_ref):
    rows = 16
    left = left_half(rows)
    arrived = [
        (0, 1, o0),
        (1, 1, o1),
        (2, -1, e2),
        (2, 1, o2),
    ]
    for part in range(W // rows):
        span = slice(part * rows, (part + 1) * rows)
        sources = [(Columns(split(sum_ref[span])), places(OWN))]
        for axis, sign, ref in arrived:
            sources.append(
                (
                    Columns(split(ref[span].astype(F32))),
                    places(arrived_layout(axis, sign)),
                )
            )
        for n, pair in enumerate(FULL):
            total = None
            for source, where in sources:
                column = compose(
                    source, where.get(pair[0]), where.get(pair[1]), left
                )
                if column is not None:
                    total = column if total is None else total + column
            if total is None:
                total = jnp.zeros((rows, 128), F32)
            out_ref[part, :, n * 128 : (n + 1) * 128] = total.astype(BF16)
        wide = len(FULL) * 128
        out_ref[part, :, wide : wide + 1024] = even0[span]
        out_ref[part, :, wide + 1024 : wide + 2048] = even1[span]


def finish_kernel(columns, y_ref, out_ref):
    device = columns[0, 0]
    rows = 16
    left = left_half(rows)
    offsets = offset_table()
    wide = len(FULL) * 128

    def write(core):
        for member in range(4):
            signs = (2 * (member & 1) - 1, 2 * (member >> 1) - 1, 2 * core - 1)

            def seen(layout):
                return {
                    tuple(v * s for v, s in zip(slot, signs)): at
                    for slot, at in places(layout).items()
                }

            def columns_of(part, first, count):
                value = y_ref[part, :, first : first + count * 128].astype(F32)
                return Columns(split(value))

            sources = [
                (columns_of(member, 0, len(FULL)), seen(FULL)),
                (columns_of(member ^ 1, wide, 8), seen(arrived_layout(0, -1))),
                (columns_of(member ^ 2, wide + 1024, 8), seen(arrived_layout(1, -1))),
            ]
            for n in range(17):
                pair = (offsets[2 * n], offsets[2 * n + 1] if n < 16 else None)
                total = None
                for source, where in sources:
                    column = compose(
                        source, where.get(pair[0]), where.get(pair[1]), left
                    )
                    if column is not None:
                        total = column if total is None else total + column
                total = total.astype(BF16)
                if n < 16:
                    out_ref[member, :, n * 128 : (n + 1) * 128] = total
                else:
                    out_ref[member, :, n * 128 : n * 128 + W] = total[:, :W]

    bit = device >> 2 & 1
    pl.when(bit == 0)(lambda: write(0))
    pl.when(bit == 1)(lambda: write(1))


VMEM = pl.BlockSpec(memory_space=pltpu.VMEM)
SMEM = pl.BlockSpec(memory_space=pltpu.SMEM)


def call(kernel, name, outs, n_in, scratch=(), flops=0, size=0):
    return pl.pallas_call(
        kernel,
        out_shape=[jax.ShapeDtypeStruct(s, d) for s, d in outs],
        in_specs=n_in,
        out_specs=[VMEM] * len(outs),
        scratch_shapes=list(scratch),
        compiler_params=pltpu.CompilerParams(vmem_limit_bytes=32 * 1024 * 1024),
        cost_estimate=pl.CostEstimate(
            flops=flops, bytes_accessed=size, transcendentals=0
        ),
        name=name,
    )


def decode(device, bits):
    position = [0, 0, 0]
    for b in range(bits):
        position[b % 3] += (device >> b & 1) << (b // 3)
    return position


def encode(position, bits):
    return sum((position[b % 3] >> (b // 3) & 1) << b for b in range(bits))


def pairs_of(axis, odd, bits):
    extent = 1 << len([b for b in range(bits) if b % 3 == axis])
    out = []
    for device in range(1 << bits):
        position = decode(device, bits)
        sense = 2 * (position[axis] & 1) - 1
        position[axis] += sense if odd else -sense
        if 0 <= position[axis] < extent:
            out.append((encode(position, bits), device))
    return out


def shards(operator_blocks, operator_columns, prolong_blocks, prolong_columns):
    devices = lax.axis_size("curve") * lax.axis_size("owner")
    bits = devices.bit_length() - 1

    def swapped(value, axis, odd):
        return lax.ppermute(value, ("curve", "owner"), pairs_of(axis, odd, bits))

    half = ((4, W, 256), BF16)
    ordered = call(
        lambda *refs: order_kernel(bits, *refs),
        "order",
        [((G, W, 256), BF16)] + [half] * 6,
        [SMEM, VMEM],
        size=1300000,
    )(prolong_columns, prolong_blocks)
    own, sides = ordered[0], ordered[1:]
    halo = [swapped(sides[2 * a + o], a, bool(o)) for a in AXES for o in (0, 1)]
    side = ((W, 1024), BF16)
    sums = call(
        lambda *refs: product_kernel(bits, *refs),
        "products",
        [((W, 1280), F32)] + [side] * 6,
        [SMEM] + [VMEM] * 8,
        [
            pltpu.VMEM((G, 7, W, 640), BF16),
            pltpu.VMEM((G * W, 1280), BF16),
            pltpu.VMEM((G * W, G * W), BF16),
            pltpu.VMEM((G * W, G * W), BF16),
        ],
        flops=900000000,
        size=2600000,
    )(operator_columns, operator_blocks, own, *halo)
    total, (e0, o0, e1, o1, e2, o2) = sums[0], sums[1:]
    o0, o1, o2 = swapped(o0, 0, True), swapped(o1, 1, True), swapped(o2, 2, True)
    e2 = swapped(e2, 2, False)
    width = len(FULL) * 128 + 2048
    gathered = call(
        gather_kernel, "gather", [((4, 16, width), BF16)], [VMEM] * 7, size=1700000
    )(total, e0, e1, o0, o1, e2, o2)[0]
    spread = lax.all_to_all(
        gathered, "owner", split_axis=0, concat_axis=0, tiled=True
    )
    return call(
        finish_kernel, "finish", [((4, 16, 33 * W), BF16)], [SMEM, VMEM], size=900000
    )(prolong_columns, spread)[0]


def solution(mesh):
    return jax.shard_map(
        shards,
        mesh=mesh,
        in_specs=(
            P(("curve", "owner"), None, None),
            P(("curve", "owner"), None),
            P(("curve", "owner"), None, None),
            P(("curve", "owner"), None),
        ),
        out_specs=P("curve", "owner", None),
        check_vma=False,
    )
```

time: 562 us -> 67.3 us (0.12)
  the two profiles are of different devices: /device:TPU:89 before, /device:TPU:25 now
where the time goes in v1:
time: 67.3 us; the launch traced here: 66.2 us
  starting transfers between devices  39.8 us (59%)
  blocking collectives  9.39 us (14%)
  waiting for transfers between devices  8.15 us (12%)
  Pallas kernels  5.99 us (9%)
  local copies, waits for them, and re-layouts  2.75 us (4%)
    ppermute x10, starting transfers between devices, swapped(): return lax.ppermute(value, ('curve', 'owner'), pairs_of(axis, odd, bits))  39.8 us
    all_to_all x1, blocking collectives, shards(): lax.all_to_all(gathered, 'owner', split_axis=0, concat_axis=0, tiled=True)  9.39 us
    ppermute x10, waiting for transfers between devices, swapped(): return lax.ppermute(value, ('curve', 'owner'), pairs_of(axis, odd, bits))  8.15 us
    pallas_call x1, Pallas kernels, shards(): call(lambda *refs: product_kernel(bits, *refs), 'products', [((W, 1280),...  3.41 us
    unnamed x7, local copies, waits for them, and re-layouts  2.75 us
    pallas_call x1, Pallas kernels, shards(): call(finish_kernel, 'finish', [((4, 16, 33 * W), BF16)], [SMEM, VMEM], si...  1.52 us
  transfers between devices with their start and end apart: 10, of which 3 were waited for; matrix products, arithmetic and copies ran while one was open for 0% of the time, Pallas kernels for 0%

profile of v1, /device:TPU:25, one launch (start us, length us, event | category | flops | bytes accessed | tf_op | source)
XLA Modules:
  0.0 66.2 jit_solution(7693173962063243930)
XLA Ops:
  0.0 0.8 %copy.6.refs_0_.columns = s32[8,4]{1,0:T(8,128)S(1)} copy(s32[8,4]{0,1:T(4,128)} %param.7) | data formatting | bytes 256 | tf_op args[3]
  0.8 0.9 %copy-done = bf16[8,64,256]{2,1,0:T(8,128)(2,1)S(1)} copy-done((bf16[8,64,256]{2,1,0:T(8,128)(2,1)S(1)}, bf16[8,64,256]{2,1,0:T(8,128)(2,1)}, u32[]{:S(2)}) %copy-start) | copy-done | bytes 262168
  1.7 0.9 %order.1 = (bf16[8,64,256]{2,1,0:T(8,128)(2,1)S(1)}, bf16[4,64,256]{2,1,0:T(8,128)(2,1)S(1)}, bf16[4,64,256]{2,1,0:T(8,128)(2,1)S(1)}, bf16[4,64,256]{2,1,0:T(8,...) custom-call(s32[8,4]{1,0:T(8,128)S(1)} %copy.6.refs_0_.columns, ...), custom_call_target="tpu_custom_call" | custom-call | bytes 1300000 | tf_op jit(solution)/shard_map/order/pallas_call | solution.py:500
  2.6 1.3 %collective-permute-start = (bf16[4,64,256]{2,1,0:T(8,128)(2,1)S(1)}, bf16[4,64,256]{2,1,0:T(8,128)(2,1)S(1)}, u32[]{:S(2)}, u32[]{:S(2)}) collective-permute-start(bf16[4,64,256]{2,1,0:T(8,128)(2,1)S(1)} %get-tuple-element.20), channel_id=1, source_target_pairs={{1,0},{0,1},{3,2},{2,3},{5,4},{4,5},{7,6},{6,7},{9,8},{8,9},{11,10... | collective-permute-start | bytes 393224 | tf_op jit(solution)/shard_map/ppermute | solution.py:497
  3.9 3.7 %collective-permute-start.1 = (bf16[4,64,256]{2,1,0:T(8,128)(2,1)S(1)}, bf16[4,64,256]{2,1,0:T(8,128)(2,1)S(1)}, u32[]{:S(2)}, u32[]{:S(2)}) collective-permute-start(bf16[4,64,256]{2,1,0:T(8,128)(2,1)S(1)} %get-tuple-element.21), channel_id=1, source_target_pairs={{8,1},{10,3},{12,5},{14,7},{1,8},{64,9},{3,10},{66,11},{5,12},{68,... | collective-permute-start | bytes 393224 | tf_op jit(solution)/shard_map/ppermute | solution.py:497
  7.6 0.0 copy-start.2
  7.6 2.8 %collective-permute-start.2 = (bf16[4,64,256]{2,1,0:T(8,128)(2,1)S(1)}, bf16[4,64,256]{2,1,0:T(8,128)(2,1)S(1)}, u32[]{:S(2)}, u32[]{:S(2)}) collective-permute-start(bf16[4,64,256]{2,1,0:T(8,128)(2,1)S(1)} %get-tuple-element.22), channel_id=1, source_target_pairs={{2,0},{3,1},{0,2},{1,3},{6,4},{7,5},{4,6},{5,7},{10,8},{11,9},{8,1... | collective-permute-start | bytes 393224 | tf_op jit(solution)/shard_map/ppermute | solution.py:497
  10.4 5.2 %collective-permute-start.3 = (bf16[4,64,256]{2,1,0:T(8,128)(2,1)S(1)}, bf16[4,64,256]{2,1,0:T(8,128)(2,1)S(1)}, u32[]{:S(2)}, u32[]{:S(2)}) collective-permute-start(bf16[4,64,256]{2,1,0:T(8,128)(2,1)S(1)} %get-tuple-element.23), channel_id=1, source_target_pairs={{16,2},{17,3},{20,6},{21,7},{24,10},{25,11},{28,14},{29,15},{2,16}... | collective-permute-start | bytes 393224 | tf_op jit(solution)/shard_map/ppermute | solution.py:497
  15.6 1.9 %collective-permute-start.4 = (bf16[4,64,256]{2,1,0:T(8,128)(2,1)S(1)}, bf16[4,64,256]{2,1,0:T(8,128)(2,1)S(1)}, u32[]{:S(2)}, u32[]{:S(2)}) collective-permute-start(bf16[4,64,256]{2,1,0:T(8,128)(2,1)S(1)} %get-tuple-element.24), channel_id=1, source_target_pairs={{4,0},{5,1},{6,2},{7,3},{0,4},{1,5},{2,6},{3,7},{12,8},{13,9},{14,... | collective-permute-start | bytes 393224 | tf_op jit(solution)/shard_map/ppermute | solution.py:497
  17.5 0.0 collective-permute-done.refs_3_
  17.5 6.0 %collective-permute-start.5 = (bf16[4,64,256]{2,1,0:T(8,128)(2,1)S(1)}, bf16[4,64,256]{2,1,0:T(8,128)(2,1)S(1)}, u32[]{:S(2)}, u32[]{:S(2)}) collective-permute-start(bf16[4,64,256]{2,1,0:T(8,128)(2,1)S(1)} %get-tuple-element.25), channel_id=1, source_target_pairs={{32,4},{33,5},{34,6},{35,7},{40,12},{41,13},{42,14},{43,15},{48,20... | collective-permute-start | bytes 393224 | tf_op jit(solution)/shard_map/ppermute | solution.py:497
  23.6 0.0 collective-permute-done.2.refs_5_
  23.6 1.4 %collective-permute-done.3.refs_6_ = bf16[4,64,256]{2,1,0:T(8,128)(2,1)S(1)} collective-permute-done((bf16[4,64,256]{2,1,0:T(8,128)(2,1)S(1)}, bf16[4,64,256]{2,1,0:T(8,128)(2,1)S(1)}, u32[]{:S(2)}, u32[]{:S(2)}) %collective-permute-start.3) | collective-permute-done | bytes 131104 | tf_op jit(solution)/shard_map/ppermute | solution.py:497
  25.0 2.7 %collective-permute-done.5.refs_8_ = bf16[4,64,256]{2,1,0:T(8,128)(2,1)S(1)} collective-permute-done((bf16[4,64,256]{2,1,0:T(8,128)(2,1)S(1)}, bf16[4,64,256]{2,1,0:T(8,128)(2,1)S(1)}, u32[]{:S(2)}, u32[]{:S(2)}) %collective-permute-start.5) | collective-permute-done | bytes 131104 | tf_op jit(solution)/shard_map/ppermute | solution.py:497
  27.7 1.0 %copy-done.1 = bf16[8,64,448]{2,1,0:T(8,128)(2,1)S(1)} copy-done((bf16[8,64,448]{2,1,0:T(8,128)(2,1)S(1)}, bf16[8,64,448]{2,1,0:T(8,128)(2,1)}, u32[]{:S(2)}) %copy-start.1) | copy-done | bytes 458776
  28.7 3.4 %products.1 = (f32[64,1280]{1,0:T(8,128)S(1)}, bf16[64,1024]{1,0:T(8,128)(2,1)S(1)}, bf16[64,1024]{1,0:T(8,128)(2,1)S(1)}, bf16[64,1024]{1,0:T(8,128)(2,1)S(1)},...) custom-call(s32[8,7]{1,0:T(8,128)S(1)} %copy-done.2, ...), custom_call_target="tpu_custom_call" | custom-call | flops 900000000 | bytes 2600000 | tf_op jit(solution)/shard_map/products/pallas_call | solution.py:510
  32.2 5.1 %collective-permute-start.6 = (bf16[64,1024]{1,0:T(8,128)(2,1)S(1)}, bf16[64,1024]{1,0:T(8,128)(2,1)S(1)}, u32[]{:S(2)}, u32[]{:S(2)}) collective-permute-start(bf16[64,1024]{1,0:T(8,128)(2,1)S(1)} %get-tuple-element.29), channel_id=1, source_target_pairs={{8,1},{10,3},{12,5},{14,7},{1,8},{64,9},{3,10},{66,11},{5,12},{68,... | collective-permute-start | bytes 393224 | tf_op jit(solution)/shard_map/ppermute | solution.py:497
  37.3 5.6 %collective-permute-start.7 = (bf16[64,1024]{1,0:T(8,128)(2,1)S(1)}, bf16[64,1024]{1,0:T(8,128)(2,1)S(1)}, u32[]{:S(2)}, u32[]{:S(2)}) collective-permute-start(bf16[64,1024]{1,0:T(8,128)(2,1)S(1)} %get-tuple-element.30), channel_id=1, source_target_pairs={{16,2},{17,3},{20,6},{21,7},{24,10},{25,11},{28,14},{29,15},{2,16}... | collective-permute-start | bytes 393224 | tf_op jit(solution)/shard_map/ppermute | solution.py:497
  42.9 0.1 collective-permute-start.8
  43.0 8.0 %collective-permute-start.9 = (bf16[64,1024]{1,0:T(8,128)(2,1)S(1)}, bf16[64,1024]{1,0:T(8,128)(2,1)S(1)}, u32[]{:S(2)}, u32[]{:S(2)}) collective-permute-start(bf16[64,1024]{1,0:T(8,128)(2,1)S(1)} %get-tuple-element.32), channel_id=1, source_target_pairs={{32,4},{33,5},{34,6},{35,7},{40,12},{41,13},{42,14},{43,15},{48,20... | collective-permute-start | bytes 393224 | tf_op jit(solution)/shard_map/ppermute | solution.py:497
  51.1 4.0 %collective-permute-done.9.o2 = bf16[64,1024]{1,0:T(8,128)(2,1)S(1)} collective-permute-done((bf16[64,1024]{1,0:T(8,128)(2,1)S(1)}, bf16[64,1024]{1,0:T(8,128)(2,1)S(1)}, u32[]{:S(2)}, u32[]{:S(2)}) %collective-permute-start.9) | collective-permute-done | bytes 131104 | tf_op jit(solution)/shard_map/ppermute | solution.py:497
  55.1 0.2 gather.1
  55.3 9.4 %all_to_all.5.y_ref = bf16[4,16,4224]{2,1,0:T(8,128)(2,1)S(1)} all-to-all(bf16[4,16,4224]{2,1,0:T(8,128)(2,1)S(1)} %gather.1), channel_id=1, replica_groups=mesh['curve'=64,'owner'=4] {'owner'}, dimensions={0} | all-to-all | bytes 1081344 | tf_op jit(solution)/shard_map/all_to_all | solution.py:531
  64.7 1.5 %finish.1 = bf16[4,16,2112]{2,1,0:T(8,128)(2,1)} custom-call(s32[8,4]{1,0:T(8,128)S(1)} %copy.6.refs_0_.columns, bf16[4,16,4224]{2,1,0:T(8,128)(2,1)S(1)} %all_to_all.5.y_ref), custom_call_target="tpu_custom_call" | custom-call | bytes 900000 | tf_op jit(solution)/shard_map/finish/pallas_call | solution.py:534
  (8 shorter events, 0.0 us)
Async XLA Ops:
  0.8 0.9 %copy-start = (bf16[8,64,256]{2,1,0:T(8,128)(2,1)S(1)}, bf16[8,64,256]{2,1,0:T(8,128)(2,1)}, u32[]{:S(2)}) copy-start(bf16[8,64,256]{2,1,0:T(8,128)(2,1)} %refs_1_.2) | copy-start | bytes 786436
  2.6 14.9 %collective-permute-start = (bf16[4,64,256]{2,1,0:T(8,128)(2,1)S(1)}, bf16[4,64,256]{2,1,0:T(8,128)(2,1)S(1)}, u32[]{:S(2)}, u32[]{:S(2)}) collective-permute-start(bf16[4,64,256]{2,1,0:T(8,128)(2,1)S(1)} %get-tuple-element.20), channel_id=1, source_target_pairs={{1,0},{0,1},{3,2},{2,3},{5,4},{4,5},{7,6},{6,7},{9,8},{8,9},{11,10... | collective-permute-start | bytes 393224 | tf_op jit(solution)/shard_map/ppermute | solution.py:497
  3.9 19.7 %collective-permute-start.1 = (bf16[4,64,256]{2,1,0:T(8,128)(2,1)S(1)}, bf16[4,64,256]{2,1,0:T(8,128)(2,1)S(1)}, u32[]{:S(2)}, u32[]{:S(2)}) collective-permute-start(bf16[4,64,256]{2,1,0:T(8,128)(2,1)S(1)} %get-tuple-element.21), channel_id=1, source_target_pairs={{8,1},{10,3},{12,5},{14,7},{1,8},{64,9},{3,10},{66,11},{5,12},{68,... | collective-permute-start | bytes 393224 | tf_op jit(solution)/shard_map/ppermute | solution.py:497
  7.6 20.1 %copy-start.2 = (s32[8,7]{1,0:T(8,128)S(1)}, s32[8,7]{1,0:T(8,128)}, u32[]{:S(2)}) copy-start(s32[8,7]{1,0:T(8,128)} %refs_0_.2) | copy-start | bytes 676
  7.6 16.0 %collective-permute-start.2 = (bf16[4,64,256]{2,1,0:T(8,128)(2,1)S(1)}, bf16[4,64,256]{2,1,0:T(8,128)(2,1)S(1)}, u32[]{:S(2)}, u32[]{:S(2)}) collective-permute-start(bf16[4,64,256]{2,1,0:T(8,128)(2,1)S(1)} %get-tuple-element.22), channel_id=1, source_target_pairs={{2,0},{3,1},{0,2},{1,3},{6,4},{7,5},{4,6},{5,7},{10,8},{11,9},{8,1... | collective-permute-start | bytes 393224 | tf_op jit(solution)/shard_map/ppermute | solution.py:497
  10.4 14.5 %collective-permute-start.3 = (bf16[4,64,256]{2,1,0:T(8,128)(2,1)S(1)}, bf16[4,64,256]{2,1,0:T(8,128)(2,1)S(1)}, u32[]{:S(2)}, u32[]{:S(2)}) collective-permute-start(bf16[4,64,256]{2,1,0:T(8,128)(2,1)S(1)} %get-tuple-element.23), channel_id=1, source_target_pairs={{16,2},{17,3},{20,6},{21,7},{24,10},{25,11},{28,14},{29,15},{2,16}... | collective-permute-start | bytes 393224 | tf_op jit(solution)/shard_map/ppermute | solution.py:497
  15.6 9.3 %collective-permute-start.4 = (bf16[4,64,256]{2,1,0:T(8,128)(2,1)S(1)}, bf16[4,64,256]{2,1,0:T(8,128)(2,1)S(1)}, u32[]{:S(2)}, u32[]{:S(2)}) collective-permute-start(bf16[4,64,256]{2,1,0:T(8,128)(2,1)S(1)} %get-tuple-element.24), channel_id=1, source_target_pairs={{4,0},{5,1},{6,2},{7,3},{0,4},{1,5},{2,6},{3,7},{12,8},{13,9},{14,... | collective-permute-start | bytes 393224 | tf_op jit(solution)/shard_map/ppermute | solution.py:497
  17.5 10.2 %collective-permute-start.5 = (bf16[4,64,256]{2,1,0:T(8,128)(2,1)S(1)}, bf16[4,64,256]{2,1,0:T(8,128)(2,1)S(1)}, u32[]{:S(2)}, u32[]{:S(2)}) collective-permute-start(bf16[4,64,256]{2,1,0:T(8,128)(2,1)S(1)} %get-tuple-element.25), channel_id=1, source_target_pairs={{32,4},{33,5},{34,6},{35,7},{40,12},{41,13},{42,14},{43,15},{48,20... | collective-permute-start | bytes 393224 | tf_op jit(solution)/shard_map/ppermute | solution.py:497
  27.7 1.0 %copy-start.1 = (bf16[8,64,448]{2,1,0:T(8,128)(2,1)S(1)}, bf16[8,64,448]{2,1,0:T(8,128)(2,1)}, u32[]{:S(2)}) copy-start(bf16[8,64,448]{2,1,0:T(8,128)(2,1)} %refs_1_.3) | copy-start | bytes 1376260
  32.2 18.9 %collective-permute-start.6 = (bf16[64,1024]{1,0:T(8,128)(2,1)S(1)}, bf16[64,1024]{1,0:T(8,128)(2,1)S(1)}, u32[]{:S(2)}, u32[]{:S(2)}) collective-permute-start(bf16[64,1024]{1,0:T(8,128)(2,1)S(1)} %get-tuple-element.29), channel_id=1, source_target_pairs={{8,1},{10,3},{12,5},{14,7},{1,8},{64,9},{3,10},{66,11},{5,12},{68,... | collective-permute-start | bytes 393224 | tf_op jit(solution)/shard_map/ppermute | solution.py:497
  37.3 13.8 %collective-permute-start.7 = (bf16[64,1024]{1,0:T(8,128)(2,1)S(1)}, bf16[64,1024]{1,0:T(8,128)(2,1)S(1)}, u32[]{:S(2)}, u32[]{:S(2)}) collective-permute-start(bf16[64,1024]{1,0:T(8,128)(2,1)S(1)} %get-tuple-element.30), channel_id=1, source_target_pairs={{16,2},{17,3},{20,6},{21,7},{24,10},{25,11},{28,14},{29,15},{2,16}... | collective-permute-start | bytes 393224 | tf_op jit(solution)/shard_map/ppermute | solution.py:497
  42.9 8.1 %collective-permute-start.8 = (bf16[64,1024]{1,0:T(8,128)(2,1)S(1)}, bf16[64,1024]{1,0:T(8,128)(2,1)S(1)}, u32[]{:S(2)}, u32[]{:S(2)}) collective-permute-start(bf16[64,1024]{1,0:T(8,128)(2,1)S(1)} %get-tuple-element.31), channel_id=1, source_target_pairs={{4,0},{5,1},{6,2},{7,3},{0,4},{1,5},{2,6},{3,7},{12,8},{13,9},{14,... | collective-permute-start | bytes 393224 | tf_op jit(solution)/shard_map/ppermute | solution.py:497
  43.0 12.1 %collective-permute-start.9 = (bf16[64,1024]{1,0:T(8,128)(2,1)S(1)}, bf16[64,1024]{1,0:T(8,128)(2,1)S(1)}, u32[]{:S(2)}, u32[]{:S(2)}) collective-permute-start(bf16[64,1024]{1,0:T(8,128)(2,1)S(1)} %get-tuple-element.32), channel_id=1, source_target_pairs={{32,4},{33,5},{34,6},{35,7},{40,12},{41,13},{42,14},{43,15},{48,20... | collective-permute-start | bytes 393224 | tf_op jit(solution)/shard_map/ppermute | solution.py:497

commit v2 on v1

v2 whole, which is shorter than its diff:
```python
import jax
import jax.numpy as jnp
from jax import lax
from jax.experimental import pallas as pl
from jax.experimental.pallas import tpu as pltpu
from jax.sharding import PartitionSpec as P


W = 64
G = 8
FIRST = (3, 2, 1, 0, 5, 4)
SECOND = (3, 2, 1, 0, 5, 4)
THIRD = (2, 1, 3)
AXES = (0, 1, 2)
F32 = jnp.float32
BF16 = jnp.bfloat16
ZERO = (0, 0, 0)


def step(axis, sign):
    return tuple(sign if a == axis else 0 for a in AXES)


def plus(u, v):
    return tuple(a + b for a, b in zip(u, v))


def both(a, sa, b, sb):
    return plus(step(a, sa), step(b, sb))


def axis_mask(axis, bits):
    return sum(1 << b for b in range(bits) if b % 3 == axis)


ROW = [
    (ZERO, step(0, 1)),
    (step(1, 1), step(2, 1)),
    (step(0, -1), step(1, -1)),
    (step(2, -1), both(0, 1, 1, 1)),
    (both(0, 1, 2, 1), both(1, 1, 2, 1)),
]
FACES = [
    (ZERO, step(0, 1)),
    (step(0, -1), step(1, 1)),
    (step(1, -1), step(2, 1)),
    (step(2, -1), None),
]
PAIRS = ((0, 1), (0, 2), (1, 2))


def edge_columns(a, b):
    return [
        (both(a, 1, b, 1), both(a, 1, b, -1)),
        (both(a, -1, b, -1), both(a, -1, b, 1)),
    ]


OWN = FACES + [c for a, b in PAIRS for c in edge_columns(a, b)]


def side_columns(axis, sign):
    out = [(pair, (n, n)) for n, pair in enumerate(FACES)]
    for p, (a, b) in enumerate(PAIRS):
        n = 4 + 2 * p
        first, second = edge_columns(a, b)
        if axis == a:
            out.append((first, (n, n)) if sign > 0 else (second, (n + 1, n + 1)))
        elif axis == b:
            if sign > 0:
                out.append(((first[0], second[1]), (n, n + 1)))
            else:
                out.append(((second[0], first[1]), (n + 1, n)))
        else:
            out.append((first, (n, n)))
            out.append((second, (n + 1, n + 1)))
    return out


def corner(x, y, z):
    return (x, y, z)


FULL = (
    FACES[:3]
    + [(step(2, -1), step(0, 2))]
    + OWN[4:]
    + [
        (corner(1, 1, 1), corner(1, 1, -1)),
        (corner(1, -1, -1), corner(1, -1, 1)),
        (corner(-1, 1, 1), corner(-1, 1, -1)),
        (corner(-1, -1, -1), corner(-1, -1, 1)),
        (step(0, -2), step(1, 2)),
        (step(1, -2), step(2, 2)),
        (step(2, -2), None),
    ]
)


def offset_table():
    table = []
    for x in range(-2, 3):
        for y in range(-2, 3):
            for z in range(-2, 3):
                if sum(max(0, 2 * abs(v) - 1) for v in (x, y, z)) <= 3:
                    table.append((x, y, z))
    return table


def mirrored(slot, axis):
    return tuple(-v if a == axis else v for a, v in enumerate(slot))


def arrived_layout(axis, sign):
    back = []
    for pair, _ in side_columns(axis, sign):
        back.append(
            tuple(
                None if s is None else plus(mirrored(s, axis), step(axis, sign))
                for s in pair
            )
        )
    return back


def places(layout):
    return {
        slot: (n, h)
        for n, pair in enumerate(layout)
        for h, slot in enumerate(pair)
        if slot is not None
    }


class Columns:
    def __init__(self, columns):
        self.columns = columns
        self.turned = {}

    def get(self, n, turn):
        if not turn:
            return self.columns[n]
        if n not in self.turned:
            self.turned[n] = swap(self.columns[n])
        return self.turned[n]


def swap(column):
    if column.dtype == F32:
        return pltpu.roll(column, W, 1)
    return pltpu.roll(column.astype(F32), W, 1).astype(column.dtype)


def compose(source, left_at, right_at, left):
    if left_at is None and right_at is None:
        return None
    a = None if left_at is None else source.get(left_at[0], left_at[1] != 0)
    b = None if right_at is None else source.get(right_at[0], right_at[1] != 1)
    if a is None:
        return jnp.where(left, jnp.zeros_like(b), b)
    if b is None:
        return jnp.where(left, a, jnp.zeros_like(a))
    if left_at[0] == right_at[0] and left_at[1] == 0 and right_at[1] == 1:
        return a
    if left_at[0] == right_at[0] and left_at[1] == 1 and right_at[1] == 0:
        return a
    return jnp.where(left, a, b)


def left_half(rows):
    return lax.broadcasted_iota(jnp.int32, (rows, 128), 1) < W


def split(value):
    return [value[:, n * 128 : (n + 1) * 128] for n in range(value.shape[1] // 128)]


def flag(condition):
    return jnp.where(condition, jnp.int32(1), jnp.int32(0))


def order_kernel(bits, columns, p_ref, own_ref, *side_refs):
    device = device_index()
    turn = 7 - (device & 7)
    left = left_half(W)
    gaps = columns[...] ^ device
    lane = lax.broadcasted_iota(jnp.int32, gaps.shape, 1)
    for member in range(G):
        row = member ^ turn
        raw = p_ref[row].astype(F32)
        first, second = raw[:, :128], raw[:, 128:]
        first_t, second_t = swap(first), swap(second)
        wide = [
            jnp.where(left, first_t, first),
            jnp.where(left, second, second_t),
            jnp.where(left, second_t, second),
        ]
        gap = jnp.sum(jnp.where(lane == row, gaps, 0), axis=1, keepdims=True)
        along = [((gap & axis_mask(axis, bits)) != 0).astype(F32) for axis in AXES]
        stays = (gap == 0).astype(F32)
        a = jnp.where(left, first, 0.0)
        b = jnp.zeros((W, 128), F32)
        for m in (1, 2, 3):
            one = slice(m, m + 1)
            a = a + jnp.where(left, stays[one], along[0][one]) * wide[m - 1]
            b = b + jnp.where(left, along[1][one], along[2][one]) * wide[m - 1]
        a, b = a.astype(BF16), b.astype(BF16)
        own_ref[member, :, :128] = a
        own_ref[member, :, 128:] = b
        for axis in AXES:
            side = side_refs[2 * axis + (member >> axis & 1)]
            rest = half_index(member, axis)
            side[rest, :, :128] = a
            side[rest, :, 128:] = b


def device_index():
    return lax.axis_index("curve") * lax.axis_size("owner") + lax.axis_index("owner")


def half_index(member, axis):
    others = [a for a in AXES if a != axis]
    return (member >> others[0] & 1) + 2 * (member >> others[1] & 1)


BLOCKS = ((0, 0), (0, 1), (1, 0), (1, 1))


def arranged(source, where, left):
    out = []
    for pair in ROW:
        at = [BLOCKS[where[s]] if s in where else None for s in pair]
        column = compose(source, at[0], at[1], left)
        out.append(jnp.zeros((W, 128), BF16) if column is None else column)
    return out


def put(ref, member, position, columns):
    rows = slice(position * W, (position + 1) * W)
    for n, column in enumerate(columns):
        ref[member, rows, n * 128 : (n + 1) * 128] = column


def inner_kernel(bits, columns, a_ref, own_ref, near_ref, far_ref, lt_ref, w_ref, l_ref):
    device = device_index()
    turn = 7 - (device & 7)
    left = left_half(W)
    missing = []
    for axis in AXES:
        mask = axis_mask(axis, bits)
        here = device & mask
        missing.append(flag(here == 0) + flag(here == mask))
    zeros = jnp.zeros((W, 128), BF16)
    self_where = {ZERO: 0}
    for axis in AXES:
        self_where[step(axis, 1)] = axis + 1
    for member in range(G):
        row = member ^ turn
        inner, outer, edge = ([[None] * 7 for _ in AXES] for _ in range(3))
        absent = [missing[axis] * (member >> axis & 1) for axis in AXES]
        rank = [0, absent[0], absent[0] + absent[1]]
        count = jnp.int32(0)
        for k in range(1, 7):
            entry = columns[row, k]
            gap = (entry & 7) ^ row
            near = flag((entry >> 3) == device)
            ends = flag(gap == 0)
            for axis in AXES:
                hit = flag(gap == (1 << axis))
                inner[axis][k] = (hit * near).astype(F32)
                outer[axis][k] = (hit * (1 - near)).astype(F32)
                edge[axis][k] = (
                    absent[axis] * ends * flag(count == rank[axis])
                ).astype(F32)
            count = count + ends
        raw = a_ref[row].astype(F32)
        raw = split(jnp.concatenate([raw, raw[:, 384:]], axis=1))
        turned = [swap(v) for v in raw]
        wide = {}
        for k in range(1, 7):
            v, t = raw[k // 2], turned[k // 2]
            wide[k] = jnp.where(left, t, v) if k % 2 else jnp.where(left, v, t)

        def placed(at_left, at_right):
            total = None
            for k in range(1, 7):
                if at_right is None:
                    term = at_left[k] * wide[k]
                else:
                    term = jnp.where(left, at_left[k], at_right[k]) * wide[k]
                total = term if total is None else total + term
            return total

        first = jnp.where(left, raw[0], placed(inner[0], None))
        last = jnp.where(left, placed(edge[2], None), 0.0)
        factor = [first, placed(inner[1], inner[2]), placed(edge[0], edge[1]), last]
        factor = jnp.concatenate([v.astype(BF16) for v in factor], axis=1)
        far_ref[member, :, :128] = placed(outer[0], outer[1]).astype(BF16)
        far_ref[member, :, 128:] = jnp.where(left, placed(outer[2], None), 0.0).astype(
            BF16
        )
        mine = Columns(split(own_ref[member]))
        self_columns = arranged(mine, self_where, left)
        for position in (0, 4, 5, 6):
            put(w_ref, member, position, self_columns)
        put(w_ref, member, 7, [zeros] * 5)
        for axis in AXES:
            where = {ZERO: 0, step(axis, -1): axis + 1}
            for b in AXES:
                if b != axis:
                    where[step(b, 1)] = b + 1
            other = Columns(split(own_ref[member ^ (1 << axis)]))
            put(w_ref, member, axis + 1, arranged(other, where, left))
        for start, stop in SPANS:
            near_ref[member, :, start:stop] = jnp.dot(
                factor, w_ref[member, :, start:stop], preferred_element_type=F32
            )
        wanted = [(0, 0)]
        for axis in AXES:
            side = member >> axis & 1
            for s in (0, 1):
                wanted.append(BLOCKS[axis + 1] if s == side else None)
        wanted.append(None)
        for n in range(4):
            column = compose(mine, wanted[2 * n], wanted[2 * n + 1], left)
            l_ref[member * W : (member + 1) * W, n * 128 : (n + 1) * 128] = (
                zeros if column is None else column
            )
    lt_ref[...] = l_ref[...].T


SPANS = ((0, 256), (256, 512), (512, 640))


def product_kernel(near_ref, far_ref, lt_ref, e0, o0, e1, o1, e2, o2, sum_ref, *rest):
    outs, (w_ref, b_ref) = rest[:6], rest[6:]
    halo = ((e0, o0), (e1, o1), (e2, o2))
    left = left_half(W)
    row_places = places(ROW)
    zeros = jnp.zeros((W, 128), BF16)
    for member in range(G):
        for axis in AXES:
            where = {step(axis, 1): 0, ZERO: axis + 1}
            for b in AXES:
                if b != axis:
                    where[both(axis, 1, b, 1)] = b + 1
            side = halo[axis][member >> axis & 1]
            there = Columns(split(side[half_index(member, axis)]))
            put(w_ref, member, axis, arranged(there, where, left))
        put(w_ref, member, 3, [zeros] * 5)
        factor = far_ref[member]
        product = []
        for start, stop in SPANS:
            product += split(
                near_ref[member, :, start:stop]
                + jnp.dot(
                    factor, w_ref[member, :, start:stop], preferred_element_type=F32
                )
            )
        source = Columns(product)

        def local(slot):
            if slot is None:
                return None
            return row_places.get(
                tuple(v if member >> a & 1 else -v for a, v in enumerate(slot))
            )

        for n, pair in enumerate(OWN):
            column = compose(source, local(pair[0]), local(pair[1]), left)
            column = zeros if column is None else column.astype(BF16)
            b_ref[member * W : (member + 1) * W, n * 128 : (n + 1) * 128] = column
    held = {}
    for chunk in range(len(OWN) // 2):
        total = jnp.dot(
            lt_ref[: 7 * W],
            b_ref[:, chunk * 256 : (chunk + 1) * 256],
            preferred_element_type=F32,
        )
        for n in (2 * chunk, 2 * chunk + 1):
            at = (n - 2 * chunk) * 128
            held[n] = total[:, at : at + 128]
            sum_ref[:, n * 128 : (n + 1) * 128] = held[n][:W]
        for axis in AXES:
            for s in (0, 1):
                rows = slice((1 + 2 * axis + s) * W, (2 + 2 * axis + s) * W)
                for n, (_, (i, j)) in enumerate(side_columns(axis, 2 * s - 1)):
                    if max(i, j) // 2 != chunk:
                        continue
                    column = (
                        held[i][rows]
                        if i == j
                        else jnp.where(left, held[i][rows], held[j][rows])
                    )
                    outs[2 * axis + s][:, n * 128 : (n + 1) * 128] = column.astype(BF16)


def gather_kernel(sum_ref, e0, o0, e1, o1, e2, o2, *rest):
    out_refs, full_ref = rest[:4], rest[4]
    rows = 16
    device = device_index()
    owner = lax.axis_index("owner")
    left = left_half(rows)
    arrived = ((0, -1, e0), (0, 1, o0), (1, -1, e1), (1, 1, o1), (2, -1, e2), (2, 1, o2))
    for part in range(W // rows):
        span = slice(part * rows, (part + 1) * rows)
        sources = [(Columns(split(sum_ref[span])), places(OWN))]
        for axis, sign, ref in arrived:
            layout = places(arrived_layout(axis, sign))
            sources.append((Columns(split(ref[span].astype(F32))), layout))
        for n, pair in enumerate(FULL):
            total = None
            for source, where in sources:
                column = compose(source, where.get(pair[0]), where.get(pair[1]), left)
                if column is not None:
                    total = column if total is None else total + column
            full_ref[part, :, n * 128 : (n + 1) * 128] = total
    offsets = offset_table()

    def write(signs):
        seen = {
            tuple(v * s for v, s in zip(slot, signs)): at
            for slot, at in places(FULL).items()
        }
        for out_ref, other in zip(out_refs, (0,) + THIRD):
            source = Columns(split(full_ref[owner ^ other]))
            for n in range(17):
                right = seen[offsets[2 * n + 1]] if n < 16 else None
                total = compose(source, seen[offsets[2 * n]], right, left).astype(BF16)
                if n < 16:
                    out_ref[:, n * 128 : (n + 1) * 128] = total
                else:
                    out_ref[:, n * 128 : n * 128 + W] = total[:, :W]

    for low in range(8):
        signs = tuple(2 * (low >> axis & 1) - 1 for axis in AXES)
        pl.when((device & 7) == low)(lambda signs=signs: write(signs))


def finish_kernel(mine, first, second, third, out_ref, sems):
    owner = lax.axis_index("owner")
    copies = []
    for n, (part, other) in enumerate(zip((mine, first, second, third), (0,) + THIRD)):
        copies.append(
            pltpu.make_async_copy(part, out_ref.at[owner ^ other], sems.at[n])
        )
        copies[-1].start()
    for copy in copies:
        copy.wait()


VMEM = pl.BlockSpec(memory_space=pltpu.VMEM)
SMEM = pl.BlockSpec(memory_space=pltpu.SMEM)
ANY = pl.BlockSpec(memory_space=pl.ANY)


def call(kernel, name, outs, n_in, scratch=(), flops=0, size=0, out=None):
    return pl.pallas_call(
        kernel,
        out_shape=[jax.ShapeDtypeStruct(s, d) for s, d in outs],
        in_specs=n_in,
        out_specs=[out or VMEM] * len(outs),
        scratch_shapes=list(scratch),
        compiler_params=pltpu.CompilerParams(vmem_limit_bytes=32 * 1024 * 1024),
        cost_estimate=pl.CostEstimate(
            flops=flops, bytes_accessed=size, transcendentals=0
        ),
        name=name,
    )


def decode(device, bits):
    position = [0, 0, 0]
    for b in range(bits):
        position[b % 3] += (device >> b & 1) << (b // 3)
    return position


def encode(position, bits):
    return sum((position[b % 3] >> (b // 3) & 1) << b for b in range(bits))


def pairs_of(axis, odd, bits):
    extent = 1 << len([b for b in range(bits) if b % 3 == axis])
    out = []
    for device in range(1 << bits):
        position = decode(device, bits)
        sense = 2 * (position[axis] & 1) - 1
        position[axis] += sense if odd else -sense
        if 0 <= position[axis] < extent:
            out.append((encode(position, bits), device))
    return out


def shards(operator_blocks, operator_columns, prolong_blocks, prolong_columns):
    devices = lax.axis_size("curve") * lax.axis_size("owner")
    bits = devices.bit_length() - 1

    def swapped(value, axis, odd):
        return lax.ppermute(value, ("curve", "owner"), pairs_of(axis, odd, bits))

    def exchanged(values, order):
        return [swapped(v, n // 2, bool(n % 2)) for v, n in zip(values, order)]

    def sorted_by(refs, order):
        return [refs[order.index(n)] for n in range(6)]

    def order_step(*refs):
        order_kernel(bits, *refs[:3], *sorted_by(refs[3:], FIRST))

    def product_step(*refs):
        halo, sums, sent = refs[3:9], refs[9], refs[10:16]
        product_kernel(
            *refs[:3],
            *sorted_by(halo, FIRST),
            sums,
            *sorted_by(sent, SECOND),
            *refs[16:],
        )

    def gather_step(*refs):
        gather_kernel(refs[0], *sorted_by(refs[1:7], SECOND), *refs[7:])

    half = ((4, W, 256), BF16)
    ordered = call(
        order_step,
        "order",
        [((G, W, 256), BF16)] + [half] * 6,
        [VMEM, VMEM],
        size=1300000,
    )(prolong_columns.T, prolong_blocks)
    own, sides = ordered[0], ordered[1:]
    halo = exchanged(sides, FIRST)
    near, far, factor = call(
        lambda *refs: inner_kernel(bits, *refs),
        "inner",
        [((G, W, 640), F32), ((G, W, 256), BF16), ((G * W, G * W), BF16)],
        [SMEM, VMEM, VMEM],
        [pltpu.VMEM((G, G * W, 640), BF16), pltpu.VMEM((G * W, G * W), BF16)],
        flops=400000000,
        size=2800000,
    )(operator_columns, operator_blocks, own)
    side = ((W, 1024), BF16)
    sums = call(
        product_step,
        "products",
        [((W, 1280), F32)] + [side] * 6,
        [VMEM] * 9,
        [
            pltpu.VMEM((G, 4 * W, 640), BF16),
            pltpu.VMEM((G * W, 1280), BF16),
        ],
        flops=900000000,
        size=4000000,
    )(near, far, factor, *halo)
    total, sent = sums[0], sums[1:]
    came = exchanged(sent, SECOND)
    part = ((16, 33 * W), BF16)
    mine, *parts = call(
        gather_step,
        "gather",
        [part] * 4,
        [VMEM] * 7,
        [pltpu.VMEM((4, 16, len(FULL) * 128), F32)],
        size=1700000,
    )(total, *came)
    parts = [
        lax.ppermute(v, "owner", [(i, i ^ other) for i in range(4)])
        for v, other in zip(parts, THIRD)
    ]
    return call(
        finish_kernel,
        "finish",
        [((4, 16, 33 * W), BF16)],
        [VMEM] * 4,
        [pltpu.SemaphoreType.DMA((4,))],
        size=500000,
        out=ANY,
    )(mine, *parts)[0]


def solution(mesh):
    return jax.shard_map(
        shards,
        mesh=mesh,
        in_specs=(
            P(("curve", "owner"), None, None),
            P(("curve", "owner"), None),
            P(("curve", "owner"), None, None),
            P(("curve", "owner"), None),
        ),
        out_specs=P("curve", "owner", None),
        check_vma=False,
    )
```

time: 67.3 us -> 60.1 us (0.89)
  the two profiles are of different devices: /device:TPU:25 before, /device:TPU:1 now
where the time goes in v2:
time: 60.1 us; the launch traced here: 59.8 us
  starting transfers between devices  43.8 us (73%)
  waiting for transfers between devices  6.63 us (11%)
  Pallas kernels  5.78 us (10%)
  local copies, waits for them, and re-layouts  3.35 us (6%)
    ppermute x12, starting transfers between devices, swapped(): return lax.ppermute(value, ('curve', 'owner'), pairs_of(axis, odd, bits))  40.5 us
    ppermute x12, waiting for transfers between devices, swapped(): return lax.ppermute(value, ('curve', 'owner'), pairs_of(axis, odd, bits))  3.44 us
    unnamed x8, local copies, waits for them, and re-layouts  3.35 us
    ppermute x3, starting transfers between devices, shards(): lax.ppermute(v, 'owner', [(i, i ^ other) for i in range(4)])  3.34 us
    ppermute x3, waiting for transfers between devices, shards(): lax.ppermute(v, 'owner', [(i, i ^ other) for i in range(4)])  3.18 us
    pallas_call x1, Pallas kernels, shards(): call(lambda *refs: inner_kernel(bits, *refs), 'inner', [((G, W, 640), F32...  2.68 us
    pallas_call x1, Pallas kernels, shards(): call(product_step, 'products', [((W, 1280), F32)] + [side] * 6, [VMEM] *...  1.62 us
  transfers between devices with their start and end apart: 15, of which 3 were waited for; matrix products, arithmetic and copies ran while one was open for 0% of the time, Pallas kernels for 4%

profile of v2, /device:TPU:1, one launch (start us, length us, event | category | flops | bytes accessed | tf_op | source)
XLA Modules:
  0.0 59.8 jit_solution(4493084802668789129)
XLA Ops:
  0.0 0.9 %copy-done = bf16[8,64,256]{2,1,0:T(8,128)(2,1)S(1)} copy-done((bf16[8,64,256]{2,1,0:T(8,128)(2,1)S(1)}, bf16[8,64,256]{2,1,0:T(8,128)(2,1)}, u32[]{:S(2)}) %copy-start) | copy-done | bytes 262168
  1.0 0.7 %copy-done.1 = s32[8,4]{0,1:T(4,128)S(1)} copy-done((s32[8,4]{0,1:T(4,128)S(1)}, s32[8,4]{0,1:T(4,128)}, u32[]{:S(2)}) %copy-start.1) | copy-done | bytes 152
  1.6 0.4 order.1
  2.0 0.7 %collective-permute-start = (bf16[4,64,256]{2,1,0:T(8,128)(2,1)S(1)}, bf16[4,64,256]{2,1,0:T(8,128)(2,1)S(1)}, u32[]{:S(2)}, u32[]{:S(2)}) collective-permute-start(bf16[4,64,256]{2,1,0:T(8,128)(2,1)S(1)} %get-tuple-element.30), channel_id=1, source_target_pairs={{16,2},{17,3},{20,6},{21,7},{24,10},{25,11},{28,14},{29,15},{2,16}... | collective-permute-start | bytes 393224 | tf_op jit(solution)/shard_map/ppermute | solution.py:500
  2.7 7.8 %collective-permute-start.1 = (bf16[4,64,256]{2,1,0:T(8,128)(2,1)S(1)}, bf16[4,64,256]{2,1,0:T(8,128)(2,1)S(1)}, u32[]{:S(2)}, u32[]{:S(2)}) collective-permute-start(bf16[4,64,256]{2,1,0:T(8,128)(2,1)S(1)} %get-tuple-element.31), channel_id=1, source_target_pairs={{2,0},{3,1},{0,2},{1,3},{6,4},{7,5},{4,6},{5,7},{10,8},{11,9},{8,1... | collective-permute-start | bytes 393224 | tf_op jit(solution)/shard_map/ppermute | solution.py:500
  10.5 0.7 %collective-permute-start.2 = (bf16[4,64,256]{2,1,0:T(8,128)(2,1)S(1)}, bf16[4,64,256]{2,1,0:T(8,128)(2,1)S(1)}, u32[]{:S(2)}, u32[]{:S(2)}) collective-permute-start(bf16[4,64,256]{2,1,0:T(8,128)(2,1)S(1)} %get-tuple-element.32), channel_id=1, source_target_pairs={{8,1},{10,3},{12,5},{14,7},{1,8},{64,9},{3,10},{66,11},{5,12},{68,... | collective-permute-start | bytes 393224 | tf_op jit(solution)/shard_map/ppermute | solution.py:500
  11.2 4.1 %collective-permute-start.3 = (bf16[4,64,256]{2,1,0:T(8,128)(2,1)S(1)}, bf16[4,64,256]{2,1,0:T(8,128)(2,1)S(1)}, u32[]{:S(2)}, u32[]{:S(2)}) collective-permute-start(bf16[4,64,256]{2,1,0:T(8,128)(2,1)S(1)} %get-tuple-element.33), channel_id=1, source_target_pairs={{1,0},{0,1},{3,2},{2,3},{5,4},{4,5},{7,6},{6,7},{9,8},{8,9},{11,10... | collective-permute-start | bytes 393224 | tf_op jit(solution)/shard_map/ppermute | solution.py:500
  15.3 7.8 %collective-permute-start.4 = (bf16[4,64,256]{2,1,0:T(8,128)(2,1)S(1)}, bf16[4,64,256]{2,1,0:T(8,128)(2,1)S(1)}, u32[]{:S(2)}, u32[]{:S(2)}) collective-permute-start(bf16[4,64,256]{2,1,0:T(8,128)(2,1)S(1)} %get-tuple-element.34), channel_id=1, source_target_pairs={{32,4},{33,5},{34,6},{35,7},{40,12},{41,13},{42,14},{43,15},{48,20... | collective-permute-start | bytes 393224 | tf_op jit(solution)/shard_map/ppermute | solution.py:500
  23.3 1.0 %copy-done.2 = bf16[8,64,448]{2,1,0:T(8,128)(2,1)S(1)} copy-done((bf16[8,64,448]{2,1,0:T(8,128)(2,1)S(1)}, bf16[8,64,448]{2,1,0:T(8,128)(2,1)}, u32[]{:S(2)}) %copy-start.2) | copy-done | bytes 458776
  24.3 0.7 %copy-done.3 = s32[8,7]{1,0:T(8,128)S(1)} copy-done((s32[8,7]{1,0:T(8,128)S(1)}, s32[8,7]{1,0:T(8,128)}, u32[]{:S(2)}) %copy-start.3) | copy-done | bytes 248
  25.0 2.7 %inner.1 = (f32[8,64,640]{2,1,0:T(8,128)S(1)}, bf16[8,64,256]{2,1,0:T(8,128)(2,1)S(1)}, bf16[512,512]{1,0:T(8,128)(2,1)S(1)}) custom-call(s32[8,7]{1,0:T(8,128)S(1)} %copy-done.3, bf16[8,64,448]{2,1,0:T(8,128)(2,1)S(1)} %copy-done.2, bf16[8,64,256]{2,1,0:T(8,128)(2,1)S(1)} %get-tuple-element.26.refs_2_), custom_call_target="tpu_custom_call" | custom-call | flops 400000000 | bytes 2800000 | tf_op jit(solution)/shard_map/inner/pallas_call | solution.py:534
  27.7 1.6 %products.1 = (f32[64,1280]{1,0:T(8,128)S(1)}, bf16[64,1024]{1,0:T(8,128)(2,1)S(1)}, bf16[64,1024]{1,0:T(8,128)(2,1)S(1)}, bf16[64,1024]{1,0:T(8,128)(2,1)S(1)},...) custom-call(f32[8,64,640]{2,1,0:T(8,128)S(1)} %get-tuple-element.27.refs_0_, ...), custom_call_target="tpu_custom_call" | custom-call | flops 900000000 | bytes 4000000 | tf_op jit(solution)/shard_map/products/pallas_call | solution.py:544
  29.3 0.7 %collective-permute-start.6 = (bf16[64,1024]{1,0:T(8,128)(2,1)S(1)}, bf16[64,1024]{1,0:T(8,128)(2,1)S(1)}, u32[]{:S(2)}, u32[]{:S(2)}) collective-permute-start(bf16[64,1024]{1,0:T(8,128)(2,1)S(1)} %get-tuple-element.37), channel_id=1, source_target_pairs={{16,2},{17,3},{20,6},{21,7},{24,10},{25,11},{28,14},{29,15},{2,16}... | collective-permute-start | bytes 393224 | tf_op jit(solution)/shard_map/ppermute | solution.py:500
  30.0 7.8 %collective-permute-start.7 = (bf16[64,1024]{1,0:T(8,128)(2,1)S(1)}, bf16[64,1024]{1,0:T(8,128)(2,1)S(1)}, u32[]{:S(2)}, u32[]{:S(2)}) collective-permute-start(bf16[64,1024]{1,0:T(8,128)(2,1)S(1)} %get-tuple-element.38), channel_id=1, source_target_pairs={{2,0},{3,1},{0,2},{1,3},{6,4},{7,5},{4,6},{5,7},{10,8},{11,9},{8,1... | collective-permute-start | bytes 393224 | tf_op jit(solution)/shard_map/ppermute | solution.py:500
  37.8 0.7 %collective-permute-start.8 = (bf16[64,1024]{1,0:T(8,128)(2,1)S(1)}, bf16[64,1024]{1,0:T(8,128)(2,1)S(1)}, u32[]{:S(2)}, u32[]{:S(2)}) collective-permute-start(bf16[64,1024]{1,0:T(8,128)(2,1)S(1)} %get-tuple-element.39), channel_id=1, source_target_pairs={{8,1},{10,3},{12,5},{14,7},{1,8},{64,9},{3,10},{66,11},{5,12},{68,... | collective-permute-start | bytes 393224 | tf_op jit(solution)/shard_map/ppermute | solution.py:500
  38.5 3.4 %collective-permute-start.9 = (bf16[64,1024]{1,0:T(8,128)(2,1)S(1)}, bf16[64,1024]{1,0:T(8,128)(2,1)S(1)}, u32[]{:S(2)}, u32[]{:S(2)}) collective-permute-start(bf16[64,1024]{1,0:T(8,128)(2,1)S(1)} %get-tuple-element.40), channel_id=1, source_target_pairs={{1,0},{0,1},{3,2},{2,3},{5,4},{4,5},{7,6},{6,7},{9,8},{8,9},{11,10... | collective-permute-start | bytes 393224 | tf_op jit(solution)/shard_map/ppermute | solution.py:500
  41.9 6.7 %collective-permute-start.10 = (bf16[64,1024]{1,0:T(8,128)(2,1)S(1)}, bf16[64,1024]{1,0:T(8,128)(2,1)S(1)}, u32[]{:S(2)}, u32[]{:S(2)}) collective-permute-start(bf16[64,1024]{1,0:T(8,128)(2,1)S(1)} %get-tuple-element.41), channel_id=1, source_target_pairs={{32,4},{33,5},{34,6},{35,7},{40,12},{41,13},{42,14},{43,15},{48,20... | collective-permute-start | bytes 393224 | tf_op jit(solution)/shard_map/ppermute | solution.py:500
  48.7 3.4 %collective-permute-done.10.refs_5_ = bf16[64,1024]{1,0:T(8,128)(2,1)S(1)} collective-permute-done((bf16[64,1024]{1,0:T(8,128)(2,1)S(1)}, bf16[64,1024]{1,0:T(8,128)(2,1)S(1)}, u32[]{:S(2)}, u32[]{:S(2)}) %collective-permute-start.10) | collective-permute-done | bytes 131104 | tf_op jit(solution)/shard_map/ppermute | solution.py:500
  52.1 0.4 gather.1
  52.5 0.1 collective-permute-start.12
  52.7 3.1 %collective-permute-start.14 = (bf16[16,2112]{1,0:T(8,128)(2,1)S(1)}, bf16[16,2112]{1,0:T(8,128)(2,1)S(1)}, u32[]{:S(2)}, u32[]{:S(2)}) collective-permute-start(bf16[16,2112]{1,0:T(8,128)(2,1)S(1)} %get-tuple-element.46), channel_id=1, source_target_pairs={{0,3},{1,2},{2,1},{3,0},{4,7},{5,6},{6,5},{7,4},{8,11},{9,10},{10,... | collective-permute-start | bytes 202760 | tf_op jit(solution)/shard_map/ppermute | solution.py:568
  55.9 1.5 %collective-permute-done.12.first = bf16[16,2112]{1,0:T(8,128)(2,1)S(1)} collective-permute-done((bf16[16,2112]{1,0:T(8,128)(2,1)S(1)}, bf16[16,2112]{1,0:T(8,128)(2,1)S(1)}, u32[]{:S(2)}, u32[]{:S(2)}) %collective-permute-start.12) | collective-permute-done | bytes 67616 | tf_op jit(solution)/shard_map/ppermute | solution.py:568
  57.3 1.7 %collective-permute-done.14.third = bf16[16,2112]{1,0:T(8,128)(2,1)S(1)} collective-permute-done((bf16[16,2112]{1,0:T(8,128)(2,1)S(1)}, bf16[16,2112]{1,0:T(8,128)(2,1)S(1)}, u32[]{:S(2)}, u32[]{:S(2)}) %collective-permute-start.14) | collective-permute-done | bytes 67616 | tf_op jit(solution)/shard_map/ppermute | solution.py:568
  59.0 0.7 %finish.1 = bf16[4,16,2112]{2,1,0:T(8,128)(2,1)} custom-call(bf16[16,2112]{1,0:T(8,128)(2,1)S(1)} %get-tuple-element.43.mine, bf16[16,2112]{1,0:T(8,128)(2,1)S(1)} %collective-permute-done.12.first, bf16[16,2112]{1,0:T(8,128)(2,1)S(1)} %collective-permute-done.13.second, bf16[16,2112]{1,0:T(8,128)(2,1)S(1)} %collective-permute-done.14.third), custom_call_target="tpu_custom_call" | custom-call | bytes 500000 | tf_op jit(solution)/shard_map/finish/pallas_call | solution.py:571
  (19 shorter events, 0.3 us)
Async XLA Ops:
  0.0 0.9 %copy-start = (bf16[8,64,256]{2,1,0:T(8,128)(2,1)S(1)}, bf16[8,64,256]{2,1,0:T(8,128)(2,1)}, u32[]{:S(2)}) copy-start(bf16[8,64,256]{2,1,0:T(8,128)(2,1)} %refs_1_.2) | copy-start | bytes 786436
  1.0 0.7 %copy-start.1 = (s32[8,4]{0,1:T(4,128)S(1)}, s32[8,4]{0,1:T(4,128)}, u32[]{:S(2)}) copy-start(s32[8,4]{0,1:T(4,128)} %param.7) | copy-start | bytes 388
  2.0 21.1 %collective-permute-start = (bf16[4,64,256]{2,1,0:T(8,128)(2,1)S(1)}, bf16[4,64,256]{2,1,0:T(8,128)(2,1)S(1)}, u32[]{:S(2)}, u32[]{:S(2)}) collective-permute-start(bf16[4,64,256]{2,1,0:T(8,128)(2,1)S(1)} %get-tuple-element.30), channel_id=1, source_target_pairs={{16,2},{17,3},{20,6},{21,7},{24,10},{25,11},{28,14},{29,15},{2,16}... | collective-permute-start | bytes 393224 | tf_op jit(solution)/shard_map/ppermute | solution.py:500
  2.7 25.0 %collective-permute-start.1 = (bf16[4,64,256]{2,1,0:T(8,128)(2,1)S(1)}, bf16[4,64,256]{2,1,0:T(8,128)(2,1)S(1)}, u32[]{:S(2)}, u32[]{:S(2)}) collective-permute-start(bf16[4,64,256]{2,1,0:T(8,128)(2,1)S(1)} %get-tuple-element.31), channel_id=1, source_target_pairs={{2,0},{3,1},{0,2},{1,3},{6,4},{7,5},{4,6},{5,7},{10,8},{11,9},{8,1... | collective-permute-start | bytes 393224 | tf_op jit(solution)/shard_map/ppermute | solution.py:500
  10.5 17.1 %collective-permute-start.2 = (bf16[4,64,256]{2,1,0:T(8,128)(2,1)S(1)}, bf16[4,64,256]{2,1,0:T(8,128)(2,1)S(1)}, u32[]{:S(2)}, u32[]{:S(2)}) collective-permute-start(bf16[4,64,256]{2,1,0:T(8,128)(2,1)S(1)} %get-tuple-element.32), channel_id=1, source_target_pairs={{8,1},{10,3},{12,5},{14,7},{1,8},{64,9},{3,10},{66,11},{5,12},{68,... | collective-permute-start | bytes 393224 | tf_op jit(solution)/shard_map/ppermute | solution.py:500
  11.2 16.5 %collective-permute-start.3 = (bf16[4,64,256]{2,1,0:T(8,128)(2,1)S(1)}, bf16[4,64,256]{2,1,0:T(8,128)(2,1)S(1)}, u32[]{:S(2)}, u32[]{:S(2)}) collective-permute-start(bf16[4,64,256]{2,1,0:T(8,128)(2,1)S(1)} %get-tuple-element.33), channel_id=1, source_target_pairs={{1,0},{0,1},{3,2},{2,3},{5,4},{4,5},{7,6},{6,7},{9,8},{8,9},{11,10... | collective-permute-start | bytes 393224 | tf_op jit(solution)/shard_map/ppermute | solution.py:500
  15.3 12.4 %collective-permute-start.4 = (bf16[4,64,256]{2,1,0:T(8,128)(2,1)S(1)}, bf16[4,64,256]{2,1,0:T(8,128)(2,1)S(1)}, u32[]{:S(2)}, u32[]{:S(2)}) collective-permute-start(bf16[4,64,256]{2,1,0:T(8,128)(2,1)S(1)} %get-tuple-element.34), channel_id=1, source_target_pairs={{32,4},{33,5},{34,6},{35,7},{40,12},{41,13},{42,14},{43,15},{48,20... | collective-permute-start | bytes 393224 | tf_op jit(solution)/shard_map/ppermute | solution.py:500
  23.1 4.6 %collective-permute-start.5 = (bf16[4,64,256]{2,1,0:T(8,128)(2,1)S(1)}, bf16[4,64,256]{2,1,0:T(8,128)(2,1)S(1)}, u32[]{:S(2)}, u32[]{:S(2)}) collective-permute-start(bf16[4,64,256]{2,1,0:T(8,128)(2,1)S(1)} %get-tuple-element.35), channel_id=1, source_target_pairs={{4,0},{5,1},{6,2},{7,3},{0,4},{1,5},{2,6},{3,7},{12,8},{13,9},{14,... | collective-permute-start | bytes 393224 | tf_op jit(solution)/shard_map/ppermute | solution.py:500
  23.2 1.0 %copy-start.2 = (bf16[8,64,448]{2,1,0:T(8,128)(2,1)S(1)}, bf16[8,64,448]{2,1,0:T(8,128)(2,1)}, u32[]{:S(2)}) copy-start(bf16[8,64,448]{2,1,0:T(8,128)(2,1)} %refs_1_.3) | copy-start | bytes 1376260
  24.3 0.7 %copy-start.3 = (s32[8,7]{1,0:T(8,128)S(1)}, s32[8,7]{1,0:T(8,128)}, u32[]{:S(2)}) copy-start(s32[8,7]{1,0:T(8,128)} %refs_0_.1) | copy-start | bytes 676
  29.3 19.2 %collective-permute-start.6 = (bf16[64,1024]{1,0:T(8,128)(2,1)S(1)}, bf16[64,1024]{1,0:T(8,128)(2,1)S(1)}, u32[]{:S(2)}, u32[]{:S(2)}) collective-permute-start(bf16[64,1024]{1,0:T(8,128)(2,1)S(1)} %get-tuple-element.37), channel_id=1, source_target_pairs={{16,2},{17,3},{20,6},{21,7},{24,10},{25,11},{28,14},{29,15},{2,16}... | collective-permute-start | bytes 393224 | tf_op jit(solution)/shard_map/ppermute | solution.py:500
  30.0 18.7 %collective-permute-start.7 = (bf16[64,1024]{1,0:T(8,128)(2,1)S(1)}, bf16[64,1024]{1,0:T(8,128)(2,1)S(1)}, u32[]{:S(2)}, u32[]{:S(2)}) collective-permute-start(bf16[64,1024]{1,0:T(8,128)(2,1)S(1)} %get-tuple-element.38), channel_id=1, source_target_pairs={{2,0},{3,1},{0,2},{1,3},{6,4},{7,5},{4,6},{5,7},{10,8},{11,9},{8,1... | collective-permute-start | bytes 393224 | tf_op jit(solution)/shard_map/ppermute | solution.py:500
  37.8 10.9 %collective-permute-start.8 = (bf16[64,1024]{1,0:T(8,128)(2,1)S(1)}, bf16[64,1024]{1,0:T(8,128)(2,1)S(1)}, u32[]{:S(2)}, u32[]{:S(2)}) collective-permute-start(bf16[64,1024]{1,0:T(8,128)(2,1)S(1)} %get-tuple-element.39), channel_id=1, source_target_pairs={{8,1},{10,3},{12,5},{14,7},{1,8},{64,9},{3,10},{66,11},{5,12},{68,... | collective-permute-start | bytes 393224 | tf_op jit(solution)/shard_map/ppermute | solution.py:500
  38.5 10.2 %collective-permute-start.9 = (bf16[64,1024]{1,0:T(8,128)(2,1)S(1)}, bf16[64,1024]{1,0:T(8,128)(2,1)S(1)}, u32[]{:S(2)}, u32[]{:S(2)}) collective-permute-start(bf16[64,1024]{1,0:T(8,128)(2,1)S(1)} %get-tuple-element.40), channel_id=1, source_target_pairs={{1,0},{0,1},{3,2},{2,3},{5,4},{4,5},{7,6},{6,7},{9,8},{8,9},{11,10... | collective-permute-start | bytes 393224 | tf_op jit(solution)/shard_map/ppermute | solution.py:500
  41.9 10.3 %collective-permute-start.10 = (bf16[64,1024]{1,0:T(8,128)(2,1)S(1)}, bf16[64,1024]{1,0:T(8,128)(2,1)S(1)}, u32[]{:S(2)}, u32[]{:S(2)}) collective-permute-start(bf16[64,1024]{1,0:T(8,128)(2,1)S(1)} %get-tuple-element.41), channel_id=1, source_target_pairs={{32,4},{33,5},{34,6},{35,7},{40,12},{41,13},{42,14},{43,15},{48,20... | collective-permute-start | bytes 393224 | tf_op jit(solution)/shard_map/ppermute | solution.py:500
  48.6 3.6 %collective-permute-start.11 = (bf16[64,1024]{1,0:T(8,128)(2,1)S(1)}, bf16[64,1024]{1,0:T(8,128)(2,1)S(1)}, u32[]{:S(2)}, u32[]{:S(2)}) collective-permute-start(bf16[64,1024]{1,0:T(8,128)(2,1)S(1)} %get-tuple-element.42), channel_id=1, source_target_pairs={{4,0},{5,1},{6,2},{7,3},{0,4},{1,5},{2,6},{3,7},{12,8},{13,9},{14,... | collective-permute-start | bytes 393224 | tf_op jit(solution)/shard_map/ppermute | solution.py:500
  52.5 4.8 %collective-permute-start.12 = (bf16[16,2112]{1,0:T(8,128)(2,1)S(1)}, bf16[16,2112]{1,0:T(8,128)(2,1)S(1)}, u32[]{:S(2)}, u32[]{:S(2)}) collective-permute-start(bf16[16,2112]{1,0:T(8,128)(2,1)S(1)} %get-tuple-element.44), channel_id=1, source_target_pairs={{0,2},{1,3},{2,0},{3,1},{4,6},{5,7},{6,4},{7,5},{8,10},{9,11},{10,... | collective-permute-start | bytes 202760 | tf_op jit(solution)/shard_map/ppermute | solution.py:568
  52.6 4.7 %collective-permute-start.13 = (bf16[16,2112]{1,0:T(8,128)(2,1)S(1)}, bf16[16,2112]{1,0:T(8,128)(2,1)S(1)}, u32[]{:S(2)}, u32[]{:S(2)}) collective-permute-start(bf16[16,2112]{1,0:T(8,128)(2,1)S(1)} %get-tuple-element.45), channel_id=1, source_target_pairs={{0,1},{1,0},{2,3},{3,2},{4,5},{5,4},{6,7},{7,6},{8,9},{9,8},{10,11... | collective-permute-start | bytes 202760 | tf_op jit(solution)/shard_map/ppermute | solution.py:568
  52.7 6.3 %collective-permute-start.14 = (bf16[16,2112]{1,0:T(8,128)(2,1)S(1)}, bf16[16,2112]{1,0:T(8,128)(2,1)S(1)}, u32[]{:S(2)}, u32[]{:S(2)}) collective-permute-start(bf16[16,2112]{1,0:T(8,128)(2,1)S(1)} %get-tuple-element.46), channel_id=1, source_target_pairs={{0,3},{1,2},{2,1},{3,0},{4,7},{5,6},{6,5},{7,4},{8,11},{9,10},{10,... | collective-permute-start | bytes 202760 | tf_op jit(solution)/shard_map/ppermute | solution.py:568

commit v3 on v2

--- a/solution.py
+++ b/solution.py
@@ -8,8 +8,8 @@
 
 W = 64
 G = 8
-FIRST = (3, 2, 1, 0, 5, 4)
-SECOND = (3, 2, 1, 0, 5, 4)
+FIRST = (3, 2, 5, 1, 0, 4)
+SECOND = (3, 2, 5, 1, 0, 4)
 THIRD = (2, 1, 3)
 AXES = (0, 1, 2)
 F32 = jnp.float32

time: 60.1 us -> 57.8 us (0.962)
  the two profiles are of different devices: /device:TPU:1 before, /device:TPU:25 now
where the time goes in v3:
time: 57.8 us; the launch traced here: 57.4 us
  starting transfers between devices  42.2 us (73%)
  waiting for transfers between devices  5.91 us (10%)
  Pallas kernels  5.79 us (10%)
  local copies, waits for them, and re-layouts  3.36 us (6%)
    ppermute x12, starting transfers between devices, swapped(): return lax.ppermute(value, ('curve', 'owner'), pairs_of(axis, odd, bits))  37.8 us
    ppermute x3, starting transfers between devices, shards(): lax.ppermute(v, 'owner', [(i, i ^ other) for i in range(4)])  4.39 us
    ppermute x3, waiting for transfers between devices, shards(): lax.ppermute(v, 'owner', [(i, i ^ other) for i in range(4)])  3.76 us
    unnamed x8, local copies, waits for them, and re-layouts  3.36 us
    pallas_call x1, Pallas kernels, shards(): call(lambda *refs: inner_kernel(bits, *refs), 'inner', [((G, W, 640), F32...  2.67 us
    ppermute x12, waiting for transfers between devices, swapped(): return lax.ppermute(value, ('curve', 'owner'), pairs_of(axis, odd, bits))  2.16 us
    pallas_call x1, Pallas kernels, shards(): call(product_step, 'products', [((W, 1280), F32)] + [side] * 6, [VMEM] *...  1.63 us
  transfers between devices with their start and end apart: 15, of which 5 were waited for; matrix products, arithmetic and copies ran while one was open for 0% of the time, Pallas kernels for 5%

profile of v3, /device:TPU:25, one launch (start us, length us, event | category | flops | bytes accessed | tf_op | source)
XLA Modules:
  0.0 57.4 jit_solution(11844294490740023376)
XLA Ops:
  0.0 0.9 %copy-done = bf16[8,64,256]{2,1,0:T(8,128)(2,1)S(1)} copy-done((bf16[8,64,256]{2,1,0:T(8,128)(2,1)S(1)}, bf16[8,64,256]{2,1,0:T(8,128)(2,1)}, u32[]{:S(2)}) %copy-start) | copy-done | bytes 262168
  1.0 0.7 %copy-done.1 = s32[8,4]{0,1:T(4,128)S(1)} copy-done((s32[8,4]{0,1:T(4,128)S(1)}, s32[8,4]{0,1:T(4,128)}, u32[]{:S(2)}) %copy-start.1) | copy-done | bytes 152
  2.0 8.0 %collective-permute-start = (bf16[4,64,256]{2,1,0:T(8,128)(2,1)S(1)}, bf16[4,64,256]{2,1,0:T(8,128)(2,1)S(1)}, u32[]{:S(2)}, u32[]{:S(2)}) collective-permute-start(bf16[4,64,256]{2,1,0:T(8,128)(2,1)S(1)} %get-tuple-element.30), channel_id=1, source_target_pairs={{16,2},{17,3},{20,6},{21,7},{24,10},{25,11},{28,14},{29,15},{2,16}... | collective-permute-start | bytes 393224 | tf_op jit(solution)/shard_map/ppermute | solution.py:500
  10.2 7.9 %collective-permute-start.2 = (bf16[4,64,256]{2,1,0:T(8,128)(2,1)S(1)}, bf16[4,64,256]{2,1,0:T(8,128)(2,1)S(1)}, u32[]{:S(2)}, u32[]{:S(2)}) collective-permute-start(bf16[4,64,256]{2,1,0:T(8,128)(2,1)S(1)} %get-tuple-element.32), channel_id=1, source_target_pairs={{32,4},{33,5},{34,6},{35,7},{40,12},{41,13},{42,14},{43,15},{48,20... | collective-permute-start | bytes 393224 | tf_op jit(solution)/shard_map/ppermute | solution.py:500
  18.0 3.6 %collective-permute-start.3 = (bf16[4,64,256]{2,1,0:T(8,128)(2,1)S(1)}, bf16[4,64,256]{2,1,0:T(8,128)(2,1)S(1)}, u32[]{:S(2)}, u32[]{:S(2)}) collective-permute-start(bf16[4,64,256]{2,1,0:T(8,128)(2,1)S(1)} %get-tuple-element.33), channel_id=1, source_target_pairs={{8,1},{10,3},{12,5},{14,7},{1,8},{64,9},{3,10},{66,11},{5,12},{68,... | collective-permute-start | bytes 393224 | tf_op jit(solution)/shard_map/ppermute | solution.py:500
  22.0 1.0 %copy-done.2 = bf16[8,64,448]{2,1,0:T(8,128)(2,1)S(1)} copy-done((bf16[8,64,448]{2,1,0:T(8,128)(2,1)S(1)}, bf16[8,64,448]{2,1,0:T(8,128)(2,1)}, u32[]{:S(2)}) %copy-start.2) | copy-done | bytes 458776
  23.0 0.7 %copy-done.3 = s32[8,7]{1,0:T(8,128)S(1)} copy-done((s32[8,7]{1,0:T(8,128)S(1)}, s32[8,7]{1,0:T(8,128)}, u32[]{:S(2)}) %copy-start.3) | copy-done | bytes 248
  23.7 2.7 %inner.1 = (f32[8,64,640]{2,1,0:T(8,128)S(1)}, bf16[8,64,256]{2,1,0:T(8,128)(2,1)S(1)}, bf16[512,512]{1,0:T(8,128)(2,1)S(1)}) custom-call(s32[8,7]{1,0:T(8,128)S(1)} %copy-done.3, bf16[8,64,448]{2,1,0:T(8,128)(2,1)S(1)} %copy-done.2, bf16[8,64,256]{2,1,0:T(8,128)(2,1)S(1)} %get-tuple-element.26.refs_2_), custom_call_target="tpu_custom_call" | custom-call | flops 400000000 | bytes 2800000 | tf_op jit(solution)/shard_map/inner/pallas_call | solution.py:534
  26.4 1.6 %products.1 = (f32[64,1280]{1,0:T(8,128)S(1)}, bf16[64,1024]{1,0:T(8,128)(2,1)S(1)}, bf16[64,1024]{1,0:T(8,128)(2,1)S(1)}, bf16[64,1024]{1,0:T(8,128)(2,1)S(1)},...) custom-call(f32[8,64,640]{2,1,0:T(8,128)S(1)} %get-tuple-element.27.refs_0_, ...), custom_call_target="tpu_custom_call" | custom-call | flops 900000000 | bytes 4000000 | tf_op jit(solution)/shard_map/products/pallas_call | solution.py:544
  28.1 6.0 %collective-permute-start.6 = (bf16[64,1024]{1,0:T(8,128)(2,1)S(1)}, bf16[64,1024]{1,0:T(8,128)(2,1)S(1)}, u32[]{:S(2)}, u32[]{:S(2)}) collective-permute-start(bf16[64,1024]{1,0:T(8,128)(2,1)S(1)} %get-tuple-element.37), channel_id=1, source_target_pairs={{16,2},{17,3},{20,6},{21,7},{24,10},{25,11},{28,14},{29,15},{2,16}... | collective-permute-start | bytes 393224 | tf_op jit(solution)/shard_map/ppermute | solution.py:500
  34.2 4.0 %collective-permute-start.8 = (bf16[64,1024]{1,0:T(8,128)(2,1)S(1)}, bf16[64,1024]{1,0:T(8,128)(2,1)S(1)}, u32[]{:S(2)}, u32[]{:S(2)}) collective-permute-start(bf16[64,1024]{1,0:T(8,128)(2,1)S(1)} %get-tuple-element.39), channel_id=1, source_target_pairs={{32,4},{33,5},{34,6},{35,7},{40,12},{41,13},{42,14},{43,15},{48,20... | collective-permute-start | bytes 393224 | tf_op jit(solution)/shard_map/ppermute | solution.py:500
  38.2 4.1 %collective-permute-start.9 = (bf16[64,1024]{1,0:T(8,128)(2,1)S(1)}, bf16[64,1024]{1,0:T(8,128)(2,1)S(1)}, u32[]{:S(2)}, u32[]{:S(2)}) collective-permute-start(bf16[64,1024]{1,0:T(8,128)(2,1)S(1)} %get-tuple-element.40), channel_id=1, source_target_pairs={{8,1},{10,3},{12,5},{14,7},{1,8},{64,9},{3,10},{66,11},{5,12},{68,... | collective-permute-start | bytes 393224 | tf_op jit(solution)/shard_map/ppermute | solution.py:500
  42.3 3.1 %collective-permute-start.10 = (bf16[64,1024]{1,0:T(8,128)(2,1)S(1)}, bf16[64,1024]{1,0:T(8,128)(2,1)S(1)}, u32[]{:S(2)}, u32[]{:S(2)}) collective-permute-start(bf16[64,1024]{1,0:T(8,128)(2,1)S(1)} %get-tuple-element.41), channel_id=1, source_target_pairs={{1,0},{0,1},{3,2},{2,3},{5,4},{4,5},{7,6},{6,7},{9,8},{8,9},{11,10... | collective-permute-start | bytes 393224 | tf_op jit(solution)/shard_map/ppermute | solution.py:500
  45.4 0.6 %collective-permute-start.11 = (bf16[64,1024]{1,0:T(8,128)(2,1)S(1)}, bf16[64,1024]{1,0:T(8,128)(2,1)S(1)}, u32[]{:S(2)}, u32[]{:S(2)}) collective-permute-start(bf16[64,1024]{1,0:T(8,128)(2,1)S(1)} %get-tuple-element.42), channel_id=1, source_target_pairs={{4,0},{5,1},{6,2},{7,3},{0,4},{1,5},{2,6},{3,7},{12,8},{13,9},{14,... | collective-permute-start | bytes 393224 | tf_op jit(solution)/shard_map/ppermute | solution.py:500
  46.0 0.5 collective-permute-done.9.refs_4_
  46.4 1.7 %collective-permute-done.10.refs_5_ = bf16[64,1024]{1,0:T(8,128)(2,1)S(1)} collective-permute-done((bf16[64,1024]{1,0:T(8,128)(2,1)S(1)}, bf16[64,1024]{1,0:T(8,128)(2,1)S(1)}, u32[]{:S(2)}, u32[]{:S(2)}) %collective-permute-start.10) | collective-permute-done | bytes 131104 | tf_op jit(solution)/shard_map/ppermute | solution.py:500
  48.1 0.4 gather.1
  48.5 2.9 %collective-permute-start.12 = (bf16[16,2112]{1,0:T(8,128)(2,1)S(1)}, bf16[16,2112]{1,0:T(8,128)(2,1)S(1)}, u32[]{:S(2)}, u32[]{:S(2)}) collective-permute-start(bf16[16,2112]{1,0:T(8,128)(2,1)S(1)} %get-tuple-element.44), channel_id=1, source_target_pairs={{0,2},{1,3},{2,0},{3,1},{4,6},{5,7},{6,4},{7,5},{8,10},{9,11},{10,... | collective-permute-start | bytes 202760 | tf_op jit(solution)/shard_map/ppermute | solution.py:568
  51.4 0.9 %collective-permute-start.13 = (bf16[16,2112]{1,0:T(8,128)(2,1)S(1)}, bf16[16,2112]{1,0:T(8,128)(2,1)S(1)}, u32[]{:S(2)}, u32[]{:S(2)}) collective-permute-start(bf16[16,2112]{1,0:T(8,128)(2,1)S(1)} %get-tuple-element.45), channel_id=1, source_target_pairs={{0,1},{1,0},{2,3},{3,2},{4,5},{5,4},{6,7},{7,6},{8,9},{9,8},{10,11... | collective-permute-start | bytes 202760 | tf_op jit(solution)/shard_map/ppermute | solution.py:568
  52.3 0.6 %collective-permute-start.14 = (bf16[16,2112]{1,0:T(8,128)(2,1)S(1)}, bf16[16,2112]{1,0:T(8,128)(2,1)S(1)}, u32[]{:S(2)}, u32[]{:S(2)}) collective-permute-start(bf16[16,2112]{1,0:T(8,128)(2,1)S(1)} %get-tuple-element.46), channel_id=1, source_target_pairs={{0,3},{1,2},{2,1},{3,0},{4,7},{5,6},{6,5},{7,4},{8,11},{9,10},{10,... | collective-permute-start | bytes 202760 | tf_op jit(solution)/shard_map/ppermute | solution.py:568
  52.9 0.8 %collective-permute-done.12.first = bf16[16,2112]{1,0:T(8,128)(2,1)S(1)} collective-permute-done((bf16[16,2112]{1,0:T(8,128)(2,1)S(1)}, bf16[16,2112]{1,0:T(8,128)(2,1)S(1)}, u32[]{:S(2)}, u32[]{:S(2)}) %collective-permute-start.12) | collective-permute-done | bytes 67616 | tf_op jit(solution)/shard_map/ppermute | solution.py:568
  53.7 2.1 %collective-permute-done.13.second = bf16[16,2112]{1,0:T(8,128)(2,1)S(1)} collective-permute-done((bf16[16,2112]{1,0:T(8,128)(2,1)S(1)}, bf16[16,2112]{1,0:T(8,128)(2,1)S(1)}, u32[]{:S(2)}, u32[]{:S(2)}) %collective-permute-start.13) | collective-permute-done | bytes 67616 | tf_op jit(solution)/shard_map/ppermute | solution.py:568
  55.8 0.9 %collective-permute-done.14.third = bf16[16,2112]{1,0:T(8,128)(2,1)S(1)} collective-permute-done((bf16[16,2112]{1,0:T(8,128)(2,1)S(1)}, bf16[16,2112]{1,0:T(8,128)(2,1)S(1)}, u32[]{:S(2)}, u32[]{:S(2)}) %collective-permute-start.14) | collective-permute-done | bytes 67616 | tf_op jit(solution)/shard_map/ppermute | solution.py:568
  56.7 0.7 %finish.1 = bf16[4,16,2112]{2,1,0:T(8,128)(2,1)} custom-call(bf16[16,2112]{1,0:T(8,128)(2,1)S(1)} %get-tuple-element.43.mine, bf16[16,2112]{1,0:T(8,128)(2,1)S(1)} %collective-permute-done.12.first, bf16[16,2112]{1,0:T(8,128)(2,1)S(1)} %collective-permute-done.13.second, bf16[16,2112]{1,0:T(8,128)(2,1)S(1)} %collective-permute-done.14.third), custom_call_target="tpu_custom_call" | custom-call | bytes 500000 | tf_op jit(solution)/shard_map/finish/pallas_call | solution.py:571
  (19 shorter events, 0.9 us)
Async XLA Ops:
  0.0 0.9 %copy-start = (bf16[8,64,256]{2,1,0:T(8,128)(2,1)S(1)}, bf16[8,64,256]{2,1,0:T(8,128)(2,1)}, u32[]{:S(2)}) copy-start(bf16[8,64,256]{2,1,0:T(8,128)(2,1)} %refs_1_.2) | copy-start | bytes 786436
  1.0 0.7 %copy-start.1 = (s32[8,4]{0,1:T(4,128)S(1)}, s32[8,4]{0,1:T(4,128)}, u32[]{:S(2)}) copy-start(s32[8,4]{0,1:T(4,128)} %param.7) | copy-start | bytes 388
  2.0 19.9 %collective-permute-start = (bf16[4,64,256]{2,1,0:T(8,128)(2,1)S(1)}, bf16[4,64,256]{2,1,0:T(8,128)(2,1)S(1)}, u32[]{:S(2)}, u32[]{:S(2)}) collective-permute-start(bf16[4,64,256]{2,1,0:T(8,128)(2,1)S(1)} %get-tuple-element.30), channel_id=1, source_target_pairs={{16,2},{17,3},{20,6},{21,7},{24,10},{25,11},{28,14},{29,15},{2,16}... | collective-permute-start | bytes 393224 | tf_op jit(solution)/shard_map/ppermute | solution.py:500
  10.1 16.3 %collective-permute-start.1 = (bf16[4,64,256]{2,1,0:T(8,128)(2,1)S(1)}, bf16[4,64,256]{2,1,0:T(8,128)(2,1)S(1)}, u32[]{:S(2)}, u32[]{:S(2)}) collective-permute-start(bf16[4,64,256]{2,1,0:T(8,128)(2,1)S(1)} %get-tuple-element.31), channel_id=1, source_target_pairs={{2,0},{3,1},{0,2},{1,3},{6,4},{7,5},{4,6},{5,7},{10,8},{11,9},{8,1... | collective-permute-start | bytes 393224 | tf_op jit(solution)/shard_map/ppermute | solution.py:500
  10.2 16.2 %collective-permute-start.2 = (bf16[4,64,256]{2,1,0:T(8,128)(2,1)S(1)}, bf16[4,64,256]{2,1,0:T(8,128)(2,1)S(1)}, u32[]{:S(2)}, u32[]{:S(2)}) collective-permute-start(bf16[4,64,256]{2,1,0:T(8,128)(2,1)S(1)} %get-tuple-element.32), channel_id=1, source_target_pairs={{32,4},{33,5},{34,6},{35,7},{40,12},{41,13},{42,14},{43,15},{48,20... | collective-permute-start | bytes 393224 | tf_op jit(solution)/shard_map/ppermute | solution.py:500
  18.0 8.4 %collective-permute-start.3 = (bf16[4,64,256]{2,1,0:T(8,128)(2,1)S(1)}, bf16[4,64,256]{2,1,0:T(8,128)(2,1)S(1)}, u32[]{:S(2)}, u32[]{:S(2)}) collective-permute-start(bf16[4,64,256]{2,1,0:T(8,128)(2,1)S(1)} %get-tuple-element.33), channel_id=1, source_target_pairs={{8,1},{10,3},{12,5},{14,7},{1,8},{64,9},{3,10},{66,11},{5,12},{68,... | collective-permute-start | bytes 393224 | tf_op jit(solution)/shard_map/ppermute | solution.py:500
  21.6 4.8 %collective-permute-start.4 = (bf16[4,64,256]{2,1,0:T(8,128)(2,1)S(1)}, bf16[4,64,256]{2,1,0:T(8,128)(2,1)S(1)}, u32[]{:S(2)}, u32[]{:S(2)}) collective-permute-start(bf16[4,64,256]{2,1,0:T(8,128)(2,1)S(1)} %get-tuple-element.34), channel_id=1, source_target_pairs={{1,0},{0,1},{3,2},{2,3},{5,4},{4,5},{7,6},{6,7},{9,8},{8,9},{11,10... | collective-permute-start | bytes 393224 | tf_op jit(solution)/shard_map/ppermute | solution.py:500
  21.9 4.5 %collective-permute-start.5 = (bf16[4,64,256]{2,1,0:T(8,128)(2,1)S(1)}, bf16[4,64,256]{2,1,0:T(8,128)(2,1)S(1)}, u32[]{:S(2)}, u32[]{:S(2)}) collective-permute-start(bf16[4,64,256]{2,1,0:T(8,128)(2,1)S(1)} %get-tuple-element.35), channel_id=1, source_target_pairs={{4,0},{5,1},{6,2},{7,3},{0,4},{1,5},{2,6},{3,7},{12,8},{13,9},{14,... | collective-permute-start | bytes 393224 | tf_op jit(solution)/shard_map/ppermute | solution.py:500
  22.0 1.0 %copy-start.2 = (bf16[8,64,448]{2,1,0:T(8,128)(2,1)S(1)}, bf16[8,64,448]{2,1,0:T(8,128)(2,1)}, u32[]{:S(2)}) copy-start(bf16[8,64,448]{2,1,0:T(8,128)(2,1)} %refs_1_.3) | copy-start | bytes 1376260
  23.0 0.7 %copy-start.3 = (s32[8,7]{1,0:T(8,128)S(1)}, s32[8,7]{1,0:T(8,128)}, u32[]{:S(2)}) copy-start(s32[8,7]{1,0:T(8,128)} %refs_0_.1) | copy-start | bytes 676
  28.1 17.3 %collective-permute-start.6 = (bf16[64,1024]{1,0:T(8,128)(2,1)S(1)}, bf16[64,1024]{1,0:T(8,128)(2,1)S(1)}, u32[]{:S(2)}, u32[]{:S(2)}) collective-permute-start(bf16[64,1024]{1,0:T(8,128)(2,1)S(1)} %get-tuple-element.37), channel_id=1, source_target_pairs={{16,2},{17,3},{20,6},{21,7},{24,10},{25,11},{28,14},{29,15},{2,16}... | collective-permute-start | bytes 393224 | tf_op jit(solution)/shard_map/ppermute | solution.py:500
  34.1 11.9 %collective-permute-start.7 = (bf16[64,1024]{1,0:T(8,128)(2,1)S(1)}, bf16[64,1024]{1,0:T(8,128)(2,1)S(1)}, u32[]{:S(2)}, u32[]{:S(2)}) collective-permute-start(bf16[64,1024]{1,0:T(8,128)(2,1)S(1)} %get-tuple-element.38), channel_id=1, source_target_pairs={{2,0},{3,1},{0,2},{1,3},{6,4},{7,5},{4,6},{5,7},{10,8},{11,9},{8,1... | collective-permute-start | bytes 393224 | tf_op jit(solution)/shard_map/ppermute | solution.py:500
  34.2 11.8 %collective-permute-start.8 = (bf16[64,1024]{1,0:T(8,128)(2,1)S(1)}, bf16[64,1024]{1,0:T(8,128)(2,1)S(1)}, u32[]{:S(2)}, u32[]{:S(2)}) collective-permute-start(bf16[64,1024]{1,0:T(8,128)(2,1)S(1)} %get-tuple-element.39), channel_id=1, source_target_pairs={{32,4},{33,5},{34,6},{35,7},{40,12},{41,13},{42,14},{43,15},{48,20... | collective-permute-start | bytes 393224 | tf_op jit(solution)/shard_map/ppermute | solution.py:500
  38.2 8.3 %collective-permute-start.9 = (bf16[64,1024]{1,0:T(8,128)(2,1)S(1)}, bf16[64,1024]{1,0:T(8,128)(2,1)S(1)}, u32[]{:S(2)}, u32[]{:S(2)}) collective-permute-start(bf16[64,1024]{1,0:T(8,128)(2,1)S(1)} %get-tuple-element.40), channel_id=1, source_target_pairs={{8,1},{10,3},{12,5},{14,7},{1,8},{64,9},{3,10},{66,11},{5,12},{68,... | collective-permute-start | bytes 393224 | tf_op jit(solution)/shard_map/ppermute | solution.py:500
  42.3 5.8 %collective-permute-start.10 = (bf16[64,1024]{1,0:T(8,128)(2,1)S(1)}, bf16[64,1024]{1,0:T(8,128)(2,1)S(1)}, u32[]{:S(2)}, u32[]{:S(2)}) collective-permute-start(bf16[64,1024]{1,0:T(8,128)(2,1)S(1)} %get-tuple-element.41), channel_id=1, source_target_pairs={{1,0},{0,1},{3,2},{2,3},{5,4},{4,5},{7,6},{6,7},{9,8},{8,9},{11,10... | collective-permute-start | bytes 393224 | tf_op jit(solution)/shard_map/ppermute | solution.py:500
  45.4 2.8 %collective-permute-start.11 = (bf16[64,1024]{1,0:T(8,128)(2,1)S(1)}, bf16[64,1024]{1,0:T(8,128)(2,1)S(1)}, u32[]{:S(2)}, u32[]{:S(2)}) collective-permute-start(bf16[64,1024]{1,0:T(8,128)(2,1)S(1)} %get-tuple-element.42), channel_id=1, source_target_pairs={{4,0},{5,1},{6,2},{7,3},{0,4},{1,5},{2,6},{3,7},{12,8},{13,9},{14,... | collective-permute-start | bytes 393224 | tf_op jit(solution)/shard_map/ppermute | solution.py:500
  48.5 5.2 %collective-permute-start.12 = (bf16[16,2112]{1,0:T(8,128)(2,1)S(1)}, bf16[16,2112]{1,0:T(8,128)(2,1)S(1)}, u32[]{:S(2)}, u32[]{:S(2)}) collective-permute-start(bf16[16,2112]{1,0:T(8,128)(2,1)S(1)} %get-tuple-element.44), channel_id=1, source_target_pairs={{0,2},{1,3},{2,0},{3,1},{4,6},{5,7},{6,4},{7,5},{8,10},{9,11},{10,... | collective-permute-start | bytes 202760 | tf_op jit(solution)/shard_map/ppermute | solution.py:568
  51.4 4.3 %collective-permute-start.13 = (bf16[16,2112]{1,0:T(8,128)(2,1)S(1)}, bf16[16,2112]{1,0:T(8,128)(2,1)S(1)}, u32[]{:S(2)}, u32[]{:S(2)}) collective-permute-start(bf16[16,2112]{1,0:T(8,128)(2,1)S(1)} %get-tuple-element.45), channel_id=1, source_target_pairs={{0,1},{1,0},{2,3},{3,2},{4,5},{5,4},{6,7},{7,6},{8,9},{9,8},{10,11... | collective-permute-start | bytes 202760 | tf_op jit(solution)/shard_map/ppermute | solution.py:568
  52.3 4.4 %collective-permute-start.14 = (bf16[16,2112]{1,0:T(8,128)(2,1)S(1)}, bf16[16,2112]{1,0:T(8,128)(2,1)S(1)}, u32[]{:S(2)}, u32[]{:S(2)}) collective-permute-start(bf16[16,2112]{1,0:T(8,128)(2,1)S(1)} %get-tuple-element.46), channel_id=1, source_target_pairs={{0,3},{1,2},{2,1},{3,0},{4,7},{5,6},{6,5},{7,4},{8,11},{9,10},{10,... | collective-permute-start | bytes 202760 | tf_op jit(solution)/shard_map/ppermute | solution.py:568

commit v4 on v3

--- a/solution.py
+++ b/solution.py
@@ -8,7 +8,7 @@
 
 W = 64
 G = 8
-FIRST = (3, 2, 5, 1, 0, 4)
+FIRST = (3, 2, 5, 0, 1, 4)
 SECOND = (3, 2, 5, 1, 0, 4)
 THIRD = (2, 1, 3)
 AXES = (0, 1, 2)
@@ -183,7 +183,7 @@
     device = device_index()
     turn = 7 - (device & 7)
     left = left_half(W)
-    gaps = columns[...] ^ device
+    gaps = columns[:4, :] ^ device
     lane = lax.broadcasted_iota(jnp.int32, gaps.shape, 1)
     for member in range(G):
         row = member ^ turn
@@ -241,38 +241,27 @@
         ref[member, rows, n * 128 : (n + 1) * 128] = column
 
 
-def inner_kernel(bits, columns, a_ref, own_ref, near_ref, far_ref, lt_ref, w_ref, l_ref):
+def inner_kernel(bits, columns, a_ref, own_ref, near_ref, far_ref, lt_ref, w_ref):
     device = device_index()
     turn = 7 - (device & 7)
     left = left_half(W)
-    missing = []
-    for axis in AXES:
-        mask = axis_mask(axis, bits)
-        here = device & mask
-        missing.append(flag(here == 0) + flag(here == mask))
     zeros = jnp.zeros((W, 128), BF16)
     self_where = {ZERO: 0}
     for axis in AXES:
         self_where[step(axis, 1)] = axis + 1
     for member in range(G):
         row = member ^ turn
-        inner, outer, edge = ([[None] * 7 for _ in AXES] for _ in range(3))
-        absent = [missing[axis] * (member >> axis & 1) for axis in AXES]
-        rank = [0, absent[0], absent[0] + absent[1]]
-        count = jnp.int32(0)
+        inner, outer = ([[None] * 7 for _ in AXES] for _ in range(2))
+        stays = [None] * 7
         for k in range(1, 7):
-            entry = columns[row, k]
+            entry = columns[4 + row, k]
             gap = (entry & 7) ^ row
             near = flag((entry >> 3) == device)
-            ends = flag(gap == 0)
+            stays[k] = flag(gap == 0).astype(F32)
             for axis in AXES:
                 hit = flag(gap == (1 << axis))
                 inner[axis][k] = (hit * near).astype(F32)
                 outer[axis][k] = (hit * (1 - near)).astype(F32)
-                edge[axis][k] = (
-                    absent[axis] * ends * flag(count == rank[axis])
-                ).astype(F32)
-            count = count + ends
         raw = a_ref[row].astype(F32)
         raw = split(jnp.concatenate([raw, raw[:, 384:]], axis=1))
         turned = [swap(v) for v in raw]
@@ -281,8 +270,7 @@
             v, t = raw[k // 2], turned[k // 2]
             wide[k] = jnp.where(left, t, v) if k % 2 else jnp.where(left, v, t)
 
-        def placed(at_left, at_right):
-            total = None
+        def placed(total, at_left, at_right):
             for k in range(1, 7):
                 if at_right is None:
                     term = at_left[k] * wide[k]
@@ -291,19 +279,15 @@
                 total = term if total is None else total + term
             return total
 
-        first = jnp.where(left, raw[0], placed(inner[0], None))
-        last = jnp.where(left, placed(edge[2], None), 0.0)
-        factor = [first, placed(inner[1], inner[2]), placed(edge[0], edge[1]), last]
-        factor = jnp.concatenate([v.astype(BF16) for v in factor], axis=1)
-        far_ref[member, :, :128] = placed(outer[0], outer[1]).astype(BF16)
-        far_ref[member, :, 128:] = jnp.where(left, placed(outer[2], None), 0.0).astype(
-            BF16
-        )
+        first = placed(jnp.where(left, raw[0], 0.0), stays, inner[0]).astype(BF16)
+        second = placed(None, inner[1], inner[2]).astype(BF16)
+        factor = jnp.concatenate([first, second], axis=1)
+        far_ref[member, :, :128] = placed(None, outer[0], outer[1]).astype(BF16)
+        far_ref[member, :, 128:] = jnp.where(
+            left, placed(None, outer[2], None), 0.0
+        ).astype(BF16)
         mine = Columns(split(own_ref[member]))
-        self_columns = arranged(mine, self_where, left)
-        for position in (0, 4, 5, 6):
-            put(w_ref, member, position, self_columns)
-        put(w_ref, member, 7, [zeros] * 5)
+        put(w_ref, member, 0, arranged(mine, self_where, left))
         for axis in AXES:
             where = {ZERO: 0, step(axis, -1): axis + 1}
             for b in AXES:
@@ -315,18 +299,21 @@
             near_ref[member, :, start:stop] = jnp.dot(
                 factor, w_ref[member, :, start:stop], preferred_element_type=F32
             )
-        wanted = [(0, 0)]
+    for pair in range(G // 2):
+        rows = jnp.concatenate([own_ref[2 * pair], own_ref[2 * pair + 1]], axis=0).T
+        at = slice(pair * 128, (pair + 1) * 128)
+        lt_ref[:W, at] = rows[:W]
         for axis in AXES:
-            side = member >> axis & 1
+            block = rows[(axis + 1) * W : (axis + 2) * W]
             for s in (0, 1):
-                wanted.append(BLOCKS[axis + 1] if s == side else None)
-        wanted.append(None)
-        for n in range(4):
-            column = compose(mine, wanted[2 * n], wanted[2 * n + 1], left)
-            l_ref[member * W : (member + 1) * W, n * 128 : (n + 1) * 128] = (
-                zeros if column is None else column
-            )
-    lt_ref[...] = l_ref[...].T
+                if axis == 0:
+                    part = (
+                        jnp.where(left, zeros, block) if s else jnp.where(left, block, zeros)
+                    )
+                else:
+                    part = block if (2 * pair >> axis & 1) == s else zeros
+                n = 1 + 2 * axis + s
+                lt_ref[n * W : (n + 1) * W, at] = part
 
 
 SPANS = ((0, 256), (256, 512), (512, 640))
@@ -347,8 +334,7 @@
             side = halo[axis][member >> axis & 1]
             there = Columns(split(side[half_index(member, axis)]))
             put(w_ref, member, axis, arranged(there, where, left))
-        put(w_ref, member, 3, [zeros] * 5)
-        factor = far_ref[member]
+        factor = far_ref[member, :, : 3 * W]
         product = []
         for start, stop in SPANS:
             product += split(
@@ -373,7 +359,7 @@
     held = {}
     for chunk in range(len(OWN) // 2):
         total = jnp.dot(
-            lt_ref[: 7 * W],
+            lt_ref[...],
             b_ref[:, chunk * 256 : (chunk + 1) * 256],
             preferred_element_type=F32,
         )
@@ -521,6 +507,9 @@
     def gather_step(*refs):
         gather_kernel(refs[0], *sorted_by(refs[1:7], SECOND), *refs[7:])
 
+    columns = jnp.concatenate(
+        [prolong_columns.T, jnp.pad(operator_columns, ((0, 0), (0, 1)))], axis=0
+    )
     half = ((4, W, 256), BF16)
     ordered = call(
         order_step,
@@ -528,18 +517,18 @@
         [((G, W, 256), BF16)] + [half] * 6,
         [VMEM, VMEM],
         size=1300000,
-    )(prolong_columns.T, prolong_blocks)
+    )(columns, prolong_blocks)
     own, sides = ordered[0], ordered[1:]
     halo = exchanged(sides, FIRST)
     near, far, factor = call(
         lambda *refs: inner_kernel(bits, *refs),
         "inner",
-        [((G, W, 640), F32), ((G, W, 256), BF16), ((G * W, G * W), BF16)],
+        [((G, W, 640), F32), ((G, W, 256), BF16), ((7 * W, G * W), BF16)],
         [SMEM, VMEM, VMEM],
-        [pltpu.VMEM((G, G * W, 640), BF16), pltpu.VMEM((G * W, G * W), BF16)],
+        [pltpu.VMEM((G, 4 * W, 640), BF16)],
         flops=400000000,
         size=2800000,
-    )(operator_columns, operator_blocks, own)
+    )(columns, operator_blocks, own)
     side = ((W, 1024), BF16)
     sums = call(
         product_step,
@@ -547,7 +536,7 @@
         [((W, 1280), F32)] + [side] * 6,
         [VMEM] * 9,
         [
-            pltpu.VMEM((G, 4 * W, 640), BF16),
+            pltpu.VMEM((G, 3 * W, 640), BF16),
             pltpu.VMEM((G * W, 1280), BF16),
         ],
         flops=900000000,

time: 57.8 us -> 56.8 us (0.983)
  waiting for transfers between devices: 5.91 us -> 7.95 us
  starting transfers between devices: 42.2 us -> 40.3 us
  local copies, waits for them, and re-layouts: 3.36 us -> 1.99 us
  Pallas kernels: 5.79 us -> 5.01 us
  other arithmetic: 0 us -> 0.7 us
    ppermute x12, waiting for transfers between devices: 2.16 us -> 4.38 us  [swapped(): return lax.ppermute(value, ('curve', 'owner'), pairs_of(axis, odd, bits))]
    ppermute x12, starting transfers between devices: 37.8 us -> 35.9 us  [swapped(): return lax.ppermute(value, ('curve', 'owner'), pairs_of(axis, odd, bits))]
    unnamed x8 -> x4, local copies, waits for them, and re-layouts: 3.36 us -> 1.99 us
    concatenate x0 -> x1, other arithmetic: none -> 0.7 us  [shards(): jnp.concatenate([prolong_columns.T, jnp.pad(operator_columns, ((0, 0), (0...]
    pallas_call x1, Pallas kernels: 2.67 us -> 1.99 us  [shards(): call(lambda *refs: inner_kernel(bits, *refs), 'inner', [((G, W, 640), F32...]
  transfers between devices with their start and end apart: 15 -> 15, of which waited for: 5 -> 8; matrix products, arithmetic and copies ran while one was open for 0% -> 0% of each run, Pallas kernels for 5% -> 4%
where the time goes in v4:
time: 56.8 us; the launch traced here: 56.1 us
  starting transfers between devices  40.3 us (71%)
  waiting for transfers between devices  7.95 us (14%)
  Pallas kernels  5.01 us (9%)
  local copies, waits for them, and re-layouts  1.99 us (4%)
  other arithmetic  0.7 us (1%)
    ppermute x12, starting transfers between devices, swapped(): return lax.ppermute(value, ('curve', 'owner'), pairs_of(axis, odd, bits))  35.9 us
    ppermute x3, starting transfers between devices, shards(): lax.ppermute(v, 'owner', [(i, i ^ other) for i in range(4)])  4.39 us
    ppermute x12, waiting for transfers between devices, swapped(): return lax.ppermute(value, ('curve', 'owner'), pairs_of(axis, odd, bits))  4.38 us
    ppermute x3, waiting for transfers between devices, shards(): lax.ppermute(v, 'owner', [(i, i ^ other) for i in range(4)])  3.57 us
    pallas_call x1, Pallas kernels, shards(): call(lambda *refs: inner_kernel(bits, *refs), 'inner', [((G, W, 640), F32...  1.99 us
    unnamed x4, local copies, waits for them, and re-layouts  1.99 us
    pallas_call x1, Pallas kernels, shards(): call(product_step, 'products', [((W, 1280), F32)] + [side] * 6, [VMEM] *...  1.54 us
  transfers between devices with their start and end apart: 15, of which 8 were waited for; matrix products, arithmetic and copies ran while one was open for 0% of the time, Pallas kernels for 4%

profile of v4, /device:TPU:25, one launch (start us, length us, event | category | flops | bytes accessed | tf_op | source)
XLA Modules:
  0.0 56.1 jit_solution(3704321261733246779)
XLA Ops:
  0.0 0.7 %pad_add_fusion.refs_0_ = s32[12,8]{1,0:T(8,128)S(1)} fusion(s32[8,7]{1,0:T(8,128)} %param.5, s32[4,8]{1,0:T(4,128)} %bitcast.1), kind=kLoop, calls=%fused_computation | loop fusion | flops 96 | bytes 736 | tf_op jit(solution)/shard_map/concatenate | solution.py:510
  0.7 0.9 %copy-done = bf16[8,64,256]{2,1,0:T(8,128)(2,1)S(1)} copy-done((bf16[8,64,256]{2,1,0:T(8,128)(2,1)S(1)}, bf16[8,64,256]{2,1,0:T(8,128)(2,1)}, u32[]{:S(2)}) %copy-start) | copy-done | bytes 262168
  1.7 0.4 order.1
  2.0 8.0 %collective-permute-start = (bf16[4,64,256]{2,1,0:T(8,128)(2,1)S(1)}, bf16[4,64,256]{2,1,0:T(8,128)(2,1)S(1)}, u32[]{:S(2)}, u32[]{:S(2)}) collective-permute-start(bf16[4,64,256]{2,1,0:T(8,128)(2,1)S(1)} %get-tuple-element.30), channel_id=1, source_target_pairs={{16,2},{17,3},{20,6},{21,7},{24,10},{25,11},{28,14},{29,15},{2,16}... | collective-permute-start | bytes 393224 | tf_op jit(solution)/shard_map/ppermute | solution.py:486
  10.2 7.9 %collective-permute-start.2 = (bf16[4,64,256]{2,1,0:T(8,128)(2,1)S(1)}, bf16[4,64,256]{2,1,0:T(8,128)(2,1)S(1)}, u32[]{:S(2)}, u32[]{:S(2)}) collective-permute-start(bf16[4,64,256]{2,1,0:T(8,128)(2,1)S(1)} %get-tuple-element.32), channel_id=1, source_target_pairs={{32,4},{33,5},{34,6},{35,7},{40,12},{41,13},{42,14},{43,15},{48,20... | collective-permute-start | bytes 393224 | tf_op jit(solution)/shard_map/ppermute | solution.py:486
  18.0 1.1 %collective-permute-start.3 = (bf16[4,64,256]{2,1,0:T(8,128)(2,1)S(1)}, bf16[4,64,256]{2,1,0:T(8,128)(2,1)S(1)}, u32[]{:S(2)}, u32[]{:S(2)}) collective-permute-start(bf16[4,64,256]{2,1,0:T(8,128)(2,1)S(1)} %get-tuple-element.33), channel_id=1, source_target_pairs={{1,0},{0,1},{3,2},{2,3},{5,4},{4,5},{7,6},{6,7},{9,8},{8,9},{11,10... | collective-permute-start | bytes 393224 | tf_op jit(solution)/shard_map/ppermute | solution.py:486
  19.2 2.8 %collective-permute-start.4 = (bf16[4,64,256]{2,1,0:T(8,128)(2,1)S(1)}, bf16[4,64,256]{2,1,0:T(8,128)(2,1)S(1)}, u32[]{:S(2)}, u32[]{:S(2)}) collective-permute-start(bf16[4,64,256]{2,1,0:T(8,128)(2,1)S(1)} %get-tuple-element.34), channel_id=1, source_target_pairs={{8,1},{10,3},{12,5},{14,7},{1,8},{64,9},{3,10},{66,11},{5,12},{68,... | collective-permute-start | bytes 393224 | tf_op jit(solution)/shard_map/ppermute | solution.py:486
  22.1 1.0 %copy-done.1 = bf16[8,64,448]{2,1,0:T(8,128)(2,1)S(1)} copy-done((bf16[8,64,448]{2,1,0:T(8,128)(2,1)S(1)}, bf16[8,64,448]{2,1,0:T(8,128)(2,1)}, u32[]{:S(2)}) %copy-start.1) | copy-done | bytes 458776
  23.1 2.0 %inner.1 = (f32[8,64,640]{2,1,0:T(8,128)S(1)}, bf16[8,64,256]{2,1,0:T(8,128)(2,1)S(1)}, bf16[448,512]{1,0:T(8,128)(2,1)S(1)}) custom-call(s32[12,8]{1,0:T(8,128)S(1)} %pad_add_fusion.refs_0_, bf16[8,64,448]{2,1,0:T(8,128)(2,1)S(1)} %copy-done.1, bf16[8,64,256]{2,1,0:T(8,128)(2,1)S(1)} %get-tuple-element.26.refs_2_), custom_call_target="tpu_custom_call" | custom-call | flops 400000000 | bytes 2800000 | tf_op jit(solution)/shard_map/inner/pallas_call | solution.py:523
  25.1 1.5 %collective-permute-done.4.refs_7_ = bf16[4,64,256]{2,1,0:T(8,128)(2,1)S(1)} collective-permute-done((bf16[4,64,256]{2,1,0:T(8,128)(2,1)S(1)}, bf16[4,64,256]{2,1,0:T(8,128)(2,1)S(1)}, u32[]{:S(2)}, u32[]{:S(2)}) %collective-permute-start.4) | collective-permute-done | bytes 131104 | tf_op jit(solution)/shard_map/ppermute | solution.py:486
  26.7 1.5 %products.1 = (f32[64,1280]{1,0:T(8,128)S(1)}, bf16[64,1024]{1,0:T(8,128)(2,1)S(1)}, bf16[64,1024]{1,0:T(8,128)(2,1)S(1)}, bf16[64,1024]{1,0:T(8,128)(2,1)S(1)},...) custom-call(f32[8,64,640]{2,1,0:T(8,128)S(1)} %get-tuple-element.27.refs_0_, ...), custom_call_target="tpu_custom_call" | custom-call | flops 900000000 | bytes 4000000 | tf_op jit(solution)/shard_map/products/pallas_call | solution.py:533
  28.2 5.9 %collective-permute-start.6 = (bf16[64,1024]{1,0:T(8,128)(2,1)S(1)}, bf16[64,1024]{1,0:T(8,128)(2,1)S(1)}, u32[]{:S(2)}, u32[]{:S(2)}) collective-permute-start(bf16[64,1024]{1,0:T(8,128)(2,1)S(1)} %get-tuple-element.37), channel_id=1, source_target_pairs={{16,2},{17,3},{20,6},{21,7},{24,10},{25,11},{28,14},{29,15},{2,16}... | collective-permute-start | bytes 393224 | tf_op jit(solution)/shard_map/ppermute | solution.py:486
  34.2 3.6 %collective-permute-start.8 = (bf16[64,1024]{1,0:T(8,128)(2,1)S(1)}, bf16[64,1024]{1,0:T(8,128)(2,1)S(1)}, u32[]{:S(2)}, u32[]{:S(2)}) collective-permute-start(bf16[64,1024]{1,0:T(8,128)(2,1)S(1)} %get-tuple-element.39), channel_id=1, source_target_pairs={{32,4},{33,5},{34,6},{35,7},{40,12},{41,13},{42,14},{43,15},{48,20... | collective-permute-start | bytes 393224 | tf_op jit(solution)/shard_map/ppermute | solution.py:486
  37.9 4.2 %collective-permute-start.9 = (bf16[64,1024]{1,0:T(8,128)(2,1)S(1)}, bf16[64,1024]{1,0:T(8,128)(2,1)S(1)}, u32[]{:S(2)}, u32[]{:S(2)}) collective-permute-start(bf16[64,1024]{1,0:T(8,128)(2,1)S(1)} %get-tuple-element.40), channel_id=1, source_target_pairs={{8,1},{10,3},{12,5},{14,7},{1,8},{64,9},{3,10},{66,11},{5,12},{68,... | collective-permute-start | bytes 393224 | tf_op jit(solution)/shard_map/ppermute | solution.py:486
  42.1 1.8 %collective-permute-start.10 = (bf16[64,1024]{1,0:T(8,128)(2,1)S(1)}, bf16[64,1024]{1,0:T(8,128)(2,1)S(1)}, u32[]{:S(2)}, u32[]{:S(2)}) collective-permute-start(bf16[64,1024]{1,0:T(8,128)(2,1)S(1)} %get-tuple-element.41), channel_id=1, source_target_pairs={{1,0},{0,1},{3,2},{2,3},{5,4},{4,5},{7,6},{6,7},{9,8},{8,9},{11,10... | collective-permute-start | bytes 393224 | tf_op jit(solution)/shard_map/ppermute | solution.py:486
  44.5 1.9 %collective-permute-done.9.refs_4_ = bf16[64,1024]{1,0:T(8,128)(2,1)S(1)} collective-permute-done((bf16[64,1024]{1,0:T(8,128)(2,1)S(1)}, bf16[64,1024]{1,0:T(8,128)(2,1)S(1)}, u32[]{:S(2)}, u32[]{:S(2)}) %collective-permute-start.9) | collective-permute-done | bytes 131104 | tf_op jit(solution)/shard_map/ppermute | solution.py:486
  46.4 0.6 %collective-permute-done.10.refs_5_ = bf16[64,1024]{1,0:T(8,128)(2,1)S(1)} collective-permute-done((bf16[64,1024]{1,0:T(8,128)(2,1)S(1)}, bf16[64,1024]{1,0:T(8,128)(2,1)S(1)}, u32[]{:S(2)}, u32[]{:S(2)}) %collective-permute-start.10) | collective-permute-done | bytes 131104 | tf_op jit(solution)/shard_map/ppermute | solution.py:486
  47.0 0.4 gather.1
  47.4 2.7 %collective-permute-start.12 = (bf16[16,2112]{1,0:T(8,128)(2,1)S(1)}, bf16[16,2112]{1,0:T(8,128)(2,1)S(1)}, u32[]{:S(2)}, u32[]{:S(2)}) collective-permute-start(bf16[16,2112]{1,0:T(8,128)(2,1)S(1)} %get-tuple-element.44), channel_id=1, source_target_pairs={{0,2},{1,3},{2,0},{3,1},{4,6},{5,7},{6,4},{7,5},{8,10},{9,11},{10,... | collective-permute-start | bytes 202760 | tf_op jit(solution)/shard_map/ppermute | solution.py:557
  50.1 0.9 %collective-permute-start.13 = (bf16[16,2112]{1,0:T(8,128)(2,1)S(1)}, bf16[16,2112]{1,0:T(8,128)(2,1)S(1)}, u32[]{:S(2)}, u32[]{:S(2)}) collective-permute-start(bf16[16,2112]{1,0:T(8,128)(2,1)S(1)} %get-tuple-element.45), channel_id=1, source_target_pairs={{0,1},{1,0},{2,3},{3,2},{4,5},{5,4},{6,7},{7,6},{8,9},{9,8},{10,11... | collective-permute-start | bytes 202760 | tf_op jit(solution)/shard_map/ppermute | solution.py:557
  51.0 0.8 %collective-permute-start.14 = (bf16[16,2112]{1,0:T(8,128)(2,1)S(1)}, bf16[16,2112]{1,0:T(8,128)(2,1)S(1)}, u32[]{:S(2)}, u32[]{:S(2)}) collective-permute-start(bf16[16,2112]{1,0:T(8,128)(2,1)S(1)} %get-tuple-element.46), channel_id=1, source_target_pairs={{0,3},{1,2},{2,1},{3,0},{4,7},{5,6},{6,5},{7,4},{8,11},{9,10},{10,... | collective-permute-start | bytes 202760 | tf_op jit(solution)/shard_map/ppermute | solution.py:557
  52.1 2.3 %collective-permute-done.13.second = bf16[16,2112]{1,0:T(8,128)(2,1)S(1)} collective-permute-done((bf16[16,2112]{1,0:T(8,128)(2,1)S(1)}, bf16[16,2112]{1,0:T(8,128)(2,1)S(1)}, u32[]{:S(2)}, u32[]{:S(2)}) %collective-permute-start.13) | collective-permute-done | bytes 67616 | tf_op jit(solution)/shard_map/ppermute | solution.py:557
  54.5 0.9 %collective-permute-done.14.third = bf16[16,2112]{1,0:T(8,128)(2,1)S(1)} collective-permute-done((bf16[16,2112]{1,0:T(8,128)(2,1)S(1)}, bf16[16,2112]{1,0:T(8,128)(2,1)S(1)}, u32[]{:S(2)}, u32[]{:S(2)}) %collective-permute-start.14) | collective-permute-done | bytes 67616 | tf_op jit(solution)/shard_map/ppermute | solution.py:557
  55.4 0.7 %finish.1 = bf16[4,16,2112]{2,1,0:T(8,128)(2,1)} custom-call(bf16[16,2112]{1,0:T(8,128)(2,1)S(1)} %get-tuple-element.43.mine, bf16[16,2112]{1,0:T(8,128)(2,1)S(1)} %collective-permute-done.12.first, bf16[16,2112]{1,0:T(8,128)(2,1)S(1)} %collective-permute-done.13.second, bf16[16,2112]{1,0:T(8,128)(2,1)S(1)} %collective-permute-done.14.third), custom_call_target="tpu_custom_call" | custom-call | bytes 500000 | tf_op jit(solution)/shard_map/finish/pallas_call | solution.py:560
  (16 shorter events, 1.3 us)
Async XLA Ops:
  0.7 0.9 %copy-start = (bf16[8,64,256]{2,1,0:T(8,128)(2,1)S(1)}, bf16[8,64,256]{2,1,0:T(8,128)(2,1)}, u32[]{:S(2)}) copy-start(bf16[8,64,256]{2,1,0:T(8,128)(2,1)} %refs_1_.2) | copy-start | bytes 786436
  2.0 19.9 %collective-permute-start = (bf16[4,64,256]{2,1,0:T(8,128)(2,1)S(1)}, bf16[4,64,256]{2,1,0:T(8,128)(2,1)S(1)}, u32[]{:S(2)}, u32[]{:S(2)}) collective-permute-start(bf16[4,64,256]{2,1,0:T(8,128)(2,1)S(1)} %get-tuple-element.30), channel_id=1, source_target_pairs={{16,2},{17,3},{20,6},{21,7},{24,10},{25,11},{28,14},{29,15},{2,16}... | collective-permute-start | bytes 393224 | tf_op jit(solution)/shard_map/ppermute | solution.py:486
  10.1 15.0 %collective-permute-start.1 = (bf16[4,64,256]{2,1,0:T(8,128)(2,1)S(1)}, bf16[4,64,256]{2,1,0:T(8,128)(2,1)S(1)}, u32[]{:S(2)}, u32[]{:S(2)}) collective-permute-start(bf16[4,64,256]{2,1,0:T(8,128)(2,1)S(1)} %get-tuple-element.31), channel_id=1, source_target_pairs={{2,0},{3,1},{0,2},{1,3},{6,4},{7,5},{4,6},{5,7},{10,8},{11,9},{8,1... | collective-permute-start | bytes 393224 | tf_op jit(solution)/shard_map/ppermute | solution.py:486
  10.2 14.9 %collective-permute-start.2 = (bf16[4,64,256]{2,1,0:T(8,128)(2,1)S(1)}, bf16[4,64,256]{2,1,0:T(8,128)(2,1)S(1)}, u32[]{:S(2)}, u32[]{:S(2)}) collective-permute-start(bf16[4,64,256]{2,1,0:T(8,128)(2,1)S(1)} %get-tuple-element.32), channel_id=1, source_target_pairs={{32,4},{33,5},{34,6},{35,7},{40,12},{41,13},{42,14},{43,15},{48,20... | collective-permute-start | bytes 393224 | tf_op jit(solution)/shard_map/ppermute | solution.py:486
  18.0 7.1 %collective-permute-start.3 = (bf16[4,64,256]{2,1,0:T(8,128)(2,1)S(1)}, bf16[4,64,256]{2,1,0:T(8,128)(2,1)S(1)}, u32[]{:S(2)}, u32[]{:S(2)}) collective-permute-start(bf16[4,64,256]{2,1,0:T(8,128)(2,1)S(1)} %get-tuple-element.33), channel_id=1, source_target_pairs={{1,0},{0,1},{3,2},{2,3},{5,4},{4,5},{7,6},{6,7},{9,8},{8,9},{11,10... | collective-permute-start | bytes 393224 | tf_op jit(solution)/shard_map/ppermute | solution.py:486
  19.2 7.5 %collective-permute-start.4 = (bf16[4,64,256]{2,1,0:T(8,128)(2,1)S(1)}, bf16[4,64,256]{2,1,0:T(8,128)(2,1)S(1)}, u32[]{:S(2)}, u32[]{:S(2)}) collective-permute-start(bf16[4,64,256]{2,1,0:T(8,128)(2,1)S(1)} %get-tuple-element.34), channel_id=1, source_target_pairs={{8,1},{10,3},{12,5},{14,7},{1,8},{64,9},{3,10},{66,11},{5,12},{68,... | collective-permute-start | bytes 393224 | tf_op jit(solution)/shard_map/ppermute | solution.py:486
  22.0 4.7 %collective-permute-start.5 = (bf16[4,64,256]{2,1,0:T(8,128)(2,1)S(1)}, bf16[4,64,256]{2,1,0:T(8,128)(2,1)S(1)}, u32[]{:S(2)}, u32[]{:S(2)}) collective-permute-start(bf16[4,64,256]{2,1,0:T(8,128)(2,1)S(1)} %get-tuple-element.35), channel_id=1, source_target_pairs={{4,0},{5,1},{6,2},{7,3},{0,4},{1,5},{2,6},{3,7},{12,8},{13,9},{14,... | collective-permute-start | bytes 393224 | tf_op jit(solution)/shard_map/ppermute | solution.py:486
  22.1 1.0 %copy-start.1 = (bf16[8,64,448]{2,1,0:T(8,128)(2,1)S(1)}, bf16[8,64,448]{2,1,0:T(8,128)(2,1)}, u32[]{:S(2)}) copy-start(bf16[8,64,448]{2,1,0:T(8,128)(2,1)} %refs_1_.3) | copy-start | bytes 1376260
  28.2 15.9 %collective-permute-start.6 = (bf16[64,1024]{1,0:T(8,128)(2,1)S(1)}, bf16[64,1024]{1,0:T(8,128)(2,1)S(1)}, u32[]{:S(2)}, u32[]{:S(2)}) collective-permute-start(bf16[64,1024]{1,0:T(8,128)(2,1)S(1)} %get-tuple-element.37), channel_id=1, source_target_pairs={{16,2},{17,3},{20,6},{21,7},{24,10},{25,11},{28,14},{29,15},{2,16}... | collective-permute-start | bytes 393224 | tf_op jit(solution)/shard_map/ppermute | solution.py:486
  34.1 10.3 %collective-permute-start.7 = (bf16[64,1024]{1,0:T(8,128)(2,1)S(1)}, bf16[64,1024]{1,0:T(8,128)(2,1)S(1)}, u32[]{:S(2)}, u32[]{:S(2)}) collective-permute-start(bf16[64,1024]{1,0:T(8,128)(2,1)S(1)} %get-tuple-element.38), channel_id=1, source_target_pairs={{2,0},{3,1},{0,2},{1,3},{6,4},{7,5},{4,6},{5,7},{10,8},{11,9},{8,1... | collective-permute-start | bytes 393224 | tf_op jit(solution)/shard_map/ppermute | solution.py:486
  34.2 10.3 %collective-permute-start.8 = (bf16[64,1024]{1,0:T(8,128)(2,1)S(1)}, bf16[64,1024]{1,0:T(8,128)(2,1)S(1)}, u32[]{:S(2)}, u32[]{:S(2)}) collective-permute-start(bf16[64,1024]{1,0:T(8,128)(2,1)S(1)} %get-tuple-element.39), channel_id=1, source_target_pairs={{32,4},{33,5},{34,6},{35,7},{40,12},{41,13},{42,14},{43,15},{48,20... | collective-permute-start | bytes 393224 | tf_op jit(solution)/shard_map/ppermute | solution.py:486
  37.9 8.6 %collective-permute-start.9 = (bf16[64,1024]{1,0:T(8,128)(2,1)S(1)}, bf16[64,1024]{1,0:T(8,128)(2,1)S(1)}, u32[]{:S(2)}, u32[]{:S(2)}) collective-permute-start(bf16[64,1024]{1,0:T(8,128)(2,1)S(1)} %get-tuple-element.40), channel_id=1, source_target_pairs={{8,1},{10,3},{12,5},{14,7},{1,8},{64,9},{3,10},{66,11},{5,12},{68,... | collective-permute-start | bytes 393224 | tf_op jit(solution)/shard_map/ppermute | solution.py:486
  42.1 4.9 %collective-permute-start.10 = (bf16[64,1024]{1,0:T(8,128)(2,1)S(1)}, bf16[64,1024]{1,0:T(8,128)(2,1)S(1)}, u32[]{:S(2)}, u32[]{:S(2)}) collective-permute-start(bf16[64,1024]{1,0:T(8,128)(2,1)S(1)} %get-tuple-element.41), channel_id=1, source_target_pairs={{1,0},{0,1},{3,2},{2,3},{5,4},{4,5},{7,6},{6,7},{9,8},{8,9},{11,10... | collective-permute-start | bytes 393224 | tf_op jit(solution)/shard_map/ppermute | solution.py:486
  44.1 2.9 %collective-permute-start.11 = (bf16[64,1024]{1,0:T(8,128)(2,1)S(1)}, bf16[64,1024]{1,0:T(8,128)(2,1)S(1)}, u32[]{:S(2)}, u32[]{:S(2)}) collective-permute-start(bf16[64,1024]{1,0:T(8,128)(2,1)S(1)} %get-tuple-element.42), channel_id=1, source_target_pairs={{4,0},{5,1},{6,2},{7,3},{0,4},{1,5},{2,6},{3,7},{12,8},{13,9},{14,... | collective-permute-start | bytes 393224 | tf_op jit(solution)/shard_map/ppermute | solution.py:486
  47.4 4.8 %collective-permute-start.12 = (bf16[16,2112]{1,0:T(8,128)(2,1)S(1)}, bf16[16,2112]{1,0:T(8,128)(2,1)S(1)}, u32[]{:S(2)}, u32[]{:S(2)}) collective-permute-start(bf16[16,2112]{1,0:T(8,128)(2,1)S(1)} %get-tuple-element.44), channel_id=1, source_target_pairs={{0,2},{1,3},{2,0},{3,1},{4,6},{5,7},{6,4},{7,5},{8,10},{9,11},{10,... | collective-permute-start | bytes 202760 | tf_op jit(solution)/shard_map/ppermute | solution.py:557
  50.1 4.3 %collective-permute-start.13 = (bf16[16,2112]{1,0:T(8,128)(2,1)S(1)}, bf16[16,2112]{1,0:T(8,128)(2,1)S(1)}, u32[]{:S(2)}, u32[]{:S(2)}) collective-permute-start(bf16[16,2112]{1,0:T(8,128)(2,1)S(1)} %get-tuple-element.45), channel_id=1, source_target_pairs={{0,1},{1,0},{2,3},{3,2},{4,5},{5,4},{6,7},{7,6},{8,9},{9,8},{10,11... | collective-permute-start | bytes 202760 | tf_op jit(solution)/shard_map/ppermute | solution.py:557
  51.0 4.4 %collective-permute-start.14 = (bf16[16,2112]{1,0:T(8,128)(2,1)S(1)}, bf16[16,2112]{1,0:T(8,128)(2,1)S(1)}, u32[]{:S(2)}, u32[]{:S(2)}) collective-permute-start(bf16[16,2112]{1,0:T(8,128)(2,1)S(1)} %get-tuple-element.46), channel_id=1, source_target_pairs={{0,3},{1,2},{2,1},{3,0},{4,7},{5,6},{6,5},{7,4},{8,11},{9,10},{10,... | collective-permute-start | bytes 202760 | tf_op jit(solution)/shard_map/ppermute | solution.py:557

commit v5 on v4

--- a/solution.py
+++ b/solution.py
@@ -8,7 +8,7 @@
 
 W = 64
 G = 8
-FIRST = (3, 2, 5, 0, 1, 4)
+FIRST = (4, 3, 2, 5, 0, 1)
 SECOND = (3, 2, 5, 1, 0, 4)
 THIRD = (2, 1, 3)
 AXES = (0, 1, 2)

time: 56.8 us -> 55.8 us (0.982)
  starting transfers between devices: 40.3 us -> 38 us
  waiting for transfers between devices: 7.95 us -> 9.61 us
    ppermute x12, starting transfers between devices: 35.9 us -> 34.6 us  [swapped(): return lax.ppermute(value, ('curve', 'owner'), pairs_of(axis, odd, bits))]
    ppermute x3, starting transfers between devices: 4.39 us -> 3.34 us  [shards(): lax.ppermute(v, 'owner', [(i, i ^ other) for i in range(4)])]
    ppermute x12, waiting for transfers between devices: 4.38 us -> 5.33 us  [swapped(): return lax.ppermute(value, ('curve', 'owner'), pairs_of(axis, odd, bits))]
    ppermute x3, waiting for transfers between devices: 3.57 us -> 4.28 us  [shards(): lax.ppermute(v, 'owner', [(i, i ^ other) for i in range(4)])]
  transfers between devices with their start and end apart: 15 -> 15, of which waited for: 8 -> 6; matrix products, arithmetic and copies ran while one was open for 0% -> 0% of each run, Pallas kernels for 4% -> 4%
where the time goes in v5:
time: 55.8 us; the launch traced here: 55.4 us
  starting transfers between devices  38 us (68%)
  waiting for transfers between devices  9.61 us (17%)
  Pallas kernels  5.01 us (9%)
  local copies, waits for them, and re-layouts  1.99 us (4%)
  other arithmetic  0.7 us (1%)
    ppermute x12, starting transfers between devices, swapped(): return lax.ppermute(value, ('curve', 'owner'), pairs_of(axis, odd, bits))  34.6 us
    ppermute x12, waiting for transfers between devices, swapped(): return lax.ppermute(value, ('curve', 'owner'), pairs_of(axis, odd, bits))  5.33 us
    ppermute x3, waiting for transfers between devices, shards(): lax.ppermute(v, 'owner', [(i, i ^ other) for i in range(4)])  4.28 us
    ppermute x3, starting transfers between devices, shards(): lax.ppermute(v, 'owner', [(i, i ^ other) for i in range(4)])  3.34 us
    pallas_call x1, Pallas kernels, shards(): call(lambda *refs: inner_kernel(bits, *refs), 'inner', [((G, W, 640), F32...  1.99 us
    unnamed x4, local copies, waits for them, and re-layouts  1.99 us
    pallas_call x1, Pallas kernels, shards(): call(product_step, 'products', [((W, 1280), F32)] + [side] * 6, [VMEM] *...  1.54 us
  transfers between devices with their start and end apart: 15, of which 6 were waited for; matrix products, arithmetic and copies ran while one was open for 0% of the time, Pallas kernels for 4%

profile of v5, /device:TPU:25, one launch (start us, length us, event | category | flops | bytes accessed | tf_op | source)
XLA Modules:
  0.0 55.4 jit_solution(6698436055405437170)
XLA Ops:
  0.0 0.7 %pad_add_fusion.refs_0_ = s32[12,8]{1,0:T(8,128)S(1)} fusion(s32[8,7]{1,0:T(8,128)} %param.5, s32[4,8]{1,0:T(4,128)} %bitcast.1), kind=kLoop, calls=%fused_computation | loop fusion | flops 96 | bytes 736 | tf_op jit(solution)/shard_map/concatenate | solution.py:510
  0.7 0.9 %copy-done = bf16[8,64,256]{2,1,0:T(8,128)(2,1)S(1)} copy-done((bf16[8,64,256]{2,1,0:T(8,128)(2,1)S(1)}, bf16[8,64,256]{2,1,0:T(8,128)(2,1)}, u32[]{:S(2)}) %copy-start) | copy-done | bytes 262168
  1.7 0.4 order.1
  2.0 0.8 %collective-permute-start = (bf16[4,64,256]{2,1,0:T(8,128)(2,1)S(1)}, bf16[4,64,256]{2,1,0:T(8,128)(2,1)S(1)}, u32[]{:S(2)}, u32[]{:S(2)}) collective-permute-start(bf16[4,64,256]{2,1,0:T(8,128)(2,1)S(1)} %get-tuple-element.30), channel_id=1, source_target_pairs={{4,0},{5,1},{6,2},{7,3},{0,4},{1,5},{2,6},{3,7},{12,8},{13,9},{14,... | collective-permute-start | bytes 393224 | tf_op jit(solution)/shard_map/ppermute | solution.py:486
  2.8 8.0 %collective-permute-start.1 = (bf16[4,64,256]{2,1,0:T(8,128)(2,1)S(1)}, bf16[4,64,256]{2,1,0:T(8,128)(2,1)S(1)}, u32[]{:S(2)}, u32[]{:S(2)}) collective-permute-start(bf16[4,64,256]{2,1,0:T(8,128)(2,1)S(1)} %get-tuple-element.31), channel_id=1, source_target_pairs={{16,2},{17,3},{20,6},{21,7},{24,10},{25,11},{28,14},{29,15},{2,16}... | collective-permute-start | bytes 393224 | tf_op jit(solution)/shard_map/ppermute | solution.py:486
  10.9 7.2 %collective-permute-start.3 = (bf16[4,64,256]{2,1,0:T(8,128)(2,1)S(1)}, bf16[4,64,256]{2,1,0:T(8,128)(2,1)S(1)}, u32[]{:S(2)}, u32[]{:S(2)}) collective-permute-start(bf16[4,64,256]{2,1,0:T(8,128)(2,1)S(1)} %get-tuple-element.33), channel_id=1, source_target_pairs={{32,4},{33,5},{34,6},{35,7},{40,12},{41,13},{42,14},{43,15},{48,20... | collective-permute-start | bytes 393224 | tf_op jit(solution)/shard_map/ppermute | solution.py:486
  18.1 1.1 %collective-permute-start.4 = (bf16[4,64,256]{2,1,0:T(8,128)(2,1)S(1)}, bf16[4,64,256]{2,1,0:T(8,128)(2,1)S(1)}, u32[]{:S(2)}, u32[]{:S(2)}) collective-permute-start(bf16[4,64,256]{2,1,0:T(8,128)(2,1)S(1)} %get-tuple-element.34), channel_id=1, source_target_pairs={{1,0},{0,1},{3,2},{2,3},{5,4},{4,5},{7,6},{6,7},{9,8},{8,9},{11,10... | collective-permute-start | bytes 393224 | tf_op jit(solution)/shard_map/ppermute | solution.py:486
  19.3 2.8 %collective-permute-start.5 = (bf16[4,64,256]{2,1,0:T(8,128)(2,1)S(1)}, bf16[4,64,256]{2,1,0:T(8,128)(2,1)S(1)}, u32[]{:S(2)}, u32[]{:S(2)}) collective-permute-start(bf16[4,64,256]{2,1,0:T(8,128)(2,1)S(1)} %get-tuple-element.35), channel_id=1, source_target_pairs={{8,1},{10,3},{12,5},{14,7},{1,8},{64,9},{3,10},{66,11},{5,12},{68,... | collective-permute-start | bytes 393224 | tf_op jit(solution)/shard_map/ppermute | solution.py:486
  22.1 1.0 %copy-done.1 = bf16[8,64,448]{2,1,0:T(8,128)(2,1)S(1)} copy-done((bf16[8,64,448]{2,1,0:T(8,128)(2,1)S(1)}, bf16[8,64,448]{2,1,0:T(8,128)(2,1)}, u32[]{:S(2)}) %copy-start.1) | copy-done | bytes 458776
  23.1 2.0 %inner.1 = (f32[8,64,640]{2,1,0:T(8,128)S(1)}, bf16[8,64,256]{2,1,0:T(8,128)(2,1)S(1)}, bf16[448,512]{1,0:T(8,128)(2,1)S(1)}) custom-call(s32[12,8]{1,0:T(8,128)S(1)} %pad_add_fusion.refs_0_, bf16[8,64,448]{2,1,0:T(8,128)(2,1)S(1)} %copy-done.1, bf16[8,64,256]{2,1,0:T(8,128)(2,1)S(1)} %get-tuple-element.26.refs_2_), custom_call_target="tpu_custom_call" | custom-call | flops 400000000 | bytes 2800000 | tf_op jit(solution)/shard_map/inner/pallas_call | solution.py:523
  25.1 1.6 %collective-permute-done.5.refs_8_ = bf16[4,64,256]{2,1,0:T(8,128)(2,1)S(1)} collective-permute-done((bf16[4,64,256]{2,1,0:T(8,128)(2,1)S(1)}, bf16[4,64,256]{2,1,0:T(8,128)(2,1)S(1)}, u32[]{:S(2)}, u32[]{:S(2)}) %collective-permute-start.5) | collective-permute-done | bytes 131104 | tf_op jit(solution)/shard_map/ppermute | solution.py:486
  26.8 1.5 %products.1 = (f32[64,1280]{1,0:T(8,128)S(1)}, bf16[64,1024]{1,0:T(8,128)(2,1)S(1)}, bf16[64,1024]{1,0:T(8,128)(2,1)S(1)}, bf16[64,1024]{1,0:T(8,128)(2,1)S(1)},...) custom-call(f32[8,64,640]{2,1,0:T(8,128)S(1)} %get-tuple-element.27.refs_0_, ...), custom_call_target="tpu_custom_call" | custom-call | flops 900000000 | bytes 4000000 | tf_op jit(solution)/shard_map/products/pallas_call | solution.py:533
  28.3 5.9 %collective-permute-start.6 = (bf16[64,1024]{1,0:T(8,128)(2,1)S(1)}, bf16[64,1024]{1,0:T(8,128)(2,1)S(1)}, u32[]{:S(2)}, u32[]{:S(2)}) collective-permute-start(bf16[64,1024]{1,0:T(8,128)(2,1)S(1)} %get-tuple-element.37), channel_id=1, source_target_pairs={{16,2},{17,3},{20,6},{21,7},{24,10},{25,11},{28,14},{29,15},{2,16}... | collective-permute-start | bytes 393224 | tf_op jit(solution)/shard_map/ppermute | solution.py:486
  34.3 3.7 %collective-permute-start.8 = (bf16[64,1024]{1,0:T(8,128)(2,1)S(1)}, bf16[64,1024]{1,0:T(8,128)(2,1)S(1)}, u32[]{:S(2)}, u32[]{:S(2)}) collective-permute-start(bf16[64,1024]{1,0:T(8,128)(2,1)S(1)} %get-tuple-element.39), channel_id=1, source_target_pairs={{32,4},{33,5},{34,6},{35,7},{40,12},{41,13},{42,14},{43,15},{48,20... | collective-permute-start | bytes 393224 | tf_op jit(solution)/shard_map/ppermute | solution.py:486
  38.0 4.8 %collective-permute-start.9 = (bf16[64,1024]{1,0:T(8,128)(2,1)S(1)}, bf16[64,1024]{1,0:T(8,128)(2,1)S(1)}, u32[]{:S(2)}, u32[]{:S(2)}) collective-permute-start(bf16[64,1024]{1,0:T(8,128)(2,1)S(1)} %get-tuple-element.40), channel_id=1, source_target_pairs={{8,1},{10,3},{12,5},{14,7},{1,8},{64,9},{3,10},{66,11},{5,12},{68,... | collective-permute-start | bytes 393224 | tf_op jit(solution)/shard_map/ppermute | solution.py:486
  43.0 2.8 %collective-permute-done.8.refs_3_ = bf16[64,1024]{1,0:T(8,128)(2,1)S(1)} collective-permute-done((bf16[64,1024]{1,0:T(8,128)(2,1)S(1)}, bf16[64,1024]{1,0:T(8,128)(2,1)S(1)}, u32[]{:S(2)}, u32[]{:S(2)}) %collective-permute-start.8) | collective-permute-done | bytes 131104 | tf_op jit(solution)/shard_map/ppermute | solution.py:486
  45.9 0.8 %collective-permute-done.10.refs_5_ = bf16[64,1024]{1,0:T(8,128)(2,1)S(1)} collective-permute-done((bf16[64,1024]{1,0:T(8,128)(2,1)S(1)}, bf16[64,1024]{1,0:T(8,128)(2,1)S(1)}, u32[]{:S(2)}, u32[]{:S(2)}) %collective-permute-start.10) | collective-permute-done | bytes 131104 | tf_op jit(solution)/shard_map/ppermute | solution.py:486
  46.7 0.4 gather.1
  47.1 2.9 %collective-permute-start.12 = (bf16[16,2112]{1,0:T(8,128)(2,1)S(1)}, bf16[16,2112]{1,0:T(8,128)(2,1)S(1)}, u32[]{:S(2)}, u32[]{:S(2)}) collective-permute-start(bf16[16,2112]{1,0:T(8,128)(2,1)S(1)} %get-tuple-element.44), channel_id=1, source_target_pairs={{0,2},{1,3},{2,0},{3,1},{4,6},{5,7},{6,4},{7,5},{8,10},{9,11},{10,... | collective-permute-start | bytes 202760 | tf_op jit(solution)/shard_map/ppermute | solution.py:557
  49.9 0.4 collective-permute-start.13
  50.4 1.7 %collective-permute-done.12.first = bf16[16,2112]{1,0:T(8,128)(2,1)S(1)} collective-permute-done((bf16[16,2112]{1,0:T(8,128)(2,1)S(1)}, bf16[16,2112]{1,0:T(8,128)(2,1)S(1)}, u32[]{:S(2)}, u32[]{:S(2)}) %collective-permute-start.12) | collective-permute-done | bytes 67616 | tf_op jit(solution)/shard_map/ppermute | solution.py:557
  52.2 1.1 %collective-permute-done.13.second = bf16[16,2112]{1,0:T(8,128)(2,1)S(1)} collective-permute-done((bf16[16,2112]{1,0:T(8,128)(2,1)S(1)}, bf16[16,2112]{1,0:T(8,128)(2,1)S(1)}, u32[]{:S(2)}, u32[]{:S(2)}) %collective-permute-start.13) | collective-permute-done | bytes 67616 | tf_op jit(solution)/shard_map/ppermute | solution.py:557
  53.3 1.4 %collective-permute-done.14.third = bf16[16,2112]{1,0:T(8,128)(2,1)S(1)} collective-permute-done((bf16[16,2112]{1,0:T(8,128)(2,1)S(1)}, bf16[16,2112]{1,0:T(8,128)(2,1)S(1)}, u32[]{:S(2)}, u32[]{:S(2)}) %collective-permute-start.14) | collective-permute-done | bytes 67616 | tf_op jit(solution)/shard_map/ppermute | solution.py:557
  54.7 0.7 %finish.1 = bf16[4,16,2112]{2,1,0:T(8,128)(2,1)} custom-call(bf16[16,2112]{1,0:T(8,128)(2,1)S(1)} %get-tuple-element.43.mine, bf16[16,2112]{1,0:T(8,128)(2,1)S(1)} %collective-permute-done.12.first, bf16[16,2112]{1,0:T(8,128)(2,1)S(1)} %collective-permute-done.13.second, bf16[16,2112]{1,0:T(8,128)(2,1)S(1)} %collective-permute-done.14.third), custom_call_target="tpu_custom_call" | custom-call | bytes 500000 | tf_op jit(solution)/shard_map/finish/pallas_call | solution.py:560
  (16 shorter events, 0.5 us)
Async XLA Ops:
  0.7 0.9 %copy-start = (bf16[8,64,256]{2,1,0:T(8,128)(2,1)S(1)}, bf16[8,64,256]{2,1,0:T(8,128)(2,1)}, u32[]{:S(2)}) copy-start(bf16[8,64,256]{2,1,0:T(8,128)(2,1)} %refs_1_.2) | copy-start | bytes 786436
  2.0 17.2 %collective-permute-start = (bf16[4,64,256]{2,1,0:T(8,128)(2,1)S(1)}, bf16[4,64,256]{2,1,0:T(8,128)(2,1)S(1)}, u32[]{:S(2)}, u32[]{:S(2)}) collective-permute-start(bf16[4,64,256]{2,1,0:T(8,128)(2,1)S(1)} %get-tuple-element.30), channel_id=1, source_target_pairs={{4,0},{5,1},{6,2},{7,3},{0,4},{1,5},{2,6},{3,7},{12,8},{13,9},{14,... | collective-permute-start | bytes 393224 | tf_op jit(solution)/shard_map/ppermute | solution.py:486
  2.8 22.3 %collective-permute-start.1 = (bf16[4,64,256]{2,1,0:T(8,128)(2,1)S(1)}, bf16[4,64,256]{2,1,0:T(8,128)(2,1)S(1)}, u32[]{:S(2)}, u32[]{:S(2)}) collective-permute-start(bf16[4,64,256]{2,1,0:T(8,128)(2,1)S(1)} %get-tuple-element.31), channel_id=1, source_target_pairs={{16,2},{17,3},{20,6},{21,7},{24,10},{25,11},{28,14},{29,15},{2,16}... | collective-permute-start | bytes 393224 | tf_op jit(solution)/shard_map/ppermute | solution.py:486
  10.8 14.3 %collective-permute-start.2 = (bf16[4,64,256]{2,1,0:T(8,128)(2,1)S(1)}, bf16[4,64,256]{2,1,0:T(8,128)(2,1)S(1)}, u32[]{:S(2)}, u32[]{:S(2)}) collective-permute-start(bf16[4,64,256]{2,1,0:T(8,128)(2,1)S(1)} %get-tuple-element.32), channel_id=1, source_target_pairs={{2,0},{3,1},{0,2},{1,3},{6,4},{7,5},{4,6},{5,7},{10,8},{11,9},{8,1... | collective-permute-start | bytes 393224 | tf_op jit(solution)/shard_map/ppermute | solution.py:486
  10.9 14.2 %collective-permute-start.3 = (bf16[4,64,256]{2,1,0:T(8,128)(2,1)S(1)}, bf16[4,64,256]{2,1,0:T(8,128)(2,1)S(1)}, u32[]{:S(2)}, u32[]{:S(2)}) collective-permute-start(bf16[4,64,256]{2,1,0:T(8,128)(2,1)S(1)} %get-tuple-element.33), channel_id=1, source_target_pairs={{32,4},{33,5},{34,6},{35,7},{40,12},{41,13},{42,14},{43,15},{48,20... | collective-permute-start | bytes 393224 | tf_op jit(solution)/shard_map/ppermute | solution.py:486
  18.1 7.0 %collective-permute-start.4 = (bf16[4,64,256]{2,1,0:T(8,128)(2,1)S(1)}, bf16[4,64,256]{2,1,0:T(8,128)(2,1)S(1)}, u32[]{:S(2)}, u32[]{:S(2)}) collective-permute-start(bf16[4,64,256]{2,1,0:T(8,128)(2,1)S(1)} %get-tuple-element.34), channel_id=1, source_target_pairs={{1,0},{0,1},{3,2},{2,3},{5,4},{4,5},{7,6},{6,7},{9,8},{8,9},{11,10... | collective-permute-start | bytes 393224 | tf_op jit(solution)/shard_map/ppermute | solution.py:486
  19.3 7.5 %collective-permute-start.5 = (bf16[4,64,256]{2,1,0:T(8,128)(2,1)S(1)}, bf16[4,64,256]{2,1,0:T(8,128)(2,1)S(1)}, u32[]{:S(2)}, u32[]{:S(2)}) collective-permute-start(bf16[4,64,256]{2,1,0:T(8,128)(2,1)S(1)} %get-tuple-element.35), channel_id=1, source_target_pairs={{8,1},{10,3},{12,5},{14,7},{1,8},{64,9},{3,10},{66,11},{5,12},{68,... | collective-permute-start | bytes 393224 | tf_op jit(solution)/shard_map/ppermute | solution.py:486
  22.0 1.0 %copy-start.1 = (bf16[8,64,448]{2,1,0:T(8,128)(2,1)S(1)}, bf16[8,64,448]{2,1,0:T(8,128)(2,1)}, u32[]{:S(2)}) copy-start(bf16[8,64,448]{2,1,0:T(8,128)(2,1)} %refs_1_.3) | copy-start | bytes 1376260
  28.3 14.6 %collective-permute-start.6 = (bf16[64,1024]{1,0:T(8,128)(2,1)S(1)}, bf16[64,1024]{1,0:T(8,128)(2,1)S(1)}, u32[]{:S(2)}, u32[]{:S(2)}) collective-permute-start(bf16[64,1024]{1,0:T(8,128)(2,1)S(1)} %get-tuple-element.37), channel_id=1, source_target_pairs={{16,2},{17,3},{20,6},{21,7},{24,10},{25,11},{28,14},{29,15},{2,16}... | collective-permute-start | bytes 393224 | tf_op jit(solution)/shard_map/ppermute | solution.py:486
  34.2 8.8 %collective-permute-start.7 = (bf16[64,1024]{1,0:T(8,128)(2,1)S(1)}, bf16[64,1024]{1,0:T(8,128)(2,1)S(1)}, u32[]{:S(2)}, u32[]{:S(2)}) collective-permute-start(bf16[64,1024]{1,0:T(8,128)(2,1)S(1)} %get-tuple-element.38), channel_id=1, source_target_pairs={{2,0},{3,1},{0,2},{1,3},{6,4},{7,5},{4,6},{5,7},{10,8},{11,9},{8,1... | collective-permute-start | bytes 393224 | tf_op jit(solution)/shard_map/ppermute | solution.py:486
  34.3 11.5 %collective-permute-start.8 = (bf16[64,1024]{1,0:T(8,128)(2,1)S(1)}, bf16[64,1024]{1,0:T(8,128)(2,1)S(1)}, u32[]{:S(2)}, u32[]{:S(2)}) collective-permute-start(bf16[64,1024]{1,0:T(8,128)(2,1)S(1)} %get-tuple-element.39), channel_id=1, source_target_pairs={{32,4},{33,5},{34,6},{35,7},{40,12},{41,13},{42,14},{43,15},{48,20... | collective-permute-start | bytes 393224 | tf_op jit(solution)/shard_map/ppermute | solution.py:486
  38.0 7.8 %collective-permute-start.9 = (bf16[64,1024]{1,0:T(8,128)(2,1)S(1)}, bf16[64,1024]{1,0:T(8,128)(2,1)S(1)}, u32[]{:S(2)}, u32[]{:S(2)}) collective-permute-start(bf16[64,1024]{1,0:T(8,128)(2,1)S(1)} %get-tuple-element.40), channel_id=1, source_target_pairs={{8,1},{10,3},{12,5},{14,7},{1,8},{64,9},{3,10},{66,11},{5,12},{68,... | collective-permute-start | bytes 393224 | tf_op jit(solution)/shard_map/ppermute | solution.py:486
  42.8 3.9 %collective-permute-start.10 = (bf16[64,1024]{1,0:T(8,128)(2,1)S(1)}, bf16[64,1024]{1,0:T(8,128)(2,1)S(1)}, u32[]{:S(2)}, u32[]{:S(2)}) collective-permute-start(bf16[64,1024]{1,0:T(8,128)(2,1)S(1)} %get-tuple-element.41), channel_id=1, source_target_pairs={{1,0},{0,1},{3,2},{2,3},{5,4},{4,5},{7,6},{6,7},{9,8},{8,9},{11,10... | collective-permute-start | bytes 393224 | tf_op jit(solution)/shard_map/ppermute | solution.py:486
  42.9 3.8 %collective-permute-start.11 = (bf16[64,1024]{1,0:T(8,128)(2,1)S(1)}, bf16[64,1024]{1,0:T(8,128)(2,1)S(1)}, u32[]{:S(2)}, u32[]{:S(2)}) collective-permute-start(bf16[64,1024]{1,0:T(8,128)(2,1)S(1)} %get-tuple-element.42), channel_id=1, source_target_pairs={{4,0},{5,1},{6,2},{7,3},{0,4},{1,5},{2,6},{3,7},{12,8},{13,9},{14,... | collective-permute-start | bytes 393224 | tf_op jit(solution)/shard_map/ppermute | solution.py:486
  47.1 5.1 %collective-permute-start.12 = (bf16[16,2112]{1,0:T(8,128)(2,1)S(1)}, bf16[16,2112]{1,0:T(8,128)(2,1)S(1)}, u32[]{:S(2)}, u32[]{:S(2)}) collective-permute-start(bf16[16,2112]{1,0:T(8,128)(2,1)S(1)} %get-tuple-element.44), channel_id=1, source_target_pairs={{0,2},{1,3},{2,0},{3,1},{4,6},{5,7},{6,4},{7,5},{8,10},{9,11},{10,... | collective-permute-start | bytes 202760 | tf_op jit(solution)/shard_map/ppermute | solution.py:557
  49.9 3.4 %collective-permute-start.13 = (bf16[16,2112]{1,0:T(8,128)(2,1)S(1)}, bf16[16,2112]{1,0:T(8,128)(2,1)S(1)}, u32[]{:S(2)}, u32[]{:S(2)}) collective-permute-start(bf16[16,2112]{1,0:T(8,128)(2,1)S(1)} %get-tuple-element.45), channel_id=1, source_target_pairs={{0,1},{1,0},{2,3},{3,2},{4,5},{5,4},{6,7},{7,6},{8,9},{9,8},{10,11... | collective-permute-start | bytes 202760 | tf_op jit(solution)/shard_map/ppermute | solution.py:557
  50.3 4.4 %collective-permute-start.14 = (bf16[16,2112]{1,0:T(8,128)(2,1)S(1)}, bf16[16,2112]{1,0:T(8,128)(2,1)S(1)}, u32[]{:S(2)}, u32[]{:S(2)}) collective-permute-start(bf16[16,2112]{1,0:T(8,128)(2,1)S(1)} %get-tuple-element.46), channel_id=1, source_target_pairs={{0,3},{1,2},{2,1},{3,0},{4,7},{5,6},{6,5},{7,4},{8,11},{9,10},{10,... | collective-permute-start | bytes 202760 | tf_op jit(solution)/shard_map/ppermute | solution.py:557

commit v6 on v5

--- a/solution.py
+++ b/solution.py
@@ -8,7 +8,7 @@
 
 W = 64
 G = 8
-FIRST = (4, 3, 2, 5, 0, 1)
+FIRST = (4, 3, 5, 2, 0, 1)
 SECOND = (3, 2, 5, 1, 0, 4)
 THIRD = (2, 1, 3)
 AXES = (0, 1, 2)

time: 55.8 us -> 56.1 us (level)
  starting transfers between devices: 38 us -> 38.9 us
where the time goes in v6:
time: 56.1 us; the launch traced here: 55.8 us
  starting transfers between devices  38.9 us (69%)
  waiting for transfers between devices  9.1 us (16%)
  Pallas kernels  5.01 us (9%)
  local copies, waits for them, and re-layouts  1.99 us (4%)
  other arithmetic  0.7 us (1%)
    ppermute x12, starting transfers between devices, swapped(): return lax.ppermute(value, ('curve', 'owner'), pairs_of(axis, odd, bits))  35 us
    ppermute x12, waiting for transfers between devices, swapped(): return lax.ppermute(value, ('curve', 'owner'), pairs_of(axis, odd, bits))  5.05 us
    ppermute x3, waiting for transfers between devices, shards(): lax.ppermute(v, 'owner', [(i, i ^ other) for i in range(4)])  4.04 us
    ppermute x3, starting transfers between devices, shards(): lax.ppermute(v, 'owner', [(i, i ^ other) for i in range(4)])  3.84 us
    pallas_call x1, Pallas kernels, shards(): call(lambda *refs: inner_kernel(bits, *refs), 'inner', [((G, W, 640), F32...  1.99 us
    unnamed x4, local copies, waits for them, and re-layouts  1.99 us
    pallas_call x1, Pallas kernels, shards(): call(product_step, 'products', [((W, 1280), F32)] + [side] * 6, [VMEM] *...  1.54 us
  transfers between devices with their start and end apart: 15, of which 6 were waited for; matrix products, arithmetic and copies ran while one was open for 0% of the time, Pallas kernels for 4%

profile of v6, /device:TPU:25, one launch (start us, length us, event | category | flops | bytes accessed | tf_op | source)
XLA Modules:
  0.0 55.8 jit_solution(17268628110881062101)
XLA Ops:
  0.0 0.7 %pad_add_fusion.refs_0_ = s32[12,8]{1,0:T(8,128)S(1)} fusion(s32[8,7]{1,0:T(8,128)} %param.5, s32[4,8]{1,0:T(4,128)} %bitcast.1), kind=kLoop, calls=%fused_computation | loop fusion | flops 96 | bytes 736 | tf_op jit(solution)/shard_map/concatenate | solution.py:510
  0.7 0.9 %copy-done = bf16[8,64,256]{2,1,0:T(8,128)(2,1)S(1)} copy-done((bf16[8,64,256]{2,1,0:T(8,128)(2,1)S(1)}, bf16[8,64,256]{2,1,0:T(8,128)(2,1)}, u32[]{:S(2)}) %copy-start) | copy-done | bytes 262168
  2.0 0.8 %collective-permute-start = (bf16[4,64,256]{2,1,0:T(8,128)(2,1)S(1)}, bf16[4,64,256]{2,1,0:T(8,128)(2,1)S(1)}, u32[]{:S(2)}, u32[]{:S(2)}) collective-permute-start(bf16[4,64,256]{2,1,0:T(8,128)(2,1)S(1)} %get-tuple-element.30), channel_id=1, source_target_pairs={{4,0},{5,1},{6,2},{7,3},{0,4},{1,5},{2,6},{3,7},{12,8},{13,9},{14,... | collective-permute-start | bytes 393224 | tf_op jit(solution)/shard_map/ppermute | solution.py:486
  2.8 8.0 %collective-permute-start.1 = (bf16[4,64,256]{2,1,0:T(8,128)(2,1)S(1)}, bf16[4,64,256]{2,1,0:T(8,128)(2,1)S(1)}, u32[]{:S(2)}, u32[]{:S(2)}) collective-permute-start(bf16[4,64,256]{2,1,0:T(8,128)(2,1)S(1)} %get-tuple-element.31), channel_id=1, source_target_pairs={{16,2},{17,3},{20,6},{21,7},{24,10},{25,11},{28,14},{29,15},{2,16}... | collective-permute-start | bytes 393224 | tf_op jit(solution)/shard_map/ppermute | solution.py:486
  10.8 7.2 %collective-permute-start.2 = (bf16[4,64,256]{2,1,0:T(8,128)(2,1)S(1)}, bf16[4,64,256]{2,1,0:T(8,128)(2,1)S(1)}, u32[]{:S(2)}, u32[]{:S(2)}) collective-permute-start(bf16[4,64,256]{2,1,0:T(8,128)(2,1)S(1)} %get-tuple-element.32), channel_id=1, source_target_pairs={{32,4},{33,5},{34,6},{35,7},{40,12},{41,13},{42,14},{43,15},{48,20... | collective-permute-start | bytes 393224 | tf_op jit(solution)/shard_map/ppermute | solution.py:486
  18.1 0.8 %collective-permute-start.4 = (bf16[4,64,256]{2,1,0:T(8,128)(2,1)S(1)}, bf16[4,64,256]{2,1,0:T(8,128)(2,1)S(1)}, u32[]{:S(2)}, u32[]{:S(2)}) collective-permute-start(bf16[4,64,256]{2,1,0:T(8,128)(2,1)S(1)} %get-tuple-element.34), channel_id=1, source_target_pairs={{1,0},{0,1},{3,2},{2,3},{5,4},{4,5},{7,6},{6,7},{9,8},{8,9},{11,10... | collective-permute-start | bytes 393224 | tf_op jit(solution)/shard_map/ppermute | solution.py:486
  18.9 2.8 %collective-permute-start.5 = (bf16[4,64,256]{2,1,0:T(8,128)(2,1)S(1)}, bf16[4,64,256]{2,1,0:T(8,128)(2,1)S(1)}, u32[]{:S(2)}, u32[]{:S(2)}) collective-permute-start(bf16[4,64,256]{2,1,0:T(8,128)(2,1)S(1)} %get-tuple-element.35), channel_id=1, source_target_pairs={{8,1},{10,3},{12,5},{14,7},{1,8},{64,9},{3,10},{66,11},{5,12},{68,... | collective-permute-start | bytes 393224 | tf_op jit(solution)/shard_map/ppermute | solution.py:486
  21.7 1.0 %copy-done.1 = bf16[8,64,448]{2,1,0:T(8,128)(2,1)S(1)} copy-done((bf16[8,64,448]{2,1,0:T(8,128)(2,1)S(1)}, bf16[8,64,448]{2,1,0:T(8,128)(2,1)}, u32[]{:S(2)}) %copy-start.1) | copy-done | bytes 458776
  22.7 2.0 %inner.1 = (f32[8,64,640]{2,1,0:T(8,128)S(1)}, bf16[8,64,256]{2,1,0:T(8,128)(2,1)S(1)}, bf16[448,512]{1,0:T(8,128)(2,1)S(1)}) custom-call(s32[12,8]{1,0:T(8,128)S(1)} %pad_add_fusion.refs_0_, bf16[8,64,448]{2,1,0:T(8,128)(2,1)S(1)} %copy-done.1, bf16[8,64,256]{2,1,0:T(8,128)(2,1)S(1)} %get-tuple-element.26.refs_2_), custom_call_target="tpu_custom_call" | custom-call | flops 400000000 | bytes 2800000 | tf_op jit(solution)/shard_map/inner/pallas_call | solution.py:523
  24.8 1.6 %collective-permute-done.5.refs_8_ = bf16[4,64,256]{2,1,0:T(8,128)(2,1)S(1)} collective-permute-done((bf16[4,64,256]{2,1,0:T(8,128)(2,1)S(1)}, bf16[4,64,256]{2,1,0:T(8,128)(2,1)S(1)}, u32[]{:S(2)}, u32[]{:S(2)}) %collective-permute-start.5) | collective-permute-done | bytes 131104 | tf_op jit(solution)/shard_map/ppermute | solution.py:486
  26.4 1.5 %products.1 = (f32[64,1280]{1,0:T(8,128)S(1)}, bf16[64,1024]{1,0:T(8,128)(2,1)S(1)}, bf16[64,1024]{1,0:T(8,128)(2,1)S(1)}, bf16[64,1024]{1,0:T(8,128)(2,1)S(1)},...) custom-call(f32[8,64,640]{2,1,0:T(8,128)S(1)} %get-tuple-element.27.refs_0_, ...), custom_call_target="tpu_custom_call" | custom-call | flops 900000000 | bytes 4000000 | tf_op jit(solution)/shard_map/products/pallas_call | solution.py:533
  27.9 5.9 %collective-permute-start.6 = (bf16[64,1024]{1,0:T(8,128)(2,1)S(1)}, bf16[64,1024]{1,0:T(8,128)(2,1)S(1)}, u32[]{:S(2)}, u32[]{:S(2)}) collective-permute-start(bf16[64,1024]{1,0:T(8,128)(2,1)S(1)} %get-tuple-element.37), channel_id=1, source_target_pairs={{16,2},{17,3},{20,6},{21,7},{24,10},{25,11},{28,14},{29,15},{2,16}... | collective-permute-start | bytes 393224 | tf_op jit(solution)/shard_map/ppermute | solution.py:486
  34.0 4.2 %collective-permute-start.8 = (bf16[64,1024]{1,0:T(8,128)(2,1)S(1)}, bf16[64,1024]{1,0:T(8,128)(2,1)S(1)}, u32[]{:S(2)}, u32[]{:S(2)}) collective-permute-start(bf16[64,1024]{1,0:T(8,128)(2,1)S(1)} %get-tuple-element.39), channel_id=1, source_target_pairs={{32,4},{33,5},{34,6},{35,7},{40,12},{41,13},{42,14},{43,15},{48,20... | collective-permute-start | bytes 393224 | tf_op jit(solution)/shard_map/ppermute | solution.py:486
  38.1 4.7 %collective-permute-start.9 = (bf16[64,1024]{1,0:T(8,128)(2,1)S(1)}, bf16[64,1024]{1,0:T(8,128)(2,1)S(1)}, u32[]{:S(2)}, u32[]{:S(2)}) collective-permute-start(bf16[64,1024]{1,0:T(8,128)(2,1)S(1)} %get-tuple-element.40), channel_id=1, source_target_pairs={{8,1},{10,3},{12,5},{14,7},{1,8},{64,9},{3,10},{66,11},{5,12},{68,... | collective-permute-start | bytes 393224 | tf_op jit(solution)/shard_map/ppermute | solution.py:486
  42.9 0.5 collective-permute-start.10
  43.4 2.3 %collective-permute-done.8.refs_3_ = bf16[64,1024]{1,0:T(8,128)(2,1)S(1)} collective-permute-done((bf16[64,1024]{1,0:T(8,128)(2,1)S(1)}, bf16[64,1024]{1,0:T(8,128)(2,1)S(1)}, u32[]{:S(2)}, u32[]{:S(2)}) %collective-permute-start.8) | collective-permute-done | bytes 131104 | tf_op jit(solution)/shard_map/ppermute | solution.py:486
  45.7 1.0 %collective-permute-done.10.refs_5_ = bf16[64,1024]{1,0:T(8,128)(2,1)S(1)} collective-permute-done((bf16[64,1024]{1,0:T(8,128)(2,1)S(1)}, bf16[64,1024]{1,0:T(8,128)(2,1)S(1)}, u32[]{:S(2)}, u32[]{:S(2)}) %collective-permute-start.10) | collective-permute-done | bytes 131104 | tf_op jit(solution)/shard_map/ppermute | solution.py:486
  46.8 0.4 gather.1
  47.2 2.2 %collective-permute-start.12 = (bf16[16,2112]{1,0:T(8,128)(2,1)S(1)}, bf16[16,2112]{1,0:T(8,128)(2,1)S(1)}, u32[]{:S(2)}, u32[]{:S(2)}) collective-permute-start(bf16[16,2112]{1,0:T(8,128)(2,1)S(1)} %get-tuple-element.44), channel_id=1, source_target_pairs={{0,2},{1,3},{2,0},{3,1},{4,6},{5,7},{6,4},{7,5},{8,10},{9,11},{10,... | collective-permute-start | bytes 202760 | tf_op jit(solution)/shard_map/ppermute | solution.py:557
  49.4 1.3 %collective-permute-start.13 = (bf16[16,2112]{1,0:T(8,128)(2,1)S(1)}, bf16[16,2112]{1,0:T(8,128)(2,1)S(1)}, u32[]{:S(2)}, u32[]{:S(2)}) collective-permute-start(bf16[16,2112]{1,0:T(8,128)(2,1)S(1)} %get-tuple-element.45), channel_id=1, source_target_pairs={{0,1},{1,0},{2,3},{3,2},{4,5},{5,4},{6,7},{7,6},{8,9},{9,8},{10,11... | collective-permute-start | bytes 202760 | tf_op jit(solution)/shard_map/ppermute | solution.py:557
  51.0 1.2 %collective-permute-done.12.first = bf16[16,2112]{1,0:T(8,128)(2,1)S(1)} collective-permute-done((bf16[16,2112]{1,0:T(8,128)(2,1)S(1)}, bf16[16,2112]{1,0:T(8,128)(2,1)S(1)}, u32[]{:S(2)}, u32[]{:S(2)}) %collective-permute-start.12) | collective-permute-done | bytes 67616 | tf_op jit(solution)/shard_map/ppermute | solution.py:557
  52.3 1.7 %collective-permute-done.13.second = bf16[16,2112]{1,0:T(8,128)(2,1)S(1)} collective-permute-done((bf16[16,2112]{1,0:T(8,128)(2,1)S(1)}, bf16[16,2112]{1,0:T(8,128)(2,1)S(1)}, u32[]{:S(2)}, u32[]{:S(2)}) %collective-permute-start.13) | collective-permute-done | bytes 67616 | tf_op jit(solution)/shard_map/ppermute | solution.py:557
  54.0 1.1 %collective-permute-done.14.third = bf16[16,2112]{1,0:T(8,128)(2,1)S(1)} collective-permute-done((bf16[16,2112]{1,0:T(8,128)(2,1)S(1)}, bf16[16,2112]{1,0:T(8,128)(2,1)S(1)}, u32[]{:S(2)}, u32[]{:S(2)}) %collective-permute-start.14) | collective-permute-done | bytes 67616 | tf_op jit(solution)/shard_map/ppermute | solution.py:557
  55.1 0.7 %finish.1 = bf16[4,16,2112]{2,1,0:T(8,128)(2,1)} custom-call(bf16[16,2112]{1,0:T(8,128)(2,1)S(1)} %get-tuple-element.43.mine, bf16[16,2112]{1,0:T(8,128)(2,1)S(1)} %collective-permute-done.12.first, bf16[16,2112]{1,0:T(8,128)(2,1)S(1)} %collective-permute-done.13.second, bf16[16,2112]{1,0:T(8,128)(2,1)S(1)} %collective-permute-done.14.third), custom_call_target="tpu_custom_call" | custom-call | bytes 500000 | tf_op jit(solution)/shard_map/finish/pallas_call | solution.py:560
  (16 shorter events, 0.9 us)
Async XLA Ops:
  0.7 0.9 %copy-start = (bf16[8,64,256]{2,1,0:T(8,128)(2,1)S(1)}, bf16[8,64,256]{2,1,0:T(8,128)(2,1)}, u32[]{:S(2)}) copy-start(bf16[8,64,256]{2,1,0:T(8,128)(2,1)} %refs_1_.2) | copy-start | bytes 786436
  2.0 16.9 %collective-permute-start = (bf16[4,64,256]{2,1,0:T(8,128)(2,1)S(1)}, bf16[4,64,256]{2,1,0:T(8,128)(2,1)S(1)}, u32[]{:S(2)}, u32[]{:S(2)}) collective-permute-start(bf16[4,64,256]{2,1,0:T(8,128)(2,1)S(1)} %get-tuple-element.30), channel_id=1, source_target_pairs={{4,0},{5,1},{6,2},{7,3},{0,4},{1,5},{2,6},{3,7},{12,8},{13,9},{14,... | collective-permute-start | bytes 393224 | tf_op jit(solution)/shard_map/ppermute | solution.py:486
  2.8 21.9 %collective-permute-start.1 = (bf16[4,64,256]{2,1,0:T(8,128)(2,1)S(1)}, bf16[4,64,256]{2,1,0:T(8,128)(2,1)S(1)}, u32[]{:S(2)}, u32[]{:S(2)}) collective-permute-start(bf16[4,64,256]{2,1,0:T(8,128)(2,1)S(1)} %get-tuple-element.31), channel_id=1, source_target_pairs={{16,2},{17,3},{20,6},{21,7},{24,10},{25,11},{28,14},{29,15},{2,16}... | collective-permute-start | bytes 393224 | tf_op jit(solution)/shard_map/ppermute | solution.py:486
  10.8 13.9 %collective-permute-start.2 = (bf16[4,64,256]{2,1,0:T(8,128)(2,1)S(1)}, bf16[4,64,256]{2,1,0:T(8,128)(2,1)S(1)}, u32[]{:S(2)}, u32[]{:S(2)}) collective-permute-start(bf16[4,64,256]{2,1,0:T(8,128)(2,1)S(1)} %get-tuple-element.32), channel_id=1, source_target_pairs={{32,4},{33,5},{34,6},{35,7},{40,12},{41,13},{42,14},{43,15},{48,20... | collective-permute-start | bytes 393224 | tf_op jit(solution)/shard_map/ppermute | solution.py:486
  18.0 6.7 %collective-permute-start.3 = (bf16[4,64,256]{2,1,0:T(8,128)(2,1)S(1)}, bf16[4,64,256]{2,1,0:T(8,128)(2,1)S(1)}, u32[]{:S(2)}, u32[]{:S(2)}) collective-permute-start(bf16[4,64,256]{2,1,0:T(8,128)(2,1)S(1)} %get-tuple-element.33), channel_id=1, source_target_pairs={{2,0},{3,1},{0,2},{1,3},{6,4},{7,5},{4,6},{5,7},{10,8},{11,9},{8,1... | collective-permute-start | bytes 393224 | tf_op jit(solution)/shard_map/ppermute | solution.py:486
  18.1 6.6 %collective-permute-start.4 = (bf16[4,64,256]{2,1,0:T(8,128)(2,1)S(1)}, bf16[4,64,256]{2,1,0:T(8,128)(2,1)S(1)}, u32[]{:S(2)}, u32[]{:S(2)}) collective-permute-start(bf16[4,64,256]{2,1,0:T(8,128)(2,1)S(1)} %get-tuple-element.34), channel_id=1, source_target_pairs={{1,0},{0,1},{3,2},{2,3},{5,4},{4,5},{7,6},{6,7},{9,8},{8,9},{11,10... | collective-permute-start | bytes 393224 | tf_op jit(solution)/shard_map/ppermute | solution.py:486
  18.9 7.5 %collective-permute-start.5 = (bf16[4,64,256]{2,1,0:T(8,128)(2,1)S(1)}, bf16[4,64,256]{2,1,0:T(8,128)(2,1)S(1)}, u32[]{:S(2)}, u32[]{:S(2)}) collective-permute-start(bf16[4,64,256]{2,1,0:T(8,128)(2,1)S(1)} %get-tuple-element.35), channel_id=1, source_target_pairs={{8,1},{10,3},{12,5},{14,7},{1,8},{64,9},{3,10},{66,11},{5,12},{68,... | collective-permute-start | bytes 393224 | tf_op jit(solution)/shard_map/ppermute | solution.py:486
  21.7 1.0 %copy-start.1 = (bf16[8,64,448]{2,1,0:T(8,128)(2,1)S(1)}, bf16[8,64,448]{2,1,0:T(8,128)(2,1)}, u32[]{:S(2)}) copy-start(bf16[8,64,448]{2,1,0:T(8,128)(2,1)} %refs_1_.3) | copy-start | bytes 1376260
  27.9 15.4 %collective-permute-start.6 = (bf16[64,1024]{1,0:T(8,128)(2,1)S(1)}, bf16[64,1024]{1,0:T(8,128)(2,1)S(1)}, u32[]{:S(2)}, u32[]{:S(2)}) collective-permute-start(bf16[64,1024]{1,0:T(8,128)(2,1)S(1)} %get-tuple-element.37), channel_id=1, source_target_pairs={{16,2},{17,3},{20,6},{21,7},{24,10},{25,11},{28,14},{29,15},{2,16}... | collective-permute-start | bytes 393224 | tf_op jit(solution)/shard_map/ppermute | solution.py:486
  33.9 9.5 %collective-permute-start.7 = (bf16[64,1024]{1,0:T(8,128)(2,1)S(1)}, bf16[64,1024]{1,0:T(8,128)(2,1)S(1)}, u32[]{:S(2)}, u32[]{:S(2)}) collective-permute-start(bf16[64,1024]{1,0:T(8,128)(2,1)S(1)} %get-tuple-element.38), channel_id=1, source_target_pairs={{2,0},{3,1},{0,2},{1,3},{6,4},{7,5},{4,6},{5,7},{10,8},{11,9},{8,1... | collective-permute-start | bytes 393224 | tf_op jit(solution)/shard_map/ppermute | solution.py:486
  34.0 11.7 %collective-permute-start.8 = (bf16[64,1024]{1,0:T(8,128)(2,1)S(1)}, bf16[64,1024]{1,0:T(8,128)(2,1)S(1)}, u32[]{:S(2)}, u32[]{:S(2)}) collective-permute-start(bf16[64,1024]{1,0:T(8,128)(2,1)S(1)} %get-tuple-element.39), channel_id=1, source_target_pairs={{32,4},{33,5},{34,6},{35,7},{40,12},{41,13},{42,14},{43,15},{48,20... | collective-permute-start | bytes 393224 | tf_op jit(solution)/shard_map/ppermute | solution.py:486
  38.1 7.6 %collective-permute-start.9 = (bf16[64,1024]{1,0:T(8,128)(2,1)S(1)}, bf16[64,1024]{1,0:T(8,128)(2,1)S(1)}, u32[]{:S(2)}, u32[]{:S(2)}) collective-permute-start(bf16[64,1024]{1,0:T(8,128)(2,1)S(1)} %get-tuple-element.40), channel_id=1, source_target_pairs={{8,1},{10,3},{12,5},{14,7},{1,8},{64,9},{3,10},{66,11},{5,12},{68,... | collective-permute-start | bytes 393224 | tf_op jit(solution)/shard_map/ppermute | solution.py:486
  42.9 3.9 %collective-permute-start.10 = (bf16[64,1024]{1,0:T(8,128)(2,1)S(1)}, bf16[64,1024]{1,0:T(8,128)(2,1)S(1)}, u32[]{:S(2)}, u32[]{:S(2)}) collective-permute-start(bf16[64,1024]{1,0:T(8,128)(2,1)S(1)} %get-tuple-element.41), channel_id=1, source_target_pairs={{1,0},{0,1},{3,2},{2,3},{5,4},{4,5},{7,6},{6,7},{9,8},{8,9},{11,10... | collective-permute-start | bytes 393224 | tf_op jit(solution)/shard_map/ppermute | solution.py:486
  43.4 3.4 %collective-permute-start.11 = (bf16[64,1024]{1,0:T(8,128)(2,1)S(1)}, bf16[64,1024]{1,0:T(8,128)(2,1)S(1)}, u32[]{:S(2)}, u32[]{:S(2)}) collective-permute-start(bf16[64,1024]{1,0:T(8,128)(2,1)S(1)} %get-tuple-element.42), channel_id=1, source_target_pairs={{4,0},{5,1},{6,2},{7,3},{0,4},{1,5},{2,6},{3,7},{12,8},{13,9},{14,... | collective-permute-start | bytes 393224 | tf_op jit(solution)/shard_map/ppermute | solution.py:486
  47.2 5.1 %collective-permute-start.12 = (bf16[16,2112]{1,0:T(8,128)(2,1)S(1)}, bf16[16,2112]{1,0:T(8,128)(2,1)S(1)}, u32[]{:S(2)}, u32[]{:S(2)}) collective-permute-start(bf16[16,2112]{1,0:T(8,128)(2,1)S(1)} %get-tuple-element.44), channel_id=1, source_target_pairs={{0,2},{1,3},{2,0},{3,1},{4,6},{5,7},{6,4},{7,5},{8,10},{9,11},{10,... | collective-permute-start | bytes 202760 | tf_op jit(solution)/shard_map/ppermute | solution.py:557
  49.4 4.5 %collective-permute-start.13 = (bf16[16,2112]{1,0:T(8,128)(2,1)S(1)}, bf16[16,2112]{1,0:T(8,128)(2,1)S(1)}, u32[]{:S(2)}, u32[]{:S(2)}) collective-permute-start(bf16[16,2112]{1,0:T(8,128)(2,1)S(1)} %get-tuple-element.45), channel_id=1, source_target_pairs={{0,1},{1,0},{2,3},{3,2},{4,5},{5,4},{6,7},{7,6},{8,9},{9,8},{10,11... | collective-permute-start | bytes 202760 | tf_op jit(solution)/shard_map/ppermute | solution.py:557
  50.7 4.4 %collective-permute-start.14 = (bf16[16,2112]{1,0:T(8,128)(2,1)S(1)}, bf16[16,2112]{1,0:T(8,128)(2,1)S(1)}, u32[]{:S(2)}, u32[]{:S(2)}) collective-permute-start(bf16[16,2112]{1,0:T(8,128)(2,1)S(1)} %get-tuple-element.46), channel_id=1, source_target_pairs={{0,3},{1,2},{2,1},{3,0},{4,7},{5,6},{6,5},{7,4},{8,11},{9,10},{10,... | collective-permute-start | bytes 202760 | tf_op jit(solution)/shard_map/ppermute | solution.py:557
